TPU v7x, 512 devices: a whole 4x4x16 slice. The times are simulated.
512 devices in a mesh: dp: 64 (over x, z), cent: 8 (over y, core).
Axes of the slice: x: 4, y: 4, z: 16, core: 2. Of those that a mesh axis runs over, the one named last changes fastest.
Arguments:
- embeddings: bfloat16 [131072, 768], P('dp'), may hold values from -8 to 8
- coarse_ids: int32 [131072, 16], P('dp'), may hold values from 0 to 511, as said below
- centroids: float32 [8192, 768], P(('dp', 'cent')), may hold values from -4 to 4
- coarse_of: int32 [8192], replicated, may hold values from 0 to 511, as said below
Outputs:
- new_centroids: float32 [8192, 768], P(('dp', 'cent'))
Inputs may be any that keep to these rules, and one draw needn't show every extreme that they name: `coarse_of`: each coarse cluster holds exactly 16 centroids. `coarse_ids`: the 16 entries of a row are distinct and increase along the row; every coarse cluster is named by some row.
All inputs are finite; a program needn't handle non-finite values.
Results may differ from a plain program's by a relative error of at most 0.003.
Values may be sent and summed in bfloat16 or wider, within the bound.
No kernel may reach another device: no remote copies, remote signals or barrier semaphores. Data moves between devices by JAX's collectives and lax.ppermute only.
A program may use at most 64 MiB of HBM per device.

v0:
```python
import jax
import jax.numpy as jnp
from jax import lax
from jax.sharding import PartitionSpec as P

SWEEPS = 3


entropic_smoothing = 0.03


def unit_rows(values):
    values = values.astype(jnp.float32)
    return values * lax.rsqrt(jnp.sum(values * values, axis=-1, keepdims=True) + 1e-06)


def row_scale(similarity_exponential, col_factor):
    totals = lax.psum(jnp.sum(similarity_exponential * col_factor[None, :], axis=1), "cent")
    return 1.0 / totals


def column_scale(similarity_exponential, row_scaling, desired_load):
    column = jnp.sum(similarity_exponential * row_scaling[:, None], axis=0)
    return desired_load / lax.psum(column, "dp")


def per_device(embeddings, coarse_ids, centroids, coarse_of):
    row_count = embeddings.shape[0]
    local_count = centroids.shape[0]
    dp_size = lax.axis_size("dp")
    cent_size = lax.axis_size("cent")
    desired_load = row_count / (local_count * cent_size)
    unit_x = unit_rows(embeddings).astype(jnp.bfloat16)
    unit_c = unit_rows(centroids).astype(jnp.bfloat16)
    layout_table = coarse_of.reshape(dp_size, cent_size, local_count)
    group_ids = lax.dynamic_slice_in_dim(layout_table, lax.axis_index("cent"), 1, 1).reshape(
        dp_size * local_count
    )
    group_centroids = lax.all_gather(unit_c, "dp", axis=0, tiled=True)
    pairwise_dots = lax.dot_general(
        unit_x, group_centroids, (((1,), (1,)), ((), ())), preferred_element_type=jnp.float32
    )
    assigned_points = jnp.any(coarse_ids[:, :, None] == group_ids[None, None, :], axis=1)
    similarity_exponential = jnp.where(
        assigned_points, jnp.exp(pairwise_dots / entropic_smoothing), 0.0
    )
    row_scaling = row_scale(
        similarity_exponential, jnp.ones((similarity_exponential.shape[1],), jnp.float32)
    )
    for sweep in range(SWEEPS):
        col_factor = column_scale(similarity_exponential, row_scaling, desired_load)
        row_scaling = row_scale(similarity_exponential, col_factor)
    weighted = similarity_exponential * row_scaling[:, None]
    col_mass = jnp.sum(weighted, axis=0)
    numerator = lax.dot_general(
        weighted.astype(jnp.bfloat16),
        embeddings,
        (((0,), (0,)), ((), ())),
        preferred_element_type=jnp.float32,
    )
    numer_all, mass_all = lax.psum((numerator, col_mass), "dp")
    offset = lax.axis_index("dp") * local_count
    numer_own = lax.dynamic_slice_in_dim(numer_all, offset, local_count, 0)
    mass_own = lax.dynamic_slice_in_dim(mass_all, offset, local_count, 0)
    return (numer_own + centroids) / (mass_own + 1.0)[:, None]


def solution(mesh):
    return jax.shard_map(
        per_device,
        mesh=mesh,
        in_specs=(P("dp", None), P("dp", None), P(("dp", "cent"), None), P()),
        out_specs=P(("dp", "cent"), None),
        check_vma=False,
    )
```

profile of v0, /device:TPU:16, one launch (start us, length us, event | category | flops | bytes accessed | tf_op | source)
XLA Modules:
  0.0 948.1 jit_solution(4260132355372000483)
XLA Ops:
  6.5 0.9 multiply_reduce_fusion.7
  7.5 1.5 multiply_convert_fusion.2
  8.9 0.0 all-gather.2.cloned.1.call-update
  9.0 0.0 all-reduce.2.cloned.1.call-start
  9.0 0.9 reshape.25
  9.9 0.1 dynamic-slice_reduce_fusion
  10.0 0.1 eq.16
  10.1 1.2 copy.7
  11.3 2.6 fusion
  13.9 25.4 %compare_reduce_fusion = pred[2048,1024]{1,0:T(8,128)(4,1)S(1)} fusion(s32[1024]{0:T(1024)S(1)} %eq.16, s32[2048,16]{1,0:T(8,128)S(1)} %copy.7), kind=kLoop, calls=%fused_computation | loop fusion | flops 65011712 | bytes 2232320 | tf_op jit(solution)/shard_map/reduce_or | solution.py:43
  39.4 115.7 %all-gather.2.cloned.1.call-done = bf16[1024,768]{1,0:T(8,128)(2,1)} async-done(((bf16[16,768]{1,0:T(8,128)(2,1)}), bf16[1024,768]{1,0:T(8,128)(2,1)}) %all-gather.2.cloned.1.call-update) | async-done | bytes 1572880 | tf_op jit(solution)/shard_map/all_gather | solution.py:39
  155.1 10.1 %fusion.6 = (f32[2048]{0:T(1024)S(1)}, f32[2048,1024]{1,0:T(8,128)}) fusion(pred[2048,1024]{1,0:T(8,128)(4,1)S(1)} %compare_reduce_fusion, bf16[1024,768]{1,0:T(8,128)(2,1)} %all-gather.2.cloned.1.call-done, bf16[2048,768]{1,0:T(8,128)(2,1)} %param.4, f32[2048]{0:T(1024)S(1)} %add_rsqrt_fusion), kind=kOutput, calls=%fused_computation.31 | convolution fusion | flops 3232233472 | bytes 15220736 | tf_op jit(solution)/shard_map/dot_general | solution.py:40
  165.2 10.5 %psum.63 = f32[2048]{0:T(1024)S(1)} all-reduce(f32[2048]{0:T(1024)S(1)} %get-tuple-element.5), channel_id=1, replica_groups=mesh['dp'=64,'cent'=8] {'cent'}, use_global_device_ids=true, to_apply=%region_4.5 | all-reduce | flops 2048 | bytes 16384 | tf_op jit(solution)/shard_map/psum | solution.py:18
  175.7 4.0 multiply_reduce_fusion.5
  179.7 141.3 %psum.64 = f32[1024]{0:T(1024)S(1)} all-reduce(f32[1024]{0:T(1024)S(1)} %multiply_reduce_fusion.5), channel_id=1, replica_groups=mesh['dp'=64,'cent'=8] {'dp'}, use_global_device_ids=true, to_apply=%region_6.7 | all-reduce | flops 1024 | bytes 8192 | tf_op jit(solution)/shard_map/psum | solution.py:24
  321.0 4.0 multiply_reduce_fusion.4
  325.0 10.3 %psum.65 = f32[2048]{0:T(1024)S(1)} all-reduce(f32[2048]{0:T(1024)S(1)} %multiply_reduce_fusion.4), channel_id=1, replica_groups=mesh['dp'=64,'cent'=8] {'cent'}, use_global_device_ids=true, to_apply=%region_8.9 | all-reduce | flops 2048 | bytes 16384 | tf_op jit(solution)/shard_map/psum | solution.py:18
  335.3 4.0 multiply_reduce_fusion.3
  339.3 138.0 %psum.66 = f32[1024]{0:T(1024)S(1)} all-reduce(f32[1024]{0:T(1024)S(1)} %multiply_reduce_fusion.3), channel_id=1, replica_groups=mesh['dp'=64,'cent'=8] {'dp'}, use_global_device_ids=true, to_apply=%region_10.11 | all-reduce | flops 1024 | bytes 8192 | tf_op jit(solution)/shard_map/psum | solution.py:24
  477.3 4.0 multiply_reduce_fusion.2
  481.3 11.4 %psum.67 = f32[2048]{0:T(1024)S(1)} all-reduce(f32[2048]{0:T(1024)S(1)} %multiply_reduce_fusion.2), channel_id=1, replica_groups=mesh['dp'=64,'cent'=8] {'cent'}, use_global_device_ids=true, to_apply=%region_12.13 | all-reduce | flops 2048 | bytes 16384 | tf_op jit(solution)/shard_map/psum | solution.py:18
  492.8 4.1 multiply_reduce_fusion.1
  496.9 140.1 %psum.68 = f32[1024]{0:T(1024)S(1)} all-reduce(f32[1024]{0:T(1024)S(1)} %multiply_reduce_fusion.1), channel_id=1, replica_groups=mesh['dp'=64,'cent'=8] {'dp'}, use_global_device_ids=true, to_apply=%region_14.15 | all-reduce | flops 1024 | bytes 8192 | tf_op jit(solution)/shard_map/psum | solution.py:24
  637.1 4.0 multiply_reduce_fusion
  641.1 12.7 %psum.69 = f32[2048]{0:T(1024)S(1)} all-reduce(f32[2048]{0:T(1024)S(1)} %multiply_reduce_fusion), channel_id=1, replica_groups=mesh['dp'=64,'cent'=8] {'cent'}, use_global_device_ids=true, to_apply=%region_16.17 | all-reduce | flops 2048 | bytes 16384 | tf_op jit(solution)/shard_map/psum | solution.py:18
  653.8 8.9 fusion.2
  662.7 0.0 all-reduce.2.cloned.1.call-update
  662.7 4.0 multiply_reduce_fusion.6
  666.7 138.1 %psum.71 = f32[1024]{0:T(1024)S(1)} all-reduce(f32[1024]{0:T(1024)S(1)} %multiply_reduce_fusion.6), channel_id=1, replica_groups=mesh['dp'=64,'cent'=8] {'dp'}, use_global_device_ids=true, to_apply=%region_19.20 | all-reduce | flops 1024 | bytes 8192 | tf_op jit(solution)/shard_map/psum | solution.py:61
  804.8 0.1 dynamic-slice_add_fusion
  804.9 134.9 %all-reduce.2.cloned.1.call-done = f32[1024,768]{1,0:T(8,128)} async-done(((f32[1024,768]{1,0:T(8,128)}), f32[1024,768]{1,0:T(8,128)}) %all-reduce.2.cloned.1.call-update) | async-done | bytes 3145744 | tf_op jit(solution)/shard_map/psum | solution.py:61
  939.8 1.5 add_divide_fusion
  (14 shorter events, 0.1 us)
Async XLA Ops:
  6.5 148.5 %all-gather.2.cloned.1.call-start = ((), (), s32[]{:S(2)}) async-start(), calls=%async_computation | async-start | bytes 1597440 | tf_op jit(solution)/shard_map/all_gather | solution.py:39
  9.0 930.8 %all-reduce.2.cloned.1.call-start = ((), (), s32[]{:S(2)}) async-start(), calls=%async_computation.1 | async-start | bytes 6291456 | tf_op jit(solution)/shard_map/psum | solution.py:61
  492.8 161.0 %copy-start = (bf16[2048,768]{1,0:T(8,128)(2,1)S(1)}, bf16[2048,768]{1,0:T(8,128)(2,1)}, u32[]{:S(2)}) copy-start(bf16[2048,768]{1,0:T(8,128)(2,1)} %param.4) | copy-start | bytes 9437188
  662.7 277.1 %copy-start.1 = (f32[16,768]{1,0:T(8,128)S(1)}, f32[16,768]{1,0:T(8,128)}, u32[]{:S(2)}) copy-start(f32[16,768]{1,0:T(8,128)} %param.6) | copy-start | bytes 147460
Sparse Core Ops, SparseCore 0:
  10.3 144.7 all-gather.1
  662.8 276.8 all-reduce.1
where the time goes:
time: 949 us; the launch traced here: 948 us
  blocking collectives  602 us (63%)
  waiting for transfers between devices  251 us (26%)
  other arithmetic  60.2 us (6%)
  matrix products  19 us (2%)
  between operations  13.6 us (1%)
    psum x3, blocking collectives, column_scale(): return desired_load / lax.psum(column, 'dp')  419 us
    psum x1, blocking collectives, per_device(): numer_all, mass_all = lax.psum((numerator, col_mass), 'dp')  138 us
    psum x1, waiting for transfers between devices, per_device(): numer_all, mass_all = lax.psum((numerator, col_mass), 'dp')  135 us
    all_gather x1, waiting for transfers between devices, per_device(): group_centroids = lax.all_gather(unit_c, 'dp', axis=0, tiled=True)  116 us
    psum x4, blocking collectives, row_scale(): lax.psum(jnp.sum(similarity_exponential * col_factor[None, :], axis=1), '...  44.8 us
    reduce_or x1, other arithmetic, per_device(): jnp.any(coarse_ids[:, :, None] == group_ids[None, None, :], axis=1)  25.4 us
  transfers between devices with their start and end apart: 2, of which 2 were waited for; matrix products, arithmetic and copies ran while one was open for 4% of the time, Pallas kernels for 0%

commit v1 on v0

v1 whole, which is shorter than its diff:
```python
import jax
import jax.numpy as jnp
from jax import lax
from jax.sharding import Mesh
from jax.sharding import PartitionSpec as P

SWEEPS = 3


entropic_smoothing = 0.03


def unit_rows(values):
    values = values.astype(jnp.float32)
    return values * lax.rsqrt(jnp.sum(values * values, axis=-1, keepdims=True) + 1e-06)


def exchange(blocks, axes):
    return lax.all_to_all(blocks, axes, 0, 0)


def spread(block, axes):
    copies = jnp.broadcast_to(block[None], (lax.axis_size(axes),) + block.shape)
    return exchange(copies, axes)


def row_scale(similarity_exponential, col_factor):
    part = jnp.sum(similarity_exponential * col_factor[None, :], axis=1)
    totals = jnp.sum(spread(part.reshape(-1, 128), ("y", "core")), axis=0)
    return 1.0 / totals.reshape(-1)


def column_scale(similarity_exponential, row_scaling, desired_load):
    part = jnp.sum(similarity_exponential * row_scaling[:, None], axis=0).reshape(-1, 128)
    part = jnp.sum(spread(part, "x"), axis=0)
    part = jnp.sum(spread(part, "z"), axis=0)
    return desired_load / part.reshape(-1)


def per_device(embeddings, coarse_ids, centroids, coarse_of):
    row_count = embeddings.shape[0]
    local_count, width = centroids.shape
    x_size, z_size = lax.axis_size("x"), lax.axis_size("z")
    dp_size = x_size * z_size
    cent_size = lax.axis_size(("y", "core"))
    desired_load = row_count / (local_count * cent_size)
    unit_x = unit_rows(embeddings).astype(jnp.bfloat16)
    unit_c = unit_rows(centroids).astype(jnp.bfloat16)
    layout_table = coarse_of.reshape(dp_size, cent_size, local_count)
    group_ids = lax.dynamic_slice_in_dim(
        layout_table, lax.axis_index(("y", "core")), 1, 1
    ).reshape(dp_size * local_count)
    along_z = spread(unit_c, "z")
    group_centroids = spread(along_z, "x").reshape(dp_size * local_count, width)
    pairwise_dots = lax.dot_general(
        unit_x, group_centroids, (((1,), (1,)), ((), ())), preferred_element_type=jnp.float32
    )
    assigned_points = jnp.any(coarse_ids[:, :, None] == group_ids[None, None, :], axis=1)
    similarity_exponential = jnp.where(
        assigned_points, jnp.exp(pairwise_dots / entropic_smoothing), 0.0
    )
    row_scaling = row_scale(
        similarity_exponential, jnp.ones((similarity_exponential.shape[1],), jnp.float32)
    )
    for sweep in range(SWEEPS):
        col_factor = column_scale(similarity_exponential, row_scaling, desired_load)
        row_scaling = row_scale(similarity_exponential, col_factor)
    weighted = similarity_exponential * row_scaling[:, None]
    col_mass = jnp.sum(weighted, axis=0)
    numerator = lax.dot_general(
        weighted.astype(jnp.bfloat16),
        embeddings,
        (((0,), (0,)), ((), ())),
        preferred_element_type=jnp.float32,
    )
    sums = jnp.concatenate(
        [numerator, jnp.broadcast_to(col_mass[:, None], (col_mass.shape[0], 128))], axis=1
    )
    sums = sums.astype(jnp.bfloat16).reshape(x_size, z_size, local_count, width + 128)
    sums = jnp.sum(exchange(sums, "x").astype(jnp.float32), axis=0)
    sums = jnp.sum(exchange(sums.astype(jnp.bfloat16), "z").astype(jnp.float32), axis=0)
    numer_own, mass_own = sums[:, :width], sums[:, width]
    return (numer_own + centroids) / (mass_own + 1.0)[:, None]


def solution(mesh):
    fine = Mesh(mesh.devices.reshape(4, 16, 4, 2), ("x", "z", "y", "core"))
    return jax.shard_map(
        per_device,
        mesh=fine,
        in_specs=(
            P(("x", "z"), None),
            P(("x", "z"), None),
            P(("x", "z", "y", "core"), None),
            P(),
        ),
        out_specs=P(("x", "z", "y", "core"), None),
        check_vma=False,
    )
```

time: 949 us -> 287 us (0.30)
  the two profiles are of different devices: /device:TPU:16 before, /device:TPU:32 now
where the time goes in v1:
time: 287 us; the launch traced here: 286 us
  blocking collectives  165 us (57%)
  other arithmetic  60.9 us (21%)
  starting transfers between devices  19.6 us (7%)
  matrix products  18.3 us (6%)
  waiting for transfers between devices  17 us (6%)
  local copies, waits for them, and re-layouts  4.69 us (2%)
    all_to_all x12, blocking collectives, exchange(): return lax.all_to_all(blocks, axes, 0, 0)  165 us
    reduce_or x1, other arithmetic, per_device(): jnp.any(coarse_ids[:, :, None] == group_ids[None, None, :], axis=1)  25.4 us
    all_to_all x2, starting transfers between devices, exchange(): return lax.all_to_all(blocks, axes, 0, 0)  19.6 us
    all_to_all x2, waiting for transfers between devices, exchange(): return lax.all_to_all(blocks, axes, 0, 0)  17 us
    reduce_sum x3, other arithmetic, row_scale(): part = jnp.sum(similarity_exponential * col_factor[None, :], axis=1)  12.1 us
    reduce_sum x3, other arithmetic, column_scale(): jnp.sum(similarity_exponential * row_scaling[:, None], axis=0)  12 us
    dot_general x1, matrix products, per_device(): lax.dot_general(unit_x, group_centroids, (((1,), (1,)), ((), ())), prefer...  10 us
    dot_general x1, matrix products, per_device(): lax.dot_general(weighted.astype(jnp.bfloat16), embeddings, (((0,), (0,)),...  8.3 us
  transfers between devices with their start and end apart: 2, of which 1 were waited for; matrix products, arithmetic and copies ran while one was open for 11% of the time, Pallas kernels for 0%

profile of v1, /device:TPU:32, one launch (start us, length us, event | category | flops | bytes accessed | tf_op | source)
XLA Modules:
  0.0 285.8 jit_solution(9015270200386856043)
XLA Ops:
  0.0 0.9 multiply_reduce_fusion.7
  0.9 0.9 multiply_convert_fusion.4
  2.6 15.2 %all-to-all-start = ((bf16[16,16,768]{2,1,0:T(8,128)(2,1)}), bf16[16,16,768]{2,1,0:T(8,128)(2,1)S(1)}, u32[]{:S(2)}, u32[]{:S(2)}) async-start(bf16[16,16,768]{2,1,0:T(8,128)(2,1)} %broadcast_in_dim.46), calls=%async_computation | async-start | bytes 786432 | tf_op jit(solution)/shard_map/all_to_all | solution.py:19
  17.8 0.9 reshape.98
  18.9 1.2 copy.7
  20.1 2.6 fusion
  22.7 17.0 %all-to-all-done = bf16[16,16,768]{2,1,0:T(8,128)(2,1)S(1)} async-done(((bf16[16,16,768]{2,1,0:T(8,128)(2,1)}), bf16[16,16,768]{2,1,0:T(8,128)(2,1)S(1)}, u32[]{:S(2)}, u32[]{:S(2)}) %all-to-all-start) | async-done | bytes 393248 | tf_op jit(solution)/shard_map/all_to_all | solution.py:19
  39.7 1.3 broadcast_in_dim.47
  40.9 4.4 %all-to-all-start.1 = ((bf16[4,16,16,768]{3,2,1,0:T(8,128)(2,1)}), bf16[4,16,16,768]{3,2,1,0:T(8,128)(2,1)}, u32[]{:S(2)}, u32[]{:S(2)}) async-start(bf16[4,16,16,768]{3,2,1,0:T(8,128)(2,1)} %broadcast_in_dim.47), calls=%async_computation.1 | async-start | bytes 3145728 | tf_op jit(solution)/shard_map/all_to_all | solution.py:19
  45.3 25.4 %compare_reduce_fusion = pred[2048,1024]{1,0:T(8,128)(4,1)S(1)} fusion(s32[1024]{0:T(1024)S(1)} %eq.16, s32[2048,16]{1,0:T(8,128)S(1)} %copy.7), kind=kLoop, calls=%fused_computation | loop fusion | flops 65011712 | bytes 2232320 | tf_op jit(solution)/shard_map/reduce_or | solution.py:58
  70.8 10.0 %fusion.9 = (f32[2048]{0:T(1024)S(1)}, f32[2048,1024]{1,0:T(8,128)}) fusion(pred[2048,1024]{1,0:T(8,128)(4,1)S(1)} %compare_reduce_fusion, bf16[1024,768]{1,0:T(8,128)(2,1)} %bitcast, bf16[2048,768]{1,0:T(8,128)(2,1)} %param.4, f32[2048]{0:T(1024)S(1)} %add_rsqrt_fusion), kind=kOutput, calls=%fused_computation.36 | convolution fusion | flops 3232233472 | bytes 15220736 | tf_op jit(solution)/shard_map/dot_general | solution.py:55
  80.8 9.9 %all_to_all.70 = f32[8,16,128]{2,1,0:T(8,128)S(1)} all-to-all(f32[8,16,128]{2,1,0:T(8,128)S(1)} %broadcast_in_dim.50), channel_id=1, replica_groups=mesh['x'=4,'z'=16,'y'=4,'core'=2] {'y','core'}, dimensions={0} | all-to-all | bytes 131072 | tf_op jit(solution)/shard_map/all_to_all | solution.py:19
  90.7 4.0 %multiply_reduce_fusion.5 = f32[1024]{0:T(1024)S(1)} fusion(f32[2048,1024]{1,0:T(8,128)} %get-tuple-element.6, f32[2048]{0:T(1024)S(1)} %divide_bitcast_fusion.3), kind=kLoop, calls=%fused_computation.6 | loop fusion | flops 4193280 | bytes 8400896 | tf_op jit(solution)/shard_map/reduce_sum | solution.py:34
  94.7 9.9 %all_to_all.71 = f32[4,8,128]{2,1,0:T(8,128)S(1)} all-to-all(f32[4,8,128]{2,1,0:T(8,128)S(1)} %broadcast_in_dim.52), channel_id=1, replica_groups=mesh['x'=4,'z'=16,'y'=4,'core'=2] {'x'}, dimensions={0} | all-to-all | bytes 32768 | tf_op jit(solution)/shard_map/all_to_all | solution.py:19
  104.7 19.5 %all_to_all.72 = f32[16,8,128]{2,1,0:T(8,128)S(1)} all-to-all(f32[16,8,128]{2,1,0:T(8,128)S(1)} %broadcast_in_dim.53), channel_id=1, replica_groups=mesh['x'=4,'z'=16,'y'=4,'core'=2] {'z'}, dimensions={0} | all-to-all | bytes 131072 | tf_op jit(solution)/shard_map/all_to_all | solution.py:19
  124.2 4.0 %multiply_reduce_fusion.4 = f32[2048]{0:T(1024)S(1)} fusion(f32[2048,1024]{1,0:T(8,128)} %get-tuple-element.6, f32[1024]{0:T(1024)S(1)} %divide_bitcast_fusion.6), kind=kLoop, calls=%fused_computation.5 | loop fusion | flops 4192256 | bytes 8400896 | tf_op jit(solution)/shard_map/reduce_sum | solution.py:28
  128.2 8.0 %all_to_all.73 = f32[8,16,128]{2,1,0:T(8,128)S(1)} all-to-all(f32[8,16,128]{2,1,0:T(8,128)S(1)} %broadcast_in_dim.55), channel_id=1, replica_groups=mesh['x'=4,'z'=16,'y'=4,'core'=2] {'y','core'}, dimensions={0} | all-to-all | bytes 131072 | tf_op jit(solution)/shard_map/all_to_all | solution.py:19
  136.3 4.0 %multiply_reduce_fusion.3 = f32[1024]{0:T(1024)S(1)} fusion(f32[2048,1024]{1,0:T(8,128)} %get-tuple-element.6, f32[2048]{0:T(1024)S(1)} %divide_bitcast_fusion.2), kind=kLoop, calls=%fused_computation.4 | loop fusion | flops 4193280 | bytes 8400896 | tf_op jit(solution)/shard_map/reduce_sum | solution.py:34
  140.3 7.7 %all_to_all.74 = f32[4,8,128]{2,1,0:T(8,128)S(1)} all-to-all(f32[4,8,128]{2,1,0:T(8,128)S(1)} %broadcast_in_dim.57), channel_id=1, replica_groups=mesh['x'=4,'z'=16,'y'=4,'core'=2] {'x'}, dimensions={0} | all-to-all | bytes 32768 | tf_op jit(solution)/shard_map/all_to_all | solution.py:19
  148.0 15.4 %all_to_all.75 = f32[16,8,128]{2,1,0:T(8,128)S(1)} all-to-all(f32[16,8,128]{2,1,0:T(8,128)S(1)} %broadcast_in_dim.114), channel_id=1, replica_groups=mesh['x'=4,'z'=16,'y'=4,'core'=2] {'z'}, dimensions={0} | all-to-all | bytes 131072 | tf_op jit(solution)/shard_map/all_to_all | solution.py:19
  163.4 4.0 %multiply_reduce_fusion.2 = f32[2048]{0:T(1024)S(1)} fusion(f32[2048,1024]{1,0:T(8,128)} %get-tuple-element.6, f32[1024]{0:T(1024)S(1)} %divide_bitcast_fusion.5), kind=kLoop, calls=%fused_computation.3 | loop fusion | flops 4192256 | bytes 8400896 | tf_op jit(solution)/shard_map/reduce_sum | solution.py:28
  167.4 8.0 %all_to_all.76 = f32[8,16,128]{2,1,0:T(8,128)S(1)} all-to-all(f32[8,16,128]{2,1,0:T(8,128)S(1)} %broadcast_in_dim.116), channel_id=1, replica_groups=mesh['x'=4,'z'=16,'y'=4,'core'=2] {'y','core'}, dimensions={0} | all-to-all | bytes 131072 | tf_op jit(solution)/shard_map/all_to_all | solution.py:19
  175.5 4.0 %multiply_reduce_fusion.1 = f32[1024]{0:T(1024)S(1)} fusion(f32[2048,1024]{1,0:T(8,128)} %get-tuple-element.6, f32[2048]{0:T(1024)S(1)} %divide_bitcast_fusion.1), kind=kLoop, calls=%fused_computation.2 | loop fusion | flops 4193280 | bytes 8400896 | tf_op jit(solution)/shard_map/reduce_sum | solution.py:34
  179.5 7.7 %all_to_all.77 = f32[4,8,128]{2,1,0:T(8,128)S(1)} all-to-all(f32[4,8,128]{2,1,0:T(8,128)S(1)} %broadcast_in_dim.118), channel_id=1, replica_groups=mesh['x'=4,'z'=16,'y'=4,'core'=2] {'x'}, dimensions={0} | all-to-all | bytes 32768 | tf_op jit(solution)/shard_map/all_to_all | solution.py:19
  187.2 15.5 %all_to_all.78 = f32[16,8,128]{2,1,0:T(8,128)S(1)} all-to-all(f32[16,8,128]{2,1,0:T(8,128)S(1)} %broadcast_in_dim.119), channel_id=1, replica_groups=mesh['x'=4,'z'=16,'y'=4,'core'=2] {'z'}, dimensions={0} | all-to-all | bytes 131072 | tf_op jit(solution)/shard_map/all_to_all | solution.py:19
  202.8 4.0 %multiply_reduce_fusion = f32[2048]{0:T(1024)S(1)} fusion(f32[2048,1024]{1,0:T(8,128)} %get-tuple-element.6, f32[1024]{0:T(1024)S(1)} %divide_bitcast_fusion.4), kind=kLoop, calls=%fused_computation.1 | loop fusion | flops 4192256 | bytes 8400896 | tf_op jit(solution)/shard_map/reduce_sum | solution.py:28
  206.8 8.3 %all_to_all.79 = f32[8,16,128]{2,1,0:T(8,128)S(1)} all-to-all(f32[8,16,128]{2,1,0:T(8,128)S(1)} %broadcast_in_dim.121), channel_id=1, replica_groups=mesh['x'=4,'z'=16,'y'=4,'core'=2] {'y','core'}, dimensions={0} | all-to-all | bytes 131072 | tf_op jit(solution)/shard_map/all_to_all | solution.py:19
  215.1 4.0 %multiply_reduce_fusion.6 = bf16[1024]{0:T(1024)(128)(2,1)S(1)} fusion(f32[2048,1024]{1,0:T(8,128)} %get-tuple-element.6, f32[2048]{0:T(1024)S(1)} %divide_bitcast_fusion), kind=kLoop, calls=%fused_computation.8 | loop fusion | flops 4193280 | bytes 8398848 | tf_op jit(solution)/shard_map/reduce_sum | solution.py:69
  219.1 8.3 %fusion.6 = bf16[1024,768]{1,0:T(8,128)(2,1)} fusion(bf16[2048,768]{1,0:T(8,128)(2,1)S(1)} %copy-done, f32[2048,1024]{1,0:T(8,128)} %get-tuple-element.6, f32[2048]{0:T(1024)S(1)} %divide_bitcast_fusion), kind=kOutput, calls=%fused_computation.18 | convolution fusion | flops 3226206208 | bytes 13115392 | tf_op jit(solution)/shard_map/dot_general | solution.py:70
  227.7 1.6 pad_maximum_fusion
  229.3 26.2 %all_to_all.80 = bf16[4,16,16,896]{3,2,1,0:T(8,128)(2,1)S(1)} all-to-all(bf16[4,16,16,896]{3,2,1,0:T(8,128)(2,1)S(1)} %pad_maximum_fusion), channel_id=1, replica_groups=mesh['x'=4,'z'=16,'y'=4,'core'=2] {'x'}, dimensions={0} | all-to-all | bytes 3670016 | tf_op jit(solution)/shard_map/all_to_all | solution.py:19
  255.9 29.0 %all_to_all.81 = bf16[16,16,896]{2,1,0:T(8,128)(2,1)S(1)} all-to-all(bf16[16,16,896]{2,1,0:T(8,128)(2,1)S(1)} %reduce_sum.221), channel_id=1, replica_groups=mesh['x'=4,'z'=16,'y'=4,'core'=2] {'z'}, dimensions={0} | all-to-all | bytes 917504 | tf_op jit(solution)/shard_map/all_to_all | solution.py:19
  (43 shorter events, 2.8 us)
Async XLA Ops:
  2.6 37.1 %all-to-all-start = ((bf16[16,16,768]{2,1,0:T(8,128)(2,1)}), bf16[16,16,768]{2,1,0:T(8,128)(2,1)S(1)}, u32[]{:S(2)}, u32[]{:S(2)}) async-start(bf16[16,16,768]{2,1,0:T(8,128)(2,1)} %broadcast_in_dim.46), calls=%async_computation | async-start | bytes 786432 | tf_op jit(solution)/shard_map/all_to_all | solution.py:19
  40.9 29.8 %all-to-all-start.1 = ((bf16[4,16,16,768]{3,2,1,0:T(8,128)(2,1)}), bf16[4,16,16,768]{3,2,1,0:T(8,128)(2,1)}, u32[]{:S(2)}, u32[]{:S(2)}) async-start(bf16[4,16,16,768]{3,2,1,0:T(8,128)(2,1)} %broadcast_in_dim.47), calls=%async_computation.1 | async-start | bytes 3145728 | tf_op jit(solution)/shard_map/all_to_all | solution.py:19
  206.8 12.3 %copy-start = (bf16[2048,768]{1,0:T(8,128)(2,1)S(1)}, bf16[2048,768]{1,0:T(8,128)(2,1)}, u32[]{:S(2)}) copy-start(bf16[2048,768]{1,0:T(8,128)(2,1)} %param.4) | copy-start | bytes 9437188
  227.4 57.7 %copy-start.1 = (f32[16,768]{1,0:T(8,128)S(1)}, f32[16,768]{1,0:T(8,128)}, u32[]{:S(2)}) copy-start(f32[16,768]{1,0:T(8,128)} %param.6) | copy-start | bytes 147460

commit v2 on v1

v2 whole, which is shorter than its diff:
```python
import functools
import math

import jax
import jax.numpy as jnp
from jax import lax
from jax.experimental import pallas as pl
from jax.experimental.pallas import tpu as pltpu
from jax.sharding import Mesh
from jax.sharding import PartitionSpec as P

SWEEPS = 3
CLUSTERS = 512
LANES = 128
TILE = 256


entropic_smoothing = 0.03
MIB = 1 << 20
f32, bf16 = jnp.float32, jnp.bfloat16


def unit_rows(values):
    values = values.astype(f32)
    return values * lax.rsqrt(jnp.sum(values * values, axis=-1, keepdims=True) + 1e-06)


def exchange(blocks, axes):
    return lax.all_to_all(blocks, axes, 0, 0)


def spread(block, axes):
    copies = jnp.broadcast_to(block[None], (lax.axis_size(axes),) + block.shape)
    return exchange(copies, axes)


def as_row(tiles):
    return jnp.concatenate([tiles[q : q + 1] for q in range(tiles.shape[0])], axis=1)


def as_tiles(row):
    count = row.shape[1] // LANES
    return jnp.concatenate([row[:, q * LANES : (q + 1) * LANES] for q in range(count)], axis=0)


def two_terms(row):
    wide = jnp.broadcast_to(row, (16, row.shape[1]))
    high = wide.astype(bf16).astype(f32)
    which = lax.broadcasted_iota(jnp.int32, wide.shape, 0)
    rest = jnp.where(which == 1, wide - high, 0.0)
    return jnp.where(which == 0, high, rest).astype(bf16)


def prepare_kernel(x_ref, ids_ref, group_ref, unit_ref, match_ref, hot_ref):
    @pl.when(pl.program_id(0) == 0)
    def _():
        cluster = lax.broadcasted_iota(jnp.int32, hot_ref.shape, 0)
        hot_ref[...] = jnp.where(cluster == group_ref[...], 1.0, 0.0).astype(bf16)

    unit_ref[...] = unit_rows(x_ref[...]).astype(bf16)
    ids = ids_ref[...]
    cluster = lax.broadcasted_iota(jnp.int32, (ids.shape[0], CLUSTERS), 1)
    picked = jnp.zeros(cluster.shape, f32)
    for p in range(ids.shape[1]):
        picked = jnp.where(ids[:, p : p + 1] == cluster, 1.0, picked)
    match_ref[...] = jnp.dot(picked.astype(bf16), hot_ref[...], preferred_element_type=f32).astype(bf16)


def similarity_kernel(unit_ref, cent_ref, match_ref, sim_ref, total_ref):
    ones = jnp.ones((total_ref.shape[0], sim_ref.shape[1]), bf16)
    scale = math.log2(math.e) / entropic_smoothing
    for b in range(unit_ref.shape[0] // TILE):
        rows = pl.ds(b * TILE, TILE)
        dots = lax.dot_general(
            unit_ref[rows, :], cent_ref[...], (((1,), (1,)), ((), ())), preferred_element_type=f32
        )
        sim = (jnp.exp2(dots * scale) * match_ref[rows, :].astype(f32)).astype(bf16)
        sim_ref[rows, :] = sim
        totals = lax.dot_general(ones, sim, (((1,), (1,)), ((), ())), preferred_element_type=f32)
        for q in range(TILE // LANES):
            total_ref[:, b * (TILE // LANES) + q, :] = totals[:, q * LANES : (q + 1) * LANES]


def column_kernel(parts_ref, sim_ref, out_ref):
    factor = 1.0 / jnp.sum(parts_ref[...], axis=0)
    lhs = two_terms(as_row(factor))
    sums = jnp.dot(lhs, sim_ref[...], preferred_element_type=f32)
    out_ref[...] = jnp.broadcast_to(as_tiles(jnp.sum(sums, axis=0, keepdims=True))[None], out_ref.shape)


def row_kernel(desired_load, parts_ref, sim_ref, out_ref):
    factor = desired_load / jnp.sum(parts_ref[...], axis=0)
    lhs = two_terms(as_row(factor))
    sums = lax.dot_general(lhs, sim_ref[...], (((1,), (1,)), ((), ())), preferred_element_type=f32)
    out_ref[...] = jnp.broadcast_to(as_tiles(jnp.sum(sums, axis=0, keepdims=True))[None], out_ref.shape)


def down(row):
    return jnp.transpose(jnp.broadcast_to(row, (LANES, LANES)))


def numerator_kernel(parts_ref, sim_ref, x_ref, out_ref, weight_ref):
    factor = 1.0 / jnp.sum(parts_ref[...], axis=0)
    lhs = two_terms(as_row(factor))
    mass = jnp.sum(jnp.dot(lhs, sim_ref[...], preferred_element_type=f32), axis=0, keepdims=True)
    columns = sim_ref.shape[1]
    for q in range(sim_ref.shape[0] // LANES):
        rows = pl.ds(q * LANES, LANES)
        scale = jnp.concatenate([down(factor[q : q + 1])] * (columns // LANES), axis=1)
        weight_ref[rows, :] = (sim_ref[rows, :].astype(f32) * scale).astype(bf16)
    width = x_ref.shape[1]
    for b in range(columns // TILE):
        rows = pl.ds(b * TILE, TILE)
        out_ref[rows, :width] = lax.dot_general(
            weight_ref[:, rows], x_ref[...], (((0,), (0,)), ((), ())), preferred_element_type=f32
        ).astype(bf16)
    for q in range(columns // LANES):
        out_ref[pl.ds(q * LANES, LANES), width:] = down(mass[:, q * LANES : (q + 1) * LANES]).astype(bf16)


def call(kernel, name, operands, outs, mib, flops, scratch=()):
    moved = sum(math.prod(o.shape) * o.dtype.itemsize for o in (*operands, *outs))
    vmem = pl.BlockSpec(memory_space=pltpu.VMEM)
    single = len(outs) == 1
    return pl.pallas_call(
        kernel,
        name=name,
        out_shape=outs[0] if single else outs,
        in_specs=[vmem] * len(operands),
        out_specs=vmem if single else [vmem] * len(outs),
        scratch_shapes=scratch,
        compiler_params=pltpu.CompilerParams(vmem_limit_bytes=mib * MIB),
        cost_estimate=pl.CostEstimate(flops=flops, bytes_accessed=moved, transcendentals=0),
    )(*operands)


def prepare(embeddings, coarse_ids, group_ids):
    rows, width = embeddings.shape
    columns = group_ids.shape[1]
    return pl.pallas_call(
        prepare_kernel,
        name="prepare",
        grid=(rows // TILE,),
        in_specs=[
            pl.BlockSpec((TILE, width), lambda i: (i, 0)),
            pl.BlockSpec((TILE, coarse_ids.shape[1]), lambda i: (i, 0)),
            pl.BlockSpec((1, columns), lambda i: (0, 0)),
        ],
        out_specs=[
            pl.BlockSpec((TILE, width), lambda i: (i, 0)),
            pl.BlockSpec((TILE, columns), lambda i: (i, 0)),
        ],
        out_shape=[
            jax.ShapeDtypeStruct((rows, width), bf16),
            jax.ShapeDtypeStruct((rows, columns), bf16),
        ],
        scratch_shapes=[pltpu.VMEM((CLUSTERS, columns), bf16)],
        compiler_params=pltpu.CompilerParams(vmem_limit_bytes=16 * MIB),
        cost_estimate=pl.CostEstimate(
            flops=8 * rows * CLUSTERS * columns, bytes_accessed=32 * rows * width, transcendentals=0
        ),
    )(embeddings, coarse_ids, group_ids)


def per_device(embeddings, coarse_ids, centroids, coarse_of):
    row_count, width = embeddings.shape
    local_count = centroids.shape[0]
    x_size, z_size = lax.axis_size("x"), lax.axis_size("z")
    dp_size = x_size * z_size
    cent_size = lax.axis_size(("y", "core"))
    columns = dp_size * local_count
    desired_load = row_count / (local_count * cent_size)
    unit_c = unit_rows(centroids).astype(bf16)
    layout_table = coarse_of.reshape(dp_size, cent_size, local_count)
    group_ids = lax.dynamic_slice_in_dim(
        layout_table, lax.axis_index(("y", "core")), 1, 1
    ).reshape(1, columns)
    unit_x, matched = prepare(embeddings, coarse_ids, group_ids)
    along_z = spread(unit_c, "z")
    group_centroids = spread(along_z, "x").reshape(columns, width)

    product = 2 * row_count * columns
    row_parts = jax.ShapeDtypeStruct((cent_size, row_count // LANES, LANES), f32)
    column_parts = jax.ShapeDtypeStruct((x_size, columns // LANES, LANES), f32)
    similarity, parts = call(
        similarity_kernel,
        "similarity",
        (unit_x, group_centroids, matched),
        (jax.ShapeDtypeStruct((row_count, columns), bf16), row_parts),
        16,
        product * width,
    )
    parts = exchange(parts, ("y", "core"))
    for sweep in range(SWEEPS):
        parts = call(column_kernel, "columns", (parts, similarity), (column_parts,), 8, product * 16)
        parts = jnp.sum(exchange(parts, "x"), axis=0)
        parts = spread(parts, "z")
        parts = call(
            functools.partial(row_kernel, desired_load),
            "rows",
            (parts, similarity),
            (row_parts,),
            8,
            product * 16,
        )
        parts = exchange(parts, ("y", "core"))
    sums = call(
        numerator_kernel,
        "numerator",
        (parts, similarity, embeddings),
        (jax.ShapeDtypeStruct((columns, width + LANES), bf16),),
        16,
        product * width,
        scratch=[pltpu.VMEM((row_count, columns), bf16)],
    )
    sums = sums.reshape(x_size, z_size, local_count, width + LANES)
    sums = jnp.sum(exchange(sums, "x").astype(f32), axis=0)
    sums = jnp.sum(exchange(sums.astype(bf16), "z").astype(f32), axis=0)
    numer_own, mass_own = sums[:, :width], sums[:, width]
    return (numer_own + centroids) / (mass_own + 1.0)[:, None]


def solution(mesh):
    fine = Mesh(mesh.devices.reshape(4, 16, 4, 2), ("x", "z", "y", "core"))
    return jax.shard_map(
        per_device,
        mesh=fine,
        in_specs=(
            P(("x", "z"), None),
            P(("x", "z"), None),
            P(("x", "z", "y", "core"), None),
            P(),
        ),
        out_specs=P(("x", "z", "y", "core"), None),
        check_vma=False,
    )
```

time: 287 us -> 258 us (0.90)
  other arithmetic: 60.9 us -> 3.15 us
  blocking collectives: 165 us -> 202 us
  Pallas kernels: 0 us -> 27.1 us
  matrix products: 18.3 us -> 0 us
  waiting for transfers between devices: 17 us -> 0.56 us
  local copies, waits for them, and re-layouts: 4.69 us -> 20.1 us
  starting transfers between devices: 19.6 us -> 4.29 us
    all_to_all x12 -> x13, blocking collectives: 165 us -> 202 us  [exchange(): return lax.all_to_all(blocks, axes, 0, 0)]
    reduce_sum x19 -> x5, other arithmetic: 28.7 us -> 0.53 us  [the longest x1 0.45 us: per_device(): sums = jnp.sum(exchange(sums, 'x').astype(f32), axis=0)]
    pallas_call x0 -> x9, Pallas kernels: none -> 27.1 us  [the longest x8 14.6 us: call(): pl.pallas_call(kernel, name=name, out_shape=outs[0] if single else outs,...]
    reduce_or x1 -> x0, other arithmetic: 25.4 us -> none  [per_device(): jnp.any(coarse_ids[:, :, None] == group_ids[None, None, :], axis=1)]
    dot_general x2 -> x0, matrix products: 18.3 us -> none  [the longest x1 10 us: per_device(): lax.dot_general(unit_x, group_centroids, (((1,), (1,)), ((), ())), prefer...]
    unnamed x5 -> x29, local copies, waits for them, and re-layouts: 1.24 us -> 18.4 us
    all_to_all x2 -> x1, waiting for transfers between devices: 17 us -> 0.56 us  [exchange(): return lax.all_to_all(blocks, axes, 0, 0)]
    all_to_all x2 -> x1, starting transfers between devices: 19.6 us -> 4.29 us  [exchange(): return lax.all_to_all(blocks, axes, 0, 0)]
  transfers between devices with their start and end apart: 2 -> 1, of which waited for: 1 -> 1; matrix products, arithmetic and copies ran while one was open for 11% -> 0% of each run, Pallas kernels for 0% -> 5%
where the time goes in v2:
time: 258 us; the launch traced here: 257 us
  blocking collectives  202 us (78%)
  Pallas kernels  27.1 us (11%)
  local copies, waits for them, and re-layouts  20.1 us (8%)
  starting transfers between devices  4.29 us (2%)
  other arithmetic  3.15 us (1%)
    all_to_all x13, blocking collectives, exchange(): return lax.all_to_all(blocks, axes, 0, 0)  202 us
    unnamed x29, local copies, waits for them, and re-layouts  18.4 us
    pallas_call x8, Pallas kernels, call(): pl.pallas_call(kernel, name=name, out_shape=outs[0] if single else outs,...  14.6 us
    pallas_call x1, Pallas kernels, prepare(): pl.pallas_call(prepare_kernel, name='prepare', grid=(rows // TILE,), in_s...  12.5 us
  transfers between devices with their start and end apart: 1, of which 1 were waited for; matrix products, arithmetic and copies ran while one was open for 0% of the time, Pallas kernels for 5%

profile of v2, /device:TPU:32, one launch (start us, length us, event | category | flops | bytes accessed | tf_op | source)
XLA Modules:
  0.0 257.1 jit_solution(5089206310497004609)
XLA Ops:
  0.0 0.9 multiply_reduce_fusion
  0.9 0.9 multiply_convert_fusion
  1.8 37.0 %all_to_all.70 = bf16[16,16,768]{2,1,0:T(8,128)(2,1)S(1)} all-to-all(bf16[16,16,768]{2,1,0:T(8,128)(2,1)S(1)} %broadcast_in_dim.10), channel_id=1, replica_groups=mesh['x'=4,'z'=16,'y'=4,'core'=2] {'z'}, dimensions={0} | all-to-all | bytes 786432 | tf_op jit(solution)/shard_map/all_to_all | solution.py:29
  38.9 1.4 broadcast_in_dim.11
  40.2 4.3 %all-to-all-start.1 = ((bf16[4,16,16,768]{3,2,1,0:T(8,128)(2,1)}), bf16[4,16,16,768]{3,2,1,0:T(8,128)(2,1)S(1)}, u32[]{:S(2)}, u32[]{:S(2)}) async-start(bf16[4,16,16,768]{3,2,1,0:T(8,128)(2,1)} %broadcast_in_dim.11), calls=%async_computation.1 | async-start | bytes 3145728 | tf_op jit(solution)/shard_map/all_to_all | solution.py:29
  45.2 1.9 copy-done.5
  47.1 12.5 %prepare.1 = (bf16[2048,768]{1,0:T(8,128)(2,1)S(1)}, bf16[2048,1024]{1,0:T(8,128)(2,1)S(1)}) custom-call(bf16[2048,768]{1,0:T(8,128)(2,1)S(1)} %copy-done.5, s32[2048,16]{1,0:T(8,128)S(1)} %copy.7.ids_ref, s32[1,1024]{1,0:T(1,128)S(1)} %reshape.24.group_ref), custom_call_target="tpu_custom_call" | custom-call | flops 8589934592 | bytes 50331648 | tf_op jit(solution)/shard_map/prepare/pallas_call | solution.py:140
  59.6 1.9 copy-done.7
  61.5 1.7 copy-done.9
  63.8 2.2 copy-done.8
  66.0 1.9 copy-done.10
  67.9 5.0 %similarity.1 = (bf16[2048,1024]{1,0:T(8,128)(2,1)S(1)}, f32[8,16,128]{2,1,0:T(8,128)S(1)}) custom-call(bf16[2048,768]{1,0:T(8,128)(2,1)S(1)} %copy-done.10, bf16[1024,768]{1,0:T(8,128)(2,1)S(1)} %bitcast.3, bf16[2048,1024]{1,0:T(8,128)(2,1)S(1)} %copy-done.8), custom_call_target="tpu_custom_call" | custom-call | flops 3221225472 | bytes 13172736 | tf_op jit(solution)/shard_map/similarity/pallas_call | solution.py:125
  72.9 9.9 %all_to_all.71.parts_ref = f32[8,16,128]{2,1,0:T(8,128)S(1)} all-to-all(f32[8,16,128]{2,1,0:T(8,128)S(1)} %get-tuple-element.11), channel_id=1, replica_groups=mesh['x'=4,'z'=16,'y'=4,'core'=2] {'y','core'}, dimensions={0} | all-to-all | bytes 131072 | tf_op jit(solution)/shard_map/all_to_all | solution.py:29
  83.5 1.9 copy-done
  85.4 9.4 %all_to_all.72 = f32[4,8,128]{2,1,0:T(8,128)S(1)} all-to-all(f32[4,8,128]{2,1,0:T(8,128)S(1)} %columns.3), channel_id=1, replica_groups=mesh['x'=4,'z'=16,'y'=4,'core'=2] {'x'}, dimensions={0} | all-to-all | bytes 32768 | tf_op jit(solution)/shard_map/all_to_all | solution.py:29
  94.8 19.5 %all_to_all.73.parts_ref = f32[16,8,128]{2,1,0:T(8,128)S(1)} all-to-all(f32[16,8,128]{2,1,0:T(8,128)S(1)} %broadcast_in_dim.12), channel_id=1, replica_groups=mesh['x'=4,'z'=16,'y'=4,'core'=2] {'z'}, dimensions={0} | all-to-all | bytes 131072 | tf_op jit(solution)/shard_map/all_to_all | solution.py:29
  114.3 2.2 copy-done.1
  116.5 1.2 rows.3
  117.7 8.0 %all_to_all.74.parts_ref = f32[8,16,128]{2,1,0:T(8,128)S(1)} all-to-all(f32[8,16,128]{2,1,0:T(8,128)S(1)} %rows.3), channel_id=1, replica_groups=mesh['x'=4,'z'=16,'y'=4,'core'=2] {'y','core'}, dimensions={0} | all-to-all | bytes 131072 | tf_op jit(solution)/shard_map/all_to_all | solution.py:29
  126.4 7.7 %all_to_all.75 = f32[4,8,128]{2,1,0:T(8,128)S(1)} all-to-all(f32[4,8,128]{2,1,0:T(8,128)S(1)} %columns.4), channel_id=1, replica_groups=mesh['x'=4,'z'=16,'y'=4,'core'=2] {'x'}, dimensions={0} | all-to-all | bytes 32768 | tf_op jit(solution)/shard_map/all_to_all | solution.py:29
  134.1 15.4 %all_to_all.76.parts_ref = f32[16,8,128]{2,1,0:T(8,128)S(1)} all-to-all(f32[16,8,128]{2,1,0:T(8,128)S(1)} %broadcast_in_dim.13), channel_id=1, replica_groups=mesh['x'=4,'z'=16,'y'=4,'core'=2] {'z'}, dimensions={0} | all-to-all | bytes 131072 | tf_op jit(solution)/shard_map/all_to_all | solution.py:29
  149.5 2.2 copy-done.2
  151.7 1.2 rows.4
  152.9 8.0 %all_to_all.77.parts_ref = f32[8,16,128]{2,1,0:T(8,128)S(1)} all-to-all(f32[8,16,128]{2,1,0:T(8,128)S(1)} %rows.4), channel_id=1, replica_groups=mesh['x'=4,'z'=16,'y'=4,'core'=2] {'y','core'}, dimensions={0} | all-to-all | bytes 131072 | tf_op jit(solution)/shard_map/all_to_all | solution.py:29
  161.5 7.8 %all_to_all.78 = f32[4,8,128]{2,1,0:T(8,128)S(1)} all-to-all(f32[4,8,128]{2,1,0:T(8,128)S(1)} %columns.5), channel_id=1, replica_groups=mesh['x'=4,'z'=16,'y'=4,'core'=2] {'x'}, dimensions={0} | all-to-all | bytes 32768 | tf_op jit(solution)/shard_map/all_to_all | solution.py:29
  169.4 15.5 %all_to_all.79.parts_ref = f32[16,8,128]{2,1,0:T(8,128)S(1)} all-to-all(f32[16,8,128]{2,1,0:T(8,128)S(1)} %broadcast_in_dim.14), channel_id=1, replica_groups=mesh['x'=4,'z'=16,'y'=4,'core'=2] {'z'}, dimensions={0} | all-to-all | bytes 131072 | tf_op jit(solution)/shard_map/all_to_all | solution.py:29
  184.9 2.2 copy-done.3
  187.1 1.2 rows.5
  188.3 8.1 %all_to_all.80.parts_ref = f32[8,16,128]{2,1,0:T(8,128)S(1)} all-to-all(f32[8,16,128]{2,1,0:T(8,128)S(1)} %rows.5), channel_id=1, replica_groups=mesh['x'=4,'z'=16,'y'=4,'core'=2] {'y','core'}, dimensions={0} | all-to-all | bytes 131072 | tf_op jit(solution)/shard_map/all_to_all | solution.py:29
  196.5 4.0 %numerator.1 = bf16[1024,896]{1,0:T(8,128)(2,1)S(1)} custom-call(f32[8,16,128]{2,1,0:T(8,128)S(1)} %all_to_all.80.parts_ref, bf16[2048,1024]{1,0:T(8,128)(2,1)S(1)} %copy-done.4, bf16[2048,768]{1,0:T(8,128)(2,1)S(1)} %copy-done.6), custom_call_target="tpu_custom_call" | custom-call | flops 3221225472 | bytes 9240576 | tf_op jit(solution)/shard_map/numerator/pallas_call | solution.py:125
  200.5 26.3 %all_to_all.81 = bf16[4,16,16,896]{3,2,1,0:T(8,128)(2,1)S(1)} all-to-all(bf16[4,16,16,896]{3,2,1,0:T(8,128)(2,1)S(1)} %bitcast.2), channel_id=1, replica_groups=mesh['x'=4,'z'=16,'y'=4,'core'=2] {'x'}, dimensions={0} | all-to-all | bytes 3670016 | tf_op jit(solution)/shard_map/all_to_all | solution.py:29
  227.2 29.0 %all_to_all.82 = bf16[16,16,896]{2,1,0:T(8,128)(2,1)S(1)} all-to-all(bf16[16,16,896]{2,1,0:T(8,128)(2,1)S(1)} %reduce_sum.61), channel_id=1, replica_groups=mesh['x'=4,'z'=16,'y'=4,'core'=2] {'z'}, dimensions={0} | all-to-all | bytes 917504 | tf_op jit(solution)/shard_map/all_to_all | solution.py:29
  (39 shorter events, 4.6 us)
Async XLA Ops:
  1.8 42.7 %copy-start.13 = (s32[8192]{0:T(1024)S(1)}, s32[8192]{0:T(1024)}, u32[]{:S(2)}) copy-start(s32[8192]{0:T(1024)} %param.7) | copy-start | bytes 98308
  1.8 43.0 %copy-start.12 = (s32[2048,16]{0,1:T(8,128)S(1)}, s32[2048,16]{0,1:T(8,128)}, u32[]{:S(2)}) copy-start(s32[2048,16]{0,1:T(8,128)} %param.5) | copy-start | bytes 393220
  40.2 23.5 %all-to-all-start.1 = ((bf16[4,16,16,768]{3,2,1,0:T(8,128)(2,1)}), bf16[4,16,16,768]{3,2,1,0:T(8,128)(2,1)S(1)}, u32[]{:S(2)}, u32[]{:S(2)}) async-start(bf16[4,16,16,768]{3,2,1,0:T(8,128)(2,1)} %broadcast_in_dim.11), calls=%async_computation.1 | async-start | bytes 3145728 | tf_op jit(solution)/shard_map/all_to_all | solution.py:29
  45.2 1.9 copy-start.5
  59.6 1.9 copy-start.7
  61.5 1.7 copy-start.9
  63.8 2.2 copy-start.8
  66.0 1.9 copy-start.10
  83.5 1.9 copy-start
  114.3 2.2 copy-start.1
  149.5 2.2 copy-start.2
  160.9 35.6 %copy-start.6 = (bf16[2048,768]{1,0:T(8,128)(2,1)S(1)}, bf16[2048,768]{1,0:T(8,128)(2,1)}, u32[]{:S(2)}) copy-start(bf16[2048,768]{1,0:T(8,128)(2,1)} %x_ref.3) | copy-start | bytes 9437188
  184.9 2.2 copy-start.3
  187.1 9.4 %copy-start.4 = (bf16[2048,1024]{1,0:T(8,128)(2,1)S(1)}, bf16[2048,1024]{1,0:T(8,128)(2,1)}, u32[]{:S(2)}) copy-start(bf16[2048,1024]{1,0:T(8,128)(2,1)} %copy-done) | copy-start | bytes 12582916
  200.5 56.0 %copy-start.11 = (f32[16,768]{1,0:T(8,128)S(1)}, f32[16,768]{1,0:T(8,128)}, u32[]{:S(2)}) copy-start(f32[16,768]{1,0:T(8,128)} %param.6) | copy-start | bytes 147460

commit v3 on v2

--- a/solution.py
+++ b/solution.py
@@ -29,11 +29,6 @@
     return lax.all_to_all(blocks, axes, 0, 0)
 
 
-def spread(block, axes):
-    copies = jnp.broadcast_to(block[None], (lax.axis_size(axes),) + block.shape)
-    return exchange(copies, axes)
-
-
 def as_row(tiles):
     return jnp.concatenate([tiles[q : q + 1] for q in range(tiles.shape[0])], axis=1)
 
@@ -66,11 +61,36 @@
     match_ref[...] = jnp.dot(picked.astype(bf16), hot_ref[...], preferred_element_type=f32).astype(bf16)
 
 
-def similarity_kernel(unit_ref, cent_ref, match_ref, sim_ref, total_ref):
+def unit_copies_kernel(cent_ref, out_ref):
+    out_ref[...] = jnp.broadcast_to(unit_rows(cent_ref[...]).astype(bf16)[None], out_ref.shape)
+
+
+def copies_kernel(block_ref, out_ref):
+    for i in range(out_ref.shape[0]):
+        out_ref[i] = block_ref[...]
+
+
+def sum_copies_kernel(parts_ref, out_ref):
+    out_ref[...] = jnp.broadcast_to(jnp.sum(parts_ref[...], axis=0)[None], out_ref.shape)
+
+
+def similarity_kernel(unit_any, cent_ref, match_any, sim_ref, total_ref, unit_ref, match_ref, sems):
+    copies = []
+    for b in range(unit_ref.shape[0] // TILE):
+        rows = pl.ds(b * TILE, TILE)
+        pair = (
+            pltpu.make_async_copy(unit_any.at[rows], unit_ref.at[rows], sems.at[0, b]),
+            pltpu.make_async_copy(match_any.at[rows], match_ref.at[rows], sems.at[1, b]),
+        )
+        for copy in pair:
+            copy.start()
+        copies.append(pair)
     ones = jnp.ones((total_ref.shape[0], sim_ref.shape[1]), bf16)
     scale = math.log2(math.e) / entropic_smoothing
-    for b in range(unit_ref.shape[0] // TILE):
+    for b, pair in enumerate(copies):
         rows = pl.ds(b * TILE, TILE)
+        for copy in pair:
+            copy.wait()
         dots = lax.dot_general(
             unit_ref[rows, :], cent_ref[...], (((1,), (1,)), ((), ())), preferred_element_type=f32
         )
@@ -99,7 +119,7 @@
     return jnp.transpose(jnp.broadcast_to(row, (LANES, LANES)))
 
 
-def numerator_kernel(parts_ref, sim_ref, x_ref, out_ref, weight_ref):
+def numerator_kernel(count, parts_ref, sim_ref, x_ref, out_ref, weight_ref):
     factor = 1.0 / jnp.sum(parts_ref[...], axis=0)
     lhs = two_terms(as_row(factor))
     mass = jnp.sum(jnp.dot(lhs, sim_ref[...], preferred_element_type=f32), axis=0, keepdims=True)
@@ -108,25 +128,57 @@
         rows = pl.ds(q * LANES, LANES)
         scale = jnp.concatenate([down(factor[q : q + 1])] * (columns // LANES), axis=1)
         weight_ref[rows, :] = (sim_ref[rows, :].astype(f32) * scale).astype(bf16)
-    width = x_ref.shape[1]
-    for b in range(columns // TILE):
-        rows = pl.ds(b * TILE, TILE)
-        out_ref[rows, :width] = lax.dot_general(
-            weight_ref[:, rows], x_ref[...], (((0,), (0,)), ((), ())), preferred_element_type=f32
+    chunks = x_ref.shape[1] // LANES
+    held = columns // out_ref.shape[0]
+    base = held * chunks
+    for i in range(out_ref.shape[0]):
+        sums = lax.dot_general(
+            weight_ref[:, pl.ds(i * held, held)],
+            x_ref[...],
+            (((0,), (0,)), ((), ())),
+            preferred_element_type=f32,
         ).astype(bf16)
-    for q in range(columns // LANES):
-        out_ref[pl.ds(q * LANES, LANES), width:] = down(mass[:, q * LANES : (q + 1) * LANES]).astype(bf16)
-
-
-def call(kernel, name, operands, outs, mib, flops, scratch=()):
+        for z in range(held // count):
+            for c in range(chunks):
+                out_ref[i, pl.ds((z * chunks + c) * count, count), :] = sums[
+                    z * count : (z + 1) * count, c * LANES : (c + 1) * LANES
+                ]
+        own = as_tiles(mass[:, i * held : (i + 1) * held])
+        rest = jnp.zeros((out_ref.shape[1] - base - own.shape[0], LANES), f32)
+        out_ref[i, pl.ds(base, out_ref.shape[1] - base), :] = jnp.concatenate([own, rest], axis=0).astype(bf16)
+
+
+def hand_on_kernel(count, parts_ref, out_ref):
+    total = jnp.sum(parts_ref[...].astype(f32), axis=0)
+    chunk_rows = out_ref.shape[1] - 16
+    base = chunk_rows * out_ref.shape[0]
+    for z in range(out_ref.shape[0]):
+        out_ref[z, pl.ds(0, chunk_rows), :] = total[z * chunk_rows : (z + 1) * chunk_rows].astype(bf16)
+        at = z * count % LANES
+        row = total[base + z * count // LANES : base + z * count // LANES + 1]
+        row = jnp.concatenate([row[:, at:], row[:, :at]], axis=1) if at else row
+        out_ref[z, pl.ds(chunk_rows, 16), :] = jnp.broadcast_to(row, (16, LANES)).astype(bf16)
+
+
+def update_kernel(parts_ref, cent_ref, out_ref):
+    total = jnp.sum(parts_ref[...].astype(f32), axis=0)
+    count, width = out_ref.shape
+    chunk_rows = width // LANES * count
+    scale = 1.0 / (down(total[chunk_rows : chunk_rows + 1])[:count] + 1.0)
+    for c in range(width // LANES):
+        lanes = pl.ds(c * LANES, LANES)
+        out_ref[:, lanes] = (total[c * count : (c + 1) * count] + cent_ref[:, lanes]) * scale
+
+
+def call(kernel, name, operands, outs, mib, flops, scratch=(), anywhere=()):
     moved = sum(math.prod(o.shape) * o.dtype.itemsize for o in (*operands, *outs))
-    vmem = pl.BlockSpec(memory_space=pltpu.VMEM)
+    vmem, place = pl.BlockSpec(memory_space=pltpu.VMEM), pl.BlockSpec(memory_space=pl.ANY)
     single = len(outs) == 1
     return pl.pallas_call(
         kernel,
         name=name,
         out_shape=outs[0] if single else outs,
-        in_specs=[vmem] * len(operands),
+        in_specs=[place if i in anywhere else vmem for i in range(len(operands))],
         out_specs=vmem if single else [vmem] * len(outs),
         scratch_shapes=scratch,
         compiler_params=pltpu.CompilerParams(vmem_limit_bytes=mib * MIB),
@@ -170,54 +222,77 @@
     cent_size = lax.axis_size(("y", "core"))
     columns = dp_size * local_count
     desired_load = row_count / (local_count * cent_size)
-    unit_c = unit_rows(centroids).astype(bf16)
     layout_table = coarse_of.reshape(dp_size, cent_size, local_count)
     group_ids = lax.dynamic_slice_in_dim(
         layout_table, lax.axis_index(("y", "core")), 1, 1
     ).reshape(1, columns)
     unit_x, matched = prepare(embeddings, coarse_ids, group_ids)
-    along_z = spread(unit_c, "z")
-    group_centroids = spread(along_z, "x").reshape(columns, width)
+
+    array = jax.ShapeDtypeStruct
+    copies = call(
+        unit_copies_kernel, "units", (centroids,), (array((z_size, local_count, width), bf16),), 4, 0
+    )
+    along_z = exchange(copies, "z")
+    copies = call(copies_kernel, "copies", (along_z,), (array((x_size,) + along_z.shape, bf16),), 4, 0)
+    group_centroids = exchange(copies, "x").reshape(columns, width)
 
     product = 2 * row_count * columns
-    row_parts = jax.ShapeDtypeStruct((cent_size, row_count // LANES, LANES), f32)
-    column_parts = jax.ShapeDtypeStruct((x_size, columns // LANES, LANES), f32)
+    row_parts = array((cent_size, row_count // LANES, LANES), f32)
+    column_parts = array((x_size, columns // LANES, LANES), f32)
+    column_sums = array((z_size, columns // LANES, LANES), f32)
     similarity, parts = call(
         similarity_kernel,
         "similarity",
         (unit_x, group_centroids, matched),
-        (jax.ShapeDtypeStruct((row_count, columns), bf16), row_parts),
-        16,
+        (array((row_count, columns), bf16), row_parts),
+        20,
         product * width,
+        scratch=[
+            pltpu.VMEM((row_count, width), bf16),
+            pltpu.VMEM((row_count, columns), bf16),
+            pltpu.SemaphoreType.DMA((2, row_count // TILE)),
+        ],
+        anywhere=(0, 2),
     )
     parts = exchange(parts, ("y", "core"))
     for sweep in range(SWEEPS):
         parts = call(column_kernel, "columns", (parts, similarity), (column_parts,), 8, product * 16)
-        parts = jnp.sum(exchange(parts, "x"), axis=0)
-        parts = spread(parts, "z")
+        parts = call(sum_copies_kernel, "across", (exchange(parts, "x"),), (column_sums,), 2, 0)
         parts = call(
             functools.partial(row_kernel, desired_load),
             "rows",
-            (parts, similarity),
+            (exchange(parts, "z"), similarity),
             (row_parts,),
             8,
             product * 16,
         )
         parts = exchange(parts, ("y", "core"))
+    chunk_rows = width // LANES * local_count
     sums = call(
-        numerator_kernel,
+        functools.partial(numerator_kernel, local_count),
         "numerator",
         (parts, similarity, embeddings),
-        (jax.ShapeDtypeStruct((columns, width + LANES), bf16),),
+        (array((x_size, z_size * chunk_rows + 16, LANES), bf16),),
         16,
         product * width,
         scratch=[pltpu.VMEM((row_count, columns), bf16)],
     )
-    sums = sums.reshape(x_size, z_size, local_count, width + LANES)
-    sums = jnp.sum(exchange(sums, "x").astype(f32), axis=0)
-    sums = jnp.sum(exchange(sums.astype(bf16), "z").astype(f32), axis=0)
-    numer_own, mass_own = sums[:, :width], sums[:, width]
-    return (numer_own + centroids) / (mass_own + 1.0)[:, None]
+    sums = call(
+        functools.partial(hand_on_kernel, local_count),
+        "hand_on",
+        (exchange(sums, "x"),),
+        (array((z_size, chunk_rows + 16, LANES), bf16),),
+        8,
+        0,
+    )
+    return call(
+        update_kernel,
+        "update",
+        (exchange(sums, "z"), centroids),
+        (array(centroids.shape, f32),),
+        4,
+        0,
+    )
 
 
 def solution(mesh):

time: 258 us -> 249 us (0.965)
  local copies, waits for them, and re-layouts: 20.1 us -> 11 us
  Pallas kernels: 27.1 us -> 33.3 us
  other arithmetic: 3.15 us -> 0 us
  blocking collectives: 202 us -> 199 us
    unnamed x29 -> x21, local copies, waits for them, and re-layouts: 18.4 us -> 10.7 us
    pallas_call x8 -> x15, Pallas kernels: 14.6 us -> 20.8 us  [call(): pl.pallas_call(kernel, name=name, out_shape=outs[0] if single else outs,...]
    all_to_all x13, blocking collectives: 202 us -> 199 us  [exchange(): return lax.all_to_all(blocks, axes, 0, 0)]
where the time goes in v3:
time: 249 us; the launch traced here: 248 us
  blocking collectives  199 us (80%)
  Pallas kernels  33.3 us (13%)
  local copies, waits for them, and re-layouts  11 us (4%)
  starting transfers between devices  4.29 us (2%)
    all_to_all x13, blocking collectives, exchange(): return lax.all_to_all(blocks, axes, 0, 0)  199 us
    pallas_call x15, Pallas kernels, call(): pl.pallas_call(kernel, name=name, out_shape=outs[0] if single else outs,...  20.8 us
    pallas_call x1, Pallas kernels, prepare(): pl.pallas_call(prepare_kernel, name='prepare', grid=(rows // TILE,), in_s...  12.5 us
    unnamed x21, local copies, waits for them, and re-layouts  10.7 us
  transfers between devices with their start and end apart: 1, of which 1 were waited for; matrix products, arithmetic and copies ran while one was open for 0% of the time, Pallas kernels for 5%

profile of v3, /device:TPU:32, one launch (start us, length us, event | category | flops | bytes accessed | tf_op | source)
XLA Modules:
  0.0 248.4 jit_solution(12329484644857599155)
XLA Ops:
  0.0 0.8 copy-done
  0.9 37.0 %all_to_all.70.block_ref = bf16[16,16,768]{2,1,0:T(8,128)(2,1)S(1)} all-to-all(bf16[16,16,768]{2,1,0:T(8,128)(2,1)S(1)} %units.1), channel_id=1, replica_groups=mesh['x'=4,'z'=16,'y'=4,'core'=2] {'z'}, dimensions={0} | all-to-all | bytes 786432 | tf_op jit(solution)/shard_map/all_to_all | solution.py:29
  38.0 1.4 copies.1
  39.3 4.3 %all-to-all-start.1 = ((bf16[4,16,16,768]{3,2,1,0:T(8,128)(2,1)}), bf16[4,16,16,768]{3,2,1,0:T(8,128)(2,1)S(1)}, u32[]{:S(2)}, u32[]{:S(2)}) async-start(bf16[4,16,16,768]{3,2,1,0:T(8,128)(2,1)} %copies.1), calls=%async_computation.1 | async-start | bytes 3145728 | tf_op jit(solution)/shard_map/all_to_all | solution.py:29
  44.3 1.9 copy-done.2
  46.2 12.5 %prepare.1 = (bf16[2048,768]{1,0:T(8,128)(2,1)S(1)}, bf16[2048,1024]{1,0:T(8,128)(2,1)S(1)}) custom-call(bf16[2048,768]{1,0:T(8,128)(2,1)S(1)} %copy-done.2, s32[2048,16]{1,0:T(8,128)S(1)} %copy.6.ids_ref, s32[1,1024]{1,0:T(1,128)S(1)} %reshape.10.group_ref), custom_call_target="tpu_custom_call" | custom-call | flops 8589934592 | bytes 50331648 | tf_op jit(solution)/shard_map/prepare/pallas_call | solution.py:192
  58.7 1.9 copy-done.4
  60.7 1.7 copy-done.6
  62.3 0.5 all-to-all-done.1
  62.9 2.2 copy-done.5
  65.1 1.9 copy-done.7
  66.9 8.7 %similarity.1 = (bf16[2048,1024]{1,0:T(8,128)(2,1)S(1)}, f32[8,16,128]{2,1,0:T(8,128)S(1)}) custom-call(bf16[2048,768]{1,0:T(8,128)(2,1)S(1)} %copy-done.7, bf16[1024,768]{1,0:T(8,128)(2,1)S(1)} %bitcast.1, bf16[2048,1024]{1,0:T(8,128)(2,1)S(1)} %copy-done.5), custom_call_target="tpu_custom_call" | custom-call | flops 3221225472 | bytes 13172736 | tf_op jit(solution)/shard_map/similarity/pallas_call | solution.py:177
  75.6 9.9 %all_to_all.71.parts_ref = f32[8,16,128]{2,1,0:T(8,128)S(1)} all-to-all(f32[8,16,128]{2,1,0:T(8,128)S(1)} %get-tuple-element.11), channel_id=1, replica_groups=mesh['x'=4,'z'=16,'y'=4,'core'=2] {'y','core'}, dimensions={0} | all-to-all | bytes 131072 | tf_op jit(solution)/shard_map/all_to_all | solution.py:29
  85.5 0.7 columns.3
  86.2 9.4 %all_to_all.72.parts_ref = f32[4,8,128]{2,1,0:T(8,128)S(1)} all-to-all(f32[4,8,128]{2,1,0:T(8,128)S(1)} %columns.3), channel_id=1, replica_groups=mesh['x'=4,'z'=16,'y'=4,'core'=2] {'x'}, dimensions={0} | all-to-all | bytes 32768 | tf_op jit(solution)/shard_map/all_to_all | solution.py:29
  95.6 19.5 %all_to_all.73.parts_ref = f32[16,8,128]{2,1,0:T(8,128)S(1)} all-to-all(f32[16,8,128]{2,1,0:T(8,128)S(1)} %across.3), channel_id=1, replica_groups=mesh['x'=4,'z'=16,'y'=4,'core'=2] {'z'}, dimensions={0} | all-to-all | bytes 131072 | tf_op jit(solution)/shard_map/all_to_all | solution.py:29
  115.1 1.2 rows.3
  116.3 8.0 %all_to_all.74.parts_ref = f32[8,16,128]{2,1,0:T(8,128)S(1)} all-to-all(f32[8,16,128]{2,1,0:T(8,128)S(1)} %rows.3), channel_id=1, replica_groups=mesh['x'=4,'z'=16,'y'=4,'core'=2] {'y','core'}, dimensions={0} | all-to-all | bytes 131072 | tf_op jit(solution)/shard_map/all_to_all | solution.py:29
  124.3 0.7 columns.4
  125.0 7.7 %all_to_all.75.parts_ref = f32[4,8,128]{2,1,0:T(8,128)S(1)} all-to-all(f32[4,8,128]{2,1,0:T(8,128)S(1)} %columns.4), channel_id=1, replica_groups=mesh['x'=4,'z'=16,'y'=4,'core'=2] {'x'}, dimensions={0} | all-to-all | bytes 32768 | tf_op jit(solution)/shard_map/all_to_all | solution.py:29
  132.7 15.4 %all_to_all.76.parts_ref = f32[16,8,128]{2,1,0:T(8,128)S(1)} all-to-all(f32[16,8,128]{2,1,0:T(8,128)S(1)} %across.4), channel_id=1, replica_groups=mesh['x'=4,'z'=16,'y'=4,'core'=2] {'z'}, dimensions={0} | all-to-all | bytes 131072 | tf_op jit(solution)/shard_map/all_to_all | solution.py:29
  148.1 1.2 rows.4
  149.3 8.0 %all_to_all.77.parts_ref = f32[8,16,128]{2,1,0:T(8,128)S(1)} all-to-all(f32[8,16,128]{2,1,0:T(8,128)S(1)} %rows.4), channel_id=1, replica_groups=mesh['x'=4,'z'=16,'y'=4,'core'=2] {'y','core'}, dimensions={0} | all-to-all | bytes 131072 | tf_op jit(solution)/shard_map/all_to_all | solution.py:29
  157.3 0.7 columns.5
  158.0 8.0 %all_to_all.78.parts_ref = f32[4,8,128]{2,1,0:T(8,128)S(1)} all-to-all(f32[4,8,128]{2,1,0:T(8,128)S(1)} %columns.5), channel_id=1, replica_groups=mesh['x'=4,'z'=16,'y'=4,'core'=2] {'x'}, dimensions={0} | all-to-all | bytes 32768 | tf_op jit(solution)/shard_map/all_to_all | solution.py:29
  166.0 15.5 %all_to_all.79.parts_ref = f32[16,8,128]{2,1,0:T(8,128)S(1)} all-to-all(f32[16,8,128]{2,1,0:T(8,128)S(1)} %across.5), channel_id=1, replica_groups=mesh['x'=4,'z'=16,'y'=4,'core'=2] {'z'}, dimensions={0} | all-to-all | bytes 131072 | tf_op jit(solution)/shard_map/all_to_all | solution.py:29
  181.5 1.2 rows.5
  182.7 8.0 %all_to_all.80.parts_ref = f32[8,16,128]{2,1,0:T(8,128)S(1)} all-to-all(f32[8,16,128]{2,1,0:T(8,128)S(1)} %rows.5), channel_id=1, replica_groups=mesh['x'=4,'z'=16,'y'=4,'core'=2] {'y','core'}, dimensions={0} | all-to-all | bytes 131072 | tf_op jit(solution)/shard_map/all_to_all | solution.py:29
  190.7 4.0 %numerator.1 = bf16[4,1552,128]{2,1,0:T(8,128)(2,1)S(1)} custom-call(f32[8,16,128]{2,1,0:T(8,128)S(1)} %all_to_all.80.parts_ref, bf16[2048,1024]{1,0:T(8,128)(2,1)S(1)} %get-tuple-element.12.sim_ref, bf16[2048,768]{1,0:T(8,128)(2,1)S(1)} %copy-done.3), custom_call_target="tpu_custom_call" | custom-call | flops 3221225472 | bytes 8994816 | tf_op jit(solution)/shard_map/numerator/pallas_call | solution.py:177
  194.7 23.6 %all_to_all.81.parts_ref = bf16[4,1552,128]{2,1,0:T(8,128)(2,1)S(1)} all-to-all(bf16[4,1552,128]{2,1,0:T(8,128)(2,1)S(1)} %numerator.1), channel_id=1, replica_groups=mesh['x'=4,'z'=16,'y'=4,'core'=2] {'x'}, dimensions={0} | all-to-all | bytes 3178496 | tf_op jit(solution)/shard_map/all_to_all | solution.py:29
  218.6 29.1 %all_to_all.82.parts_ref = bf16[16,112,128]{2,1,0:T(8,128)(2,1)S(1)} all-to-all(bf16[16,112,128]{2,1,0:T(8,128)(2,1)S(1)} %hand_on.1), channel_id=1, replica_groups=mesh['x'=4,'z'=16,'y'=4,'core'=2] {'z'}, dimensions={0} | all-to-all | bytes 917504 | tf_op jit(solution)/shard_map/all_to_all | solution.py:29
  247.7 0.7 update.1
  (23 shorter events, 1.1 us)
Async XLA Ops:
  0.0 0.8 copy-start
  0.8 42.8 %copy-start.9 = (s32[8192]{0:T(1024)S(1)}, s32[8192]{0:T(1024)}, u32[]{:S(2)}) copy-start(s32[8192]{0:T(1024)} %param.7) | copy-start | bytes 98308
  0.9 43.0 %copy-start.8 = (s32[2048,16]{0,1:T(8,128)S(1)}, s32[2048,16]{0,1:T(8,128)}, u32[]{:S(2)}) copy-start(s32[2048,16]{0,1:T(8,128)} %param.5) | copy-start | bytes 393220
  39.3 23.5 %all-to-all-start.1 = ((bf16[4,16,16,768]{3,2,1,0:T(8,128)(2,1)}), bf16[4,16,16,768]{3,2,1,0:T(8,128)(2,1)S(1)}, u32[]{:S(2)}, u32[]{:S(2)}) async-start(bf16[4,16,16,768]{3,2,1,0:T(8,128)(2,1)} %copies.1), calls=%async_computation.1 | async-start | bytes 3145728 | tf_op jit(solution)/shard_map/all_to_all | solution.py:29
  44.3 1.9 copy-start.2
  58.7 2.0 copy-start.4
  60.7 1.7 copy-start.6
  62.9 2.2 copy-start.5
  65.1 1.9 copy-start.7
  158.0 32.7 %copy-start.3 = (bf16[2048,768]{1,0:T(8,128)(2,1)S(1)}, bf16[2048,768]{1,0:T(8,128)(2,1)}, u32[]{:S(2)}) copy-start(bf16[2048,768]{1,0:T(8,128)(2,1)} %x_ref.3) | copy-start | bytes 9437188
  194.7 53.0 %copy-start.1 = (f32[16,768]{1,0:T(8,128)S(1)}, f32[16,768]{1,0:T(8,128)}, u32[]{:S(2)}) copy-start(f32[16,768]{1,0:T(8,128)} %cent_ref.3) | copy-start | bytes 147460

commit v4 on v3

--- a/solution.py
+++ b/solution.py
@@ -46,19 +46,36 @@
     return jnp.where(which == 0, high, rest).astype(bf16)
 
 
-def prepare_kernel(x_ref, ids_ref, group_ref, unit_ref, match_ref, hot_ref):
-    @pl.when(pl.program_id(0) == 0)
-    def _():
-        cluster = lax.broadcasted_iota(jnp.int32, hot_ref.shape, 0)
-        hot_ref[...] = jnp.where(cluster == group_ref[...], 1.0, 0.0).astype(bf16)
-
-    unit_ref[...] = unit_rows(x_ref[...]).astype(bf16)
-    ids = ids_ref[...]
-    cluster = lax.broadcasted_iota(jnp.int32, (ids.shape[0], CLUSTERS), 1)
-    picked = jnp.zeros(cluster.shape, f32)
-    for p in range(ids.shape[1]):
-        picked = jnp.where(ids[:, p : p + 1] == cluster, 1.0, picked)
-    match_ref[...] = jnp.dot(picked.astype(bf16), hot_ref[...], preferred_element_type=f32).astype(bf16)
+def prepare_kernel(x_ref, ids_ref, group_ref, unit_hbm, match_hbm, unit_ref, match_ref, hot_ref, sems):
+    cluster = lax.broadcasted_iota(jnp.int32, hot_ref.shape, 0)
+    hot_ref[...] = jnp.where(cluster == group_ref[...], 1.0, 0.0).astype(bf16)
+
+    def copies(b):
+        rows = pl.ds(b * TILE, TILE)
+        return (
+            pltpu.make_async_copy(unit_ref.at[rows], unit_hbm.at[rows], sems.at[0, b]),
+            pltpu.make_async_copy(match_ref.at[rows], match_hbm.at[rows], sems.at[1, b]),
+        )
+
+    def block(b):
+        rows = pl.ds(b * TILE, TILE)
+        unit_ref[rows, :] = unit_rows(x_ref[rows, :]).astype(bf16)
+        ids = ids_ref[rows, :]
+        cluster = lax.broadcasted_iota(jnp.int32, (TILE, CLUSTERS), 1)
+        picked = jnp.zeros(cluster.shape, f32)
+        for p in range(ids.shape[1]):
+            picked = jnp.where(ids[:, p : p + 1] == cluster, 1.0, picked)
+        matched = jnp.dot(picked.astype(bf16), hot_ref[...], preferred_element_type=f32)
+        match_ref[rows, :] = matched.astype(bf16)
+
+    count = x_ref.shape[0] // TILE
+    for b in range(count):
+        block(b)
+        for copy in copies(b):
+            copy.start()
+    for b in range(count):
+        for copy in copies(b):
+            copy.wait()
 
 
 def unit_copies_kernel(cent_ref, out_ref):
@@ -74,13 +91,13 @@
     out_ref[...] = jnp.broadcast_to(jnp.sum(parts_ref[...], axis=0)[None], out_ref.shape)
 
 
-def similarity_kernel(unit_any, cent_ref, match_any, sim_ref, total_ref, unit_ref, match_ref, sems):
+def similarity_kernel(unit_hbm, cent_ref, match_hbm, sim_ref, total_ref, unit_ref, match_ref, sems):
     copies = []
     for b in range(unit_ref.shape[0] // TILE):
         rows = pl.ds(b * TILE, TILE)
         pair = (
-            pltpu.make_async_copy(unit_any.at[rows], unit_ref.at[rows], sems.at[0, b]),
-            pltpu.make_async_copy(match_any.at[rows], match_ref.at[rows], sems.at[1, b]),
+            pltpu.make_async_copy(unit_hbm.at[rows], unit_ref.at[rows], sems.at[0, b]),
+            pltpu.make_async_copy(match_hbm.at[rows], match_ref.at[rows], sems.at[1, b]),
         )
         for copy in pair:
             copy.start()
@@ -131,18 +148,20 @@
     chunks = x_ref.shape[1] // LANES
     held = columns // out_ref.shape[0]
     base = held * chunks
-    for i in range(out_ref.shape[0]):
+    for t in range(columns // TILE):
         sums = lax.dot_general(
-            weight_ref[:, pl.ds(i * held, held)],
+            weight_ref[:, pl.ds(t * TILE, TILE)],
             x_ref[...],
             (((0,), (0,)), ((), ())),
             preferred_element_type=f32,
         ).astype(bf16)
-        for z in range(held // count):
+        for z in range(TILE // count):
+            slot, place = divmod(t * TILE + z * count, held)
             for c in range(chunks):
-                out_ref[i, pl.ds((z * chunks + c) * count, count), :] = sums[
+                out_ref[slot, pl.ds(place * chunks + c * count, count), :] = sums[
                     z * count : (z + 1) * count, c * LANES : (c + 1) * LANES
                 ]
+    for i in range(out_ref.shape[0]):
         own = as_tiles(mass[:, i * held : (i + 1) * held])
         rest = jnp.zeros((out_ref.shape[1] - base - own.shape[0], LANES), f32)
         out_ref[i, pl.ds(base, out_ref.shape[1] - base), :] = jnp.concatenate([own, rest], axis=0).astype(bf16)
@@ -170,71 +189,68 @@
         out_ref[:, lanes] = (total[c * count : (c + 1) * count] + cent_ref[:, lanes]) * scale
 
 
-def call(kernel, name, operands, outs, mib, flops, scratch=(), anywhere=()):
+def call(kernel, name, operands, outs, mib, flops, scratch=(), hbm_in=(), hbm_out=False):
     moved = sum(math.prod(o.shape) * o.dtype.itemsize for o in (*operands, *outs))
-    vmem, place = pl.BlockSpec(memory_space=pltpu.VMEM), pl.BlockSpec(memory_space=pl.ANY)
+    vmem, hbm = pl.BlockSpec(memory_space=pltpu.VMEM), pl.BlockSpec(memory_space=pltpu.HBM)
+    out = hbm if hbm_out else vmem
     single = len(outs) == 1
+    if hbm_out:
+        outs = [pltpu.HBM(o.shape, o.dtype) for o in outs]
+    operands = [
+        pltpu.with_memory_space_constraint(o, pltpu.HBM) if i in hbm_in else o
+        for i, o in enumerate(operands)
+    ]
     return pl.pallas_call(
         kernel,
         name=name,
         out_shape=outs[0] if single else outs,
-        in_specs=[place if i in anywhere else vmem for i in range(len(operands))],
-        out_specs=vmem if single else [vmem] * len(outs),
+        in_specs=[hbm if i in hbm_in else vmem for i in range(len(operands))],
+        out_specs=out if single else [out] * len(outs),
         scratch_shapes=scratch,
         compiler_params=pltpu.CompilerParams(vmem_limit_bytes=mib * MIB),
         cost_estimate=pl.CostEstimate(flops=flops, bytes_accessed=moved, transcendentals=0),
     )(*operands)
 
 
-def prepare(embeddings, coarse_ids, group_ids):
-    rows, width = embeddings.shape
-    columns = group_ids.shape[1]
-    return pl.pallas_call(
-        prepare_kernel,
-        name="prepare",
-        grid=(rows // TILE,),
-        in_specs=[
-            pl.BlockSpec((TILE, width), lambda i: (i, 0)),
-            pl.BlockSpec((TILE, coarse_ids.shape[1]), lambda i: (i, 0)),
-            pl.BlockSpec((1, columns), lambda i: (0, 0)),
-        ],
-        out_specs=[
-            pl.BlockSpec((TILE, width), lambda i: (i, 0)),
-            pl.BlockSpec((TILE, columns), lambda i: (i, 0)),
-        ],
-        out_shape=[
-            jax.ShapeDtypeStruct((rows, width), bf16),
-            jax.ShapeDtypeStruct((rows, columns), bf16),
-        ],
-        scratch_shapes=[pltpu.VMEM((CLUSTERS, columns), bf16)],
-        compiler_params=pltpu.CompilerParams(vmem_limit_bytes=16 * MIB),
-        cost_estimate=pl.CostEstimate(
-            flops=8 * rows * CLUSTERS * columns, bytes_accessed=32 * rows * width, transcendentals=0
-        ),
-    )(embeddings, coarse_ids, group_ids)
-
-
 def per_device(embeddings, coarse_ids, centroids, coarse_of):
     row_count, width = embeddings.shape
     local_count = centroids.shape[0]
-    x_size, z_size = lax.axis_size("x"), lax.axis_size("z")
-    dp_size = x_size * z_size
+    near, far, along_z = ("x", "zl"), "zh", ("zh", "zl")
+    x_size, near_size, far_size = (lax.axis_size(axes) for axes in ("x", near, far))
+    z_size = lax.axis_size(along_z)
     cent_size = lax.axis_size(("y", "core"))
-    columns = dp_size * local_count
+    columns = x_size * z_size * local_count
     desired_load = row_count / (local_count * cent_size)
-    layout_table = coarse_of.reshape(dp_size, cent_size, local_count)
-    group_ids = lax.dynamic_slice_in_dim(
-        layout_table, lax.axis_index(("y", "core")), 1, 1
-    ).reshape(1, columns)
-    unit_x, matched = prepare(embeddings, coarse_ids, group_ids)
+    layout_table = coarse_of.reshape(x_size, far_size, z_size // far_size, cent_size, local_count)
+    group_ids = lax.dynamic_index_in_dim(
+        layout_table, lax.axis_index(("y", "core")), 3, keepdims=False
+    )
+    group_ids = jnp.swapaxes(group_ids, 1, 2).reshape(1, columns)
 
     array = jax.ShapeDtypeStruct
+    unit_like, match_like = array((row_count, width), bf16), array((row_count, columns), bf16)
+    blocks = row_count // TILE
+    unit_x, matched = call(
+        prepare_kernel,
+        "prepare",
+        (embeddings, coarse_ids, group_ids),
+        (unit_like, match_like),
+        24,
+        8 * row_count * CLUSTERS * columns,
+        scratch=[
+            pltpu.VMEM(unit_like.shape, bf16),
+            pltpu.VMEM(match_like.shape, bf16),
+            pltpu.VMEM((CLUSTERS, columns), bf16),
+            pltpu.SemaphoreType.DMA((2, blocks)),
+        ],
+        hbm_out=True,
+    )
     copies = call(
-        unit_copies_kernel, "units", (centroids,), (array((z_size, local_count, width), bf16),), 4, 0
-    )
-    along_z = exchange(copies, "z")
-    copies = call(copies_kernel, "copies", (along_z,), (array((x_size,) + along_z.shape, bf16),), 4, 0)
-    group_centroids = exchange(copies, "x").reshape(columns, width)
+        unit_copies_kernel, "units", (centroids,), (array((far_size, local_count, width), bf16),), 4, 0
+    )
+    part = exchange(copies, far)
+    copies = call(copies_kernel, "copies", (part,), (array((near_size,) + part.shape, bf16),), 4, 0)
+    group_centroids = exchange(copies, near).reshape(columns, width)
 
     product = 2 * row_count * columns
     row_parts = array((cent_size, row_count // LANES, LANES), f32)
@@ -244,15 +260,15 @@
         similarity_kernel,
         "similarity",
         (unit_x, group_centroids, matched),
-        (array((row_count, columns), bf16), row_parts),
+        (match_like, row_parts),
         20,
         product * width,
         scratch=[
-            pltpu.VMEM((row_count, width), bf16),
-            pltpu.VMEM((row_count, columns), bf16),
-            pltpu.SemaphoreType.DMA((2, row_count // TILE)),
+            pltpu.VMEM(unit_like.shape, bf16),
+            pltpu.VMEM(match_like.shape, bf16),
+            pltpu.SemaphoreType.DMA((2, blocks)),
         ],
-        anywhere=(0, 2),
+        hbm_in=(0, 2),
     )
     parts = exchange(parts, ("y", "core"))
     for sweep in range(SWEEPS):
@@ -261,7 +277,7 @@
         parts = call(
             functools.partial(row_kernel, desired_load),
             "rows",
-            (exchange(parts, "z"), similarity),
+            (exchange(parts, along_z), similarity),
             (row_parts,),
             8,
             product * 16,
@@ -272,7 +288,7 @@
         functools.partial(numerator_kernel, local_count),
         "numerator",
         (parts, similarity, embeddings),
-        (array((x_size, z_size * chunk_rows + 16, LANES), bf16),),
+        (array((near_size, far_size * chunk_rows + 16, LANES), bf16),),
         16,
         product * width,
         scratch=[pltpu.VMEM((row_count, columns), bf16)],
@@ -280,15 +296,15 @@
     sums = call(
         functools.partial(hand_on_kernel, local_count),
         "hand_on",
-        (exchange(sums, "x"),),
-        (array((z_size, chunk_rows + 16, LANES), bf16),),
+        (exchange(sums, near),),
+        (array((far_size, chunk_rows + 16, LANES), bf16),),
         8,
         0,
     )
     return call(
         update_kernel,
         "update",
-        (exchange(sums, "z"), centroids),
+        (exchange(sums, far), centroids),
         (array(centroids.shape, f32),),
         4,
         0,
@@ -296,16 +312,12 @@
 
 
 def solution(mesh):
-    fine = Mesh(mesh.devices.reshape(4, 16, 4, 2), ("x", "z", "y", "core"))
+    fine = Mesh(mesh.devices.reshape(4, 8, 2, 4, 2), ("x", "zh", "zl", "y", "core"))
+    rows, held = P(("x", "zh", "zl"), None), P(("x", "zh", "zl", "y", "core"), None)
     return jax.shard_map(
         per_device,
         mesh=fine,
-        in_specs=(
-            P(("x", "z"), None),
-            P(("x", "z"), None),
-            P(("x", "z", "y", "core"), None),
-            P(),
-        ),
-        out_specs=P(("x", "z", "y", "core"), None),
+        in_specs=(rows, rows, held, P()),
+        out_specs=held,
         check_vma=False,
     )

time: 249 us -> 231 us (0.928)
  the two profiles are of different devices: /device:TPU:32 before, /device:TPU:2 now
where the time goes in v4:
time: 231 us; the launch traced here: 230 us
  blocking collectives  188 us (81%)
  Pallas kernels  34.3 us (15%)
  starting transfers between devices  4.83 us (2%)
  local copies, waits for them, and re-layouts  3.28 us (1%)
    all_to_all x13, blocking collectives, exchange(): return lax.all_to_all(blocks, axes, 0, 0)  188 us
    pallas_call x16, Pallas kernels, call(): pl.pallas_call(kernel, name=name, out_shape=outs[0] if single else outs,...  34.3 us
    all_to_all x1, starting transfers between devices, exchange(): return lax.all_to_all(blocks, axes, 0, 0)  4.83 us
  transfers between devices with their start and end apart: 1, of which 0 were waited for; matrix products, arithmetic and copies ran while one was open for 0% of the time, Pallas kernels for 6%

profile of v4, /device:TPU:2, one launch (start us, length us, event | category | flops | bytes accessed | tf_op | source)
XLA Modules:
  0.0 230.3 jit_solution(18141723185127193643)
XLA Ops:
  0.0 0.8 copy-done
  0.8 0.1 units.1
  0.9 33.6 %all_to_all.70.block_ref = bf16[8,16,768]{2,1,0:T(8,128)(2,1)S(1)} all-to-all(bf16[8,16,768]{2,1,0:T(8,128)(2,1)S(1)} %units.1), channel_id=1, replica_groups=mesh['x'=4,'zh'=8,'zl'=2,'y'=4,'core'=2] {'zh'}, dimensions={0} | all-to-all | bytes 393216 | tf_op jit(solution)/shard_map/all_to_all | solution.py:29
  34.5 1.4 copies.1
  35.8 4.8 %all-to-all-start.1 = ((bf16[8,8,16,768]{3,2,1,0:T(8,128)(2,1)}), bf16[8,8,16,768]{3,2,1,0:T(8,128)(2,1)S(1)}, u32[]{:S(2)}, u32[]{:S(2)}) async-start(bf16[8,8,16,768]{3,2,1,0:T(8,128)(2,1)} %copies.1), calls=%async_computation.1 | async-start | bytes 3145728 | tf_op jit(solution)/shard_map/all_to_all | solution.py:29
  40.7 0.1 reshape.9
  40.8 0.1 reshape.10.group_ref
  40.9 0.3 copy.8.ids_ref
  41.3 1.9 copy-done.2
  43.2 14.1 %prepare.1 = (bf16[2048,768]{1,0:T(8,128)(2,1)}, bf16[2048,1024]{1,0:T(8,128)(2,1)}) custom-call(bf16[2048,768]{1,0:T(8,128)(2,1)S(1)} %copy-done.2, s32[2048,16]{1,0:T(8,128)S(1)} %copy.8.ids_ref, s32[1,1024]{1,0:T(1,128)S(1)} %reshape.10.group_ref), custom_call_target="tpu_custom_call" | custom-call | flops 8589934592 | bytes 10620928 | tf_op jit(solution)/shard_map/prepare/pallas_call | solution.py:203
  57.3 8.0 %similarity.1 = (bf16[2048,1024]{1,0:T(8,128)(2,1)S(1)}, f32[8,16,128]{2,1,0:T(8,128)S(1)}) custom-call(bf16[2048,768]{1,0:T(8,128)(2,1)} %get-tuple-element.9.unit_hbm, bf16[1024,768]{1,0:T(8,128)(2,1)S(1)} %bitcast.8, bf16[2048,1024]{1,0:T(8,128)(2,1)} %get-tuple-element.10.match_hbm), custom_call_target="tpu_custom_call" | custom-call | flops 3221225472 | bytes 13172736 | tf_op jit(solution)/shard_map/similarity/pallas_call | solution.py:203
  65.4 9.9 %all_to_all.71.parts_ref = f32[8,16,128]{2,1,0:T(8,128)S(1)} all-to-all(f32[8,16,128]{2,1,0:T(8,128)S(1)} %get-tuple-element.11), channel_id=1, replica_groups=mesh['x'=4,'zh'=8,'zl'=2,'y'=4,'core'=2] {'y','core'}, dimensions={0} | all-to-all | bytes 131072 | tf_op jit(solution)/shard_map/all_to_all | solution.py:29
  75.3 0.7 columns.3
  75.9 8.5 %all_to_all.72.parts_ref = f32[4,8,128]{2,1,0:T(8,128)S(1)} all-to-all(f32[4,8,128]{2,1,0:T(8,128)S(1)} %columns.3), channel_id=1, replica_groups=mesh['x'=4,'zh'=8,'zl'=2,'y'=4,'core'=2] {'x'}, dimensions={0} | all-to-all | bytes 32768 | tf_op jit(solution)/shard_map/all_to_all | solution.py:29
  84.4 18.7 %all_to_all.73.parts_ref = f32[16,8,128]{2,1,0:T(8,128)S(1)} all-to-all(f32[16,8,128]{2,1,0:T(8,128)S(1)} %across.3), channel_id=1, replica_groups=mesh['x'=4,'zh'=8,'zl'=2,'y'=4,'core'=2] {'zh','zl'}, dimensions={0} | all-to-all | bytes 131072 | tf_op jit(solution)/shard_map/all_to_all | solution.py:29
  103.1 1.2 rows.3
  104.3 8.0 %all_to_all.74.parts_ref = f32[8,16,128]{2,1,0:T(8,128)S(1)} all-to-all(f32[8,16,128]{2,1,0:T(8,128)S(1)} %rows.3), channel_id=1, replica_groups=mesh['x'=4,'zh'=8,'zl'=2,'y'=4,'core'=2] {'y','core'}, dimensions={0} | all-to-all | bytes 131072 | tf_op jit(solution)/shard_map/all_to_all | solution.py:29
  112.3 0.7 columns.4
  113.0 7.7 %all_to_all.75.parts_ref = f32[4,8,128]{2,1,0:T(8,128)S(1)} all-to-all(f32[4,8,128]{2,1,0:T(8,128)S(1)} %columns.4), channel_id=1, replica_groups=mesh['x'=4,'zh'=8,'zl'=2,'y'=4,'core'=2] {'x'}, dimensions={0} | all-to-all | bytes 32768 | tf_op jit(solution)/shard_map/all_to_all | solution.py:29
  120.7 15.5 %all_to_all.76.parts_ref = f32[16,8,128]{2,1,0:T(8,128)S(1)} all-to-all(f32[16,8,128]{2,1,0:T(8,128)S(1)} %across.4), channel_id=1, replica_groups=mesh['x'=4,'zh'=8,'zl'=2,'y'=4,'core'=2] {'zh','zl'}, dimensions={0} | all-to-all | bytes 131072 | tf_op jit(solution)/shard_map/all_to_all | solution.py:29
  136.2 1.2 rows.4
  137.4 8.0 %all_to_all.77.parts_ref = f32[8,16,128]{2,1,0:T(8,128)S(1)} all-to-all(f32[8,16,128]{2,1,0:T(8,128)S(1)} %rows.4), channel_id=1, replica_groups=mesh['x'=4,'zh'=8,'zl'=2,'y'=4,'core'=2] {'y','core'}, dimensions={0} | all-to-all | bytes 131072 | tf_op jit(solution)/shard_map/all_to_all | solution.py:29
  145.4 0.7 columns.5
  146.1 8.0 %all_to_all.78.parts_ref = f32[4,8,128]{2,1,0:T(8,128)S(1)} all-to-all(f32[4,8,128]{2,1,0:T(8,128)S(1)} %columns.5), channel_id=1, replica_groups=mesh['x'=4,'zh'=8,'zl'=2,'y'=4,'core'=2] {'x'}, dimensions={0} | all-to-all | bytes 32768 | tf_op jit(solution)/shard_map/all_to_all | solution.py:29
  154.1 15.5 %all_to_all.79.parts_ref = f32[16,8,128]{2,1,0:T(8,128)S(1)} all-to-all(f32[16,8,128]{2,1,0:T(8,128)S(1)} %across.5), channel_id=1, replica_groups=mesh['x'=4,'zh'=8,'zl'=2,'y'=4,'core'=2] {'zh','zl'}, dimensions={0} | all-to-all | bytes 131072 | tf_op jit(solution)/shard_map/all_to_all | solution.py:29
  169.6 1.2 rows.5
  170.8 8.0 %all_to_all.80.parts_ref = f32[8,16,128]{2,1,0:T(8,128)S(1)} all-to-all(f32[8,16,128]{2,1,0:T(8,128)S(1)} %rows.5), channel_id=1, replica_groups=mesh['x'=4,'zh'=8,'zl'=2,'y'=4,'core'=2] {'y','core'}, dimensions={0} | all-to-all | bytes 131072 | tf_op jit(solution)/shard_map/all_to_all | solution.py:29
  178.8 4.0 %numerator.1 = bf16[8,784,128]{2,1,0:T(8,128)(2,1)S(1)} custom-call(f32[8,16,128]{2,1,0:T(8,128)S(1)} %all_to_all.80.parts_ref, bf16[2048,1024]{1,0:T(8,128)(2,1)S(1)} %get-tuple-element.12.sim_ref, bf16[2048,768]{1,0:T(8,128)(2,1)S(1)} %copy-done.3), custom_call_target="tpu_custom_call" | custom-call | flops 3221225472 | bytes 9011200 | tf_op jit(solution)/shard_map/numerator/pallas_call | solution.py:203
  182.8 24.8 %all_to_all.81.parts_ref = bf16[8,784,128]{2,1,0:T(8,128)(2,1)S(1)} all-to-all(bf16[8,784,128]{2,1,0:T(8,128)(2,1)S(1)} %numerator.1), channel_id=1, replica_groups=mesh['x'=4,'zh'=8,'zl'=2,'y'=4,'core'=2] {'x','zl'}, dimensions={0} | all-to-all | bytes 3211264 | tf_op jit(solution)/shard_map/all_to_all | solution.py:29
  207.6 0.3 hand_on.1
  207.9 21.7 %all_to_all.82.parts_ref = bf16[8,112,128]{2,1,0:T(8,128)(2,1)S(1)} all-to-all(bf16[8,112,128]{2,1,0:T(8,128)(2,1)S(1)} %hand_on.1), channel_id=1, replica_groups=mesh['x'=4,'zh'=8,'zl'=2,'y'=4,'core'=2] {'zh'}, dimensions={0} | all-to-all | bytes 458752 | tf_op jit(solution)/shard_map/all_to_all | solution.py:29
  229.6 0.7 update.1
  (16 shorter events, 0.1 us)
Async XLA Ops:
  0.0 0.8 copy-start
  0.8 39.9 %copy-start.5 = (s32[8192]{0:T(1024)S(1)}, s32[8192]{0:T(1024)}, u32[]{:S(2)}) copy-start(s32[8192]{0:T(1024)} %param.7) | copy-start | bytes 98308
  0.8 40.1 %copy-start.4 = (s32[2048,16]{0,1:T(8,128)S(1)}, s32[2048,16]{0,1:T(8,128)}, u32[]{:S(2)}) copy-start(s32[2048,16]{0,1:T(8,128)} %param.5) | copy-start | bytes 393220
  35.8 21.5 %all-to-all-start.1 = ((bf16[8,8,16,768]{3,2,1,0:T(8,128)(2,1)}), bf16[8,8,16,768]{3,2,1,0:T(8,128)(2,1)S(1)}, u32[]{:S(2)}, u32[]{:S(2)}) async-start(bf16[8,8,16,768]{3,2,1,0:T(8,128)(2,1)} %copies.1), calls=%async_computation.1 | async-start | bytes 3145728 | tf_op jit(solution)/shard_map/all_to_all | solution.py:29
  41.3 1.9 copy-start.2
  146.1 32.7 %copy-start.3 = (bf16[2048,768]{1,0:T(8,128)(2,1)S(1)}, bf16[2048,768]{1,0:T(8,128)(2,1)}, u32[]{:S(2)}) copy-start(bf16[2048,768]{1,0:T(8,128)(2,1)} %x_ref.3) | copy-start | bytes 9437188
  182.8 46.8 %copy-start.1 = (f32[16,768]{1,0:T(8,128)S(1)}, f32[16,768]{1,0:T(8,128)}, u32[]{:S(2)}) copy-start(f32[16,768]{1,0:T(8,128)} %cent_ref.3) | copy-start | bytes 147460

commit v5 on v4

--- a/solution.py
+++ b/solution.py
@@ -46,35 +46,55 @@
     return jnp.where(which == 0, high, rest).astype(bf16)
 
 
-def prepare_kernel(x_ref, ids_ref, group_ref, unit_hbm, match_hbm, unit_ref, match_ref, hot_ref, sems):
+def in_turn(blocks, copies, work, ahead=2):
+    for b in range(min(ahead, blocks)):
+        for copy in copies(b):
+            copy.start()
+    for b in range(blocks):
+        if b + ahead < blocks:
+            for copy in copies(b + ahead):
+                copy.start()
+        for copy in copies(b):
+            copy.wait()
+        work(b)
+
+
+def prepare_kernel(x_hbm, ids_ref, group_ref, unit_hbm, match_hbm, x_ref, unit_ref, match_ref, hot_ref, sems):
+    blocks = x_ref.shape[0] // TILE
+    half = CLUSTERS // 2
     cluster = lax.broadcasted_iota(jnp.int32, hot_ref.shape, 0)
     hot_ref[...] = jnp.where(cluster == group_ref[...], 1.0, 0.0).astype(bf16)
-
-    def copies(b):
+    lane = lax.broadcasted_iota(jnp.int32, (TILE, half), 1).astype(f32).astype(bf16)
+
+    def into(b):
+        rows = pl.ds(b * TILE, TILE)
+        return (pltpu.make_async_copy(x_hbm.at[rows], x_ref.at[rows], sems.at[0, b]),)
+
+    def out_of(b):
         rows = pl.ds(b * TILE, TILE)
         return (
-            pltpu.make_async_copy(unit_ref.at[rows], unit_hbm.at[rows], sems.at[0, b]),
-            pltpu.make_async_copy(match_ref.at[rows], match_hbm.at[rows], sems.at[1, b]),
+            pltpu.make_async_copy(unit_ref.at[rows], unit_hbm.at[rows], sems.at[1, b]),
+            pltpu.make_async_copy(match_ref.at[rows], match_hbm.at[rows], sems.at[2, b]),
         )
 
-    def block(b):
+    def work(b):
         rows = pl.ds(b * TILE, TILE)
         unit_ref[rows, :] = unit_rows(x_ref[rows, :]).astype(bf16)
         ids = ids_ref[rows, :]
-        cluster = lax.broadcasted_iota(jnp.int32, (TILE, CLUSTERS), 1)
-        picked = jnp.zeros(cluster.shape, f32)
-        for p in range(ids.shape[1]):
-            picked = jnp.where(ids[:, p : p + 1] == cluster, 1.0, picked)
-        matched = jnp.dot(picked.astype(bf16), hot_ref[...], preferred_element_type=f32)
+        matched = jnp.zeros((TILE, match_ref.shape[1]), f32)
+        for first in (0, half):
+            near = (ids - first).astype(f32).astype(bf16)
+            picked = jnp.zeros(lane.shape, bf16)
+            for p in range(ids.shape[1]):
+                picked = jnp.where(near[:, p : p + 1] == lane, jnp.ones_like(picked), picked)
+            matched += jnp.dot(picked, hot_ref[first : first + half, :], preferred_element_type=f32)
         match_ref[rows, :] = matched.astype(bf16)
-
-    count = x_ref.shape[0] // TILE
-    for b in range(count):
-        block(b)
-        for copy in copies(b):
+        for copy in out_of(b):
             copy.start()
-    for b in range(count):
-        for copy in copies(b):
+
+    in_turn(blocks, into, work)
+    for b in range(blocks):
+        for copy in out_of(b):
             copy.wait()
 
 
@@ -92,22 +112,18 @@
 
 
 def similarity_kernel(unit_hbm, cent_ref, match_hbm, sim_ref, total_ref, unit_ref, match_ref, sems):
-    copies = []
-    for b in range(unit_ref.shape[0] // TILE):
-        rows = pl.ds(b * TILE, TILE)
-        pair = (
+    ones = jnp.ones((total_ref.shape[0], sim_ref.shape[1]), bf16)
+    scale = math.log2(math.e) / entropic_smoothing
+
+    def into(b):
+        rows = pl.ds(b * TILE, TILE)
+        return (
             pltpu.make_async_copy(unit_hbm.at[rows], unit_ref.at[rows], sems.at[0, b]),
             pltpu.make_async_copy(match_hbm.at[rows], match_ref.at[rows], sems.at[1, b]),
         )
-        for copy in pair:
-            copy.start()
-        copies.append(pair)
-    ones = jnp.ones((total_ref.shape[0], sim_ref.shape[1]), bf16)
-    scale = math.log2(math.e) / entropic_smoothing
-    for b, pair in enumerate(copies):
-        rows = pl.ds(b * TILE, TILE)
-        for copy in pair:
-            copy.wait()
+
+    def work(b):
+        rows = pl.ds(b * TILE, TILE)
         dots = lax.dot_general(
             unit_ref[rows, :], cent_ref[...], (((1,), (1,)), ((), ())), preferred_element_type=f32
         )
@@ -116,6 +132,8 @@
         totals = lax.dot_general(ones, sim, (((1,), (1,)), ((), ())), preferred_element_type=f32)
         for q in range(TILE // LANES):
             total_ref[:, b * (TILE // LANES) + q, :] = totals[:, q * LANES : (q + 1) * LANES]
+
+    in_turn(unit_ref.shape[0] // TILE, into, work)
 
 
 def column_kernel(parts_ref, sim_ref, out_ref):
@@ -239,10 +257,12 @@
         8 * row_count * CLUSTERS * columns,
         scratch=[
             pltpu.VMEM(unit_like.shape, bf16),
+            pltpu.VMEM(unit_like.shape, bf16),
             pltpu.VMEM(match_like.shape, bf16),
             pltpu.VMEM((CLUSTERS, columns), bf16),
-            pltpu.SemaphoreType.DMA((2, blocks)),
+            pltpu.SemaphoreType.DMA((3, blocks)),
         ],
+        hbm_in=(0,),
         hbm_out=True,
     )
     copies = call(

time: 231 us -> 231 us (level)
  waiting for transfers between devices: 0.01 us -> 3.25 us
    all_to_all x1, waiting for transfers between devices: 0.01 us -> 3.25 us  [exchange(): return lax.all_to_all(blocks, axes, 0, 0)]
  transfers between devices with their start and end apart: 1 -> 1, of which waited for: 0 -> 1; matrix products, arithmetic and copies ran while one was open for 0% -> 0% of each run, Pallas kernels for 6% -> 5%
where the time goes in v5:
time: 231 us; the launch traced here: 230 us
  blocking collectives  188 us (81%)
  Pallas kernels  32.4 us (14%)
  starting transfers between devices  4.83 us (2%)
  waiting for transfers between devices  3.25 us (1%)
    all_to_all x13, blocking collectives, exchange(): return lax.all_to_all(blocks, axes, 0, 0)  188 us
    pallas_call x16, Pallas kernels, call(): pl.pallas_call(kernel, name=name, out_shape=outs[0] if single else outs,...  32.4 us
    all_to_all x1, starting transfers between devices, exchange(): return lax.all_to_all(blocks, axes, 0, 0)  4.83 us
  transfers between devices with their start and end apart: 1, of which 1 were waited for; matrix products, arithmetic and copies ran while one was open for 0% of the time, Pallas kernels for 5%

profile of v5, /device:TPU:2, one launch (start us, length us, event | category | flops | bytes accessed | tf_op | source)
XLA Modules:
  0.0 230.5 jit_solution(10051087308379934731)
XLA Ops:
  0.0 0.8 copy-done
  0.8 0.1 units.1
  0.9 33.6 %all_to_all.70.block_ref = bf16[8,16,768]{2,1,0:T(8,128)(2,1)S(1)} all-to-all(bf16[8,16,768]{2,1,0:T(8,128)(2,1)S(1)} %units.1), channel_id=1, replica_groups=mesh['x'=4,'zh'=8,'zl'=2,'y'=4,'core'=2] {'zh'}, dimensions={0} | all-to-all | bytes 393216 | tf_op jit(solution)/shard_map/all_to_all | solution.py:29
  34.5 1.3 copies.1
  35.8 4.8 %all-to-all-start.1 = ((bf16[8,8,16,768]{3,2,1,0:T(8,128)(2,1)}), bf16[8,8,16,768]{3,2,1,0:T(8,128)(2,1)S(1)}, u32[]{:S(2)}, u32[]{:S(2)}) async-start(bf16[8,8,16,768]{3,2,1,0:T(8,128)(2,1)} %copies.1), calls=%async_computation.1 | async-start | bytes 3145728 | tf_op jit(solution)/shard_map/all_to_all | solution.py:29
  40.6 0.1 reshape.9
  40.8 0.1 reshape.10.group_ref
  40.9 0.3 copy.8.ids_ref
  41.2 12.1 %prepare.1 = (bf16[2048,768]{1,0:T(8,128)(2,1)}, bf16[2048,1024]{1,0:T(8,128)(2,1)}) custom-call(bf16[2048,768]{1,0:T(8,128)(2,1)} %x_ref.1, s32[2048,16]{1,0:T(8,128)S(1)} %copy.8.ids_ref, s32[1,1024]{1,0:T(1,128)S(1)} %reshape.10.group_ref), custom_call_target="tpu_custom_call" | custom-call | flops 8589934592 | bytes 10620928 | tf_op jit(solution)/shard_map/prepare/pallas_call | solution.py:221
  53.3 3.3 %all-to-all-done.1 = bf16[8,8,16,768]{3,2,1,0:T(8,128)(2,1)S(1)} async-done(((bf16[8,8,16,768]{3,2,1,0:T(8,128)(2,1)}), bf16[8,8,16,768]{3,2,1,0:T(8,128)(2,1)S(1)}, u32[]{:S(2)}, u32[]{:S(2)}) %all-to-all-start.1) | async-done | bytes 1572896 | tf_op jit(solution)/shard_map/all_to_all | solution.py:29
  56.6 8.2 %similarity.1 = (bf16[2048,1024]{1,0:T(8,128)(2,1)S(1)}, f32[8,16,128]{2,1,0:T(8,128)S(1)}) custom-call(bf16[2048,768]{1,0:T(8,128)(2,1)} %get-tuple-element.9.unit_hbm, bf16[1024,768]{1,0:T(8,128)(2,1)S(1)} %bitcast.8, bf16[2048,1024]{1,0:T(8,128)(2,1)} %get-tuple-element.10.match_hbm), custom_call_target="tpu_custom_call" | custom-call | flops 3221225472 | bytes 13172736 | tf_op jit(solution)/shard_map/similarity/pallas_call | solution.py:221
  64.8 9.9 %all_to_all.71.parts_ref = f32[8,16,128]{2,1,0:T(8,128)S(1)} all-to-all(f32[8,16,128]{2,1,0:T(8,128)S(1)} %get-tuple-element.11), channel_id=1, replica_groups=mesh['x'=4,'zh'=8,'zl'=2,'y'=4,'core'=2] {'y','core'}, dimensions={0} | all-to-all | bytes 131072 | tf_op jit(solution)/shard_map/all_to_all | solution.py:29
  74.7 0.7 columns.3
  75.4 8.2 %all_to_all.72.parts_ref = f32[4,8,128]{2,1,0:T(8,128)S(1)} all-to-all(f32[4,8,128]{2,1,0:T(8,128)S(1)} %columns.3), channel_id=1, replica_groups=mesh['x'=4,'zh'=8,'zl'=2,'y'=4,'core'=2] {'x'}, dimensions={0} | all-to-all | bytes 32768 | tf_op jit(solution)/shard_map/all_to_all | solution.py:29
  83.6 19.7 %all_to_all.73.parts_ref = f32[16,8,128]{2,1,0:T(8,128)S(1)} all-to-all(f32[16,8,128]{2,1,0:T(8,128)S(1)} %across.3), channel_id=1, replica_groups=mesh['x'=4,'zh'=8,'zl'=2,'y'=4,'core'=2] {'zh','zl'}, dimensions={0} | all-to-all | bytes 131072 | tf_op jit(solution)/shard_map/all_to_all | solution.py:29
  103.3 1.2 rows.3
  104.5 8.0 %all_to_all.74.parts_ref = f32[8,16,128]{2,1,0:T(8,128)S(1)} all-to-all(f32[8,16,128]{2,1,0:T(8,128)S(1)} %rows.3), channel_id=1, replica_groups=mesh['x'=4,'zh'=8,'zl'=2,'y'=4,'core'=2] {'y','core'}, dimensions={0} | all-to-all | bytes 131072 | tf_op jit(solution)/shard_map/all_to_all | solution.py:29
  112.5 0.7 columns.4
  113.1 7.7 %all_to_all.75.parts_ref = f32[4,8,128]{2,1,0:T(8,128)S(1)} all-to-all(f32[4,8,128]{2,1,0:T(8,128)S(1)} %columns.4), channel_id=1, replica_groups=mesh['x'=4,'zh'=8,'zl'=2,'y'=4,'core'=2] {'x'}, dimensions={0} | all-to-all | bytes 32768 | tf_op jit(solution)/shard_map/all_to_all | solution.py:29
  120.9 15.5 %all_to_all.76.parts_ref = f32[16,8,128]{2,1,0:T(8,128)S(1)} all-to-all(f32[16,8,128]{2,1,0:T(8,128)S(1)} %across.4), channel_id=1, replica_groups=mesh['x'=4,'zh'=8,'zl'=2,'y'=4,'core'=2] {'zh','zl'}, dimensions={0} | all-to-all | bytes 131072 | tf_op jit(solution)/shard_map/all_to_all | solution.py:29
  136.4 1.2 rows.4
  137.6 8.0 %all_to_all.77.parts_ref = f32[8,16,128]{2,1,0:T(8,128)S(1)} all-to-all(f32[8,16,128]{2,1,0:T(8,128)S(1)} %rows.4), channel_id=1, replica_groups=mesh['x'=4,'zh'=8,'zl'=2,'y'=4,'core'=2] {'y','core'}, dimensions={0} | all-to-all | bytes 131072 | tf_op jit(solution)/shard_map/all_to_all | solution.py:29
  145.6 0.7 columns.5
  146.3 8.0 %all_to_all.78.parts_ref = f32[4,8,128]{2,1,0:T(8,128)S(1)} all-to-all(f32[4,8,128]{2,1,0:T(8,128)S(1)} %columns.5), channel_id=1, replica_groups=mesh['x'=4,'zh'=8,'zl'=2,'y'=4,'core'=2] {'x'}, dimensions={0} | all-to-all | bytes 32768 | tf_op jit(solution)/shard_map/all_to_all | solution.py:29
  154.2 15.5 %all_to_all.79.parts_ref = f32[16,8,128]{2,1,0:T(8,128)S(1)} all-to-all(f32[16,8,128]{2,1,0:T(8,128)S(1)} %across.5), channel_id=1, replica_groups=mesh['x'=4,'zh'=8,'zl'=2,'y'=4,'core'=2] {'zh','zl'}, dimensions={0} | all-to-all | bytes 131072 | tf_op jit(solution)/shard_map/all_to_all | solution.py:29
  169.8 1.2 rows.5
  171.0 8.0 %all_to_all.80.parts_ref = f32[8,16,128]{2,1,0:T(8,128)S(1)} all-to-all(f32[8,16,128]{2,1,0:T(8,128)S(1)} %rows.5), channel_id=1, replica_groups=mesh['x'=4,'zh'=8,'zl'=2,'y'=4,'core'=2] {'y','core'}, dimensions={0} | all-to-all | bytes 131072 | tf_op jit(solution)/shard_map/all_to_all | solution.py:29
  179.0 4.0 %numerator.1 = bf16[8,784,128]{2,1,0:T(8,128)(2,1)S(1)} custom-call(f32[8,16,128]{2,1,0:T(8,128)S(1)} %all_to_all.80.parts_ref, bf16[2048,1024]{1,0:T(8,128)(2,1)S(1)} %get-tuple-element.12.sim_ref, bf16[2048,768]{1,0:T(8,128)(2,1)S(1)} %copy-done.2), custom_call_target="tpu_custom_call" | custom-call | flops 3221225472 | bytes 9011200 | tf_op jit(solution)/shard_map/numerator/pallas_call | solution.py:221
  183.0 24.8 %all_to_all.81.parts_ref = bf16[8,784,128]{2,1,0:T(8,128)(2,1)S(1)} all-to-all(bf16[8,784,128]{2,1,0:T(8,128)(2,1)S(1)} %numerator.1), channel_id=1, replica_groups=mesh['x'=4,'zh'=8,'zl'=2,'y'=4,'core'=2] {'x','zl'}, dimensions={0} | all-to-all | bytes 3211264 | tf_op jit(solution)/shard_map/all_to_all | solution.py:29
  207.8 0.3 hand_on.1
  208.1 21.7 %all_to_all.82.parts_ref = bf16[8,112,128]{2,1,0:T(8,128)(2,1)S(1)} all-to-all(bf16[8,112,128]{2,1,0:T(8,128)(2,1)S(1)} %hand_on.1), channel_id=1, replica_groups=mesh['x'=4,'zh'=8,'zl'=2,'y'=4,'core'=2] {'zh'}, dimensions={0} | all-to-all | bytes 458752 | tf_op jit(solution)/shard_map/all_to_all | solution.py:29
  229.8 0.7 update.1
  (14 shorter events, 0.1 us)
Async XLA Ops:
  0.0 0.8 copy-start
  0.8 39.8 %copy-start.4 = (s32[8192]{0:T(1024)S(1)}, s32[8192]{0:T(1024)}, u32[]{:S(2)}) copy-start(s32[8192]{0:T(1024)} %param.7) | copy-start | bytes 98308
  0.8 40.1 %copy-start.3 = (s32[2048,16]{0,1:T(8,128)S(1)}, s32[2048,16]{0,1:T(8,128)}, u32[]{:S(2)}) copy-start(s32[2048,16]{0,1:T(8,128)} %param.5) | copy-start | bytes 393220
  35.8 20.8 %all-to-all-start.1 = ((bf16[8,8,16,768]{3,2,1,0:T(8,128)(2,1)}), bf16[8,8,16,768]{3,2,1,0:T(8,128)(2,1)S(1)}, u32[]{:S(2)}, u32[]{:S(2)}) async-start(bf16[8,8,16,768]{3,2,1,0:T(8,128)(2,1)} %copies.1), calls=%async_computation.1 | async-start | bytes 3145728 | tf_op jit(solution)/shard_map/all_to_all | solution.py:29
  146.2 32.7 %copy-start.2 = (bf16[2048,768]{1,0:T(8,128)(2,1)S(1)}, bf16[2048,768]{1,0:T(8,128)(2,1)}, u32[]{:S(2)}) copy-start(bf16[2048,768]{1,0:T(8,128)(2,1)} %x_ref.1) | copy-start | bytes 9437188
  183.0 46.8 %copy-start.1 = (f32[16,768]{1,0:T(8,128)S(1)}, f32[16,768]{1,0:T(8,128)}, u32[]{:S(2)}) copy-start(f32[16,768]{1,0:T(8,128)} %cent_ref.3) | copy-start | bytes 147460

commit v6 on v5

--- a/solution.py
+++ b/solution.py
@@ -102,7 +102,7 @@
     out_ref[...] = jnp.broadcast_to(unit_rows(cent_ref[...]).astype(bf16)[None], out_ref.shape)
 
 
-def copies_kernel(block_ref, out_ref):
+def copies_kernel(block_ref, unused, out_ref):
     for i in range(out_ref.shape[0]):
         out_ref[i] = block_ref[...]
 
@@ -111,18 +111,10 @@
     out_ref[...] = jnp.broadcast_to(jnp.sum(parts_ref[...], axis=0)[None], out_ref.shape)
 
 
-def similarity_kernel(unit_hbm, cent_ref, match_hbm, sim_ref, total_ref, unit_ref, match_ref, sems):
+def similarity_kernel(unit_ref, cent_ref, match_ref, sim_ref, total_ref):
     ones = jnp.ones((total_ref.shape[0], sim_ref.shape[1]), bf16)
     scale = math.log2(math.e) / entropic_smoothing
-
-    def into(b):
-        rows = pl.ds(b * TILE, TILE)
-        return (
-            pltpu.make_async_copy(unit_hbm.at[rows], unit_ref.at[rows], sems.at[0, b]),
-            pltpu.make_async_copy(match_hbm.at[rows], match_ref.at[rows], sems.at[1, b]),
-        )
-
-    def work(b):
+    for b in range(unit_ref.shape[0] // TILE):
         rows = pl.ds(b * TILE, TILE)
         dots = lax.dot_general(
             unit_ref[rows, :], cent_ref[...], (((1,), (1,)), ((), ())), preferred_element_type=f32
@@ -132,8 +124,6 @@
         totals = lax.dot_general(ones, sim, (((1,), (1,)), ((), ())), preferred_element_type=f32)
         for q in range(TILE // LANES):
             total_ref[:, b * (TILE // LANES) + q, :] = totals[:, q * LANES : (q + 1) * LANES]
-
-    in_turn(unit_ref.shape[0] // TILE, into, work)
 
 
 def column_kernel(parts_ref, sim_ref, out_ref):
@@ -269,7 +259,15 @@
         unit_copies_kernel, "units", (centroids,), (array((far_size, local_count, width), bf16),), 4, 0
     )
     part = exchange(copies, far)
-    copies = call(copies_kernel, "copies", (part,), (array((near_size,) + part.shape, bf16),), 4, 0)
+    copies = call(
+        copies_kernel,
+        "copies",
+        (part, matched),
+        (array((near_size,) + part.shape, bf16),),
+        4,
+        0,
+        hbm_in=(1,),
+    )
     group_centroids = exchange(copies, near).reshape(columns, width)
 
     product = 2 * row_count * columns
@@ -281,14 +279,8 @@
         "similarity",
         (unit_x, group_centroids, matched),
         (match_like, row_parts),
-        20,
+        16,
         product * width,
-        scratch=[
-            pltpu.VMEM(unit_like.shape, bf16),
-            pltpu.VMEM(match_like.shape, bf16),
-            pltpu.SemaphoreType.DMA((2, blocks)),
-        ],
-        hbm_in=(0, 2),
     )
     parts = exchange(parts, ("y", "core"))
     for sweep in range(SWEEPS):

time: 231 us -> 232 us (level)
  starting transfers between devices: 4.83 us -> 15.1 us
  blocking collectives: 188 us -> 180 us
  Pallas kernels: 32.4 us -> 28.6 us
    all_to_all x1, starting transfers between devices: 4.83 us -> 15.1 us  [exchange(): return lax.all_to_all(blocks, axes, 0, 0)]
    all_to_all x13, blocking collectives: 188 us -> 180 us  [exchange(): return lax.all_to_all(blocks, axes, 0, 0)]
    pallas_call x16, Pallas kernels: 32.4 us -> 28.6 us  [call(): pl.pallas_call(kernel, name=name, out_shape=outs[0] if single else outs,...]
  transfers between devices with their start and end apart: 1 -> 1, of which waited for: 1 -> 1; matrix products, arithmetic and copies ran while one was open for 0% -> 1% of each run, Pallas kernels for 5% -> 5%
where the time goes in v6:
time: 232 us; the launch traced here: 231 us
  blocking collectives  180 us (78%)
  Pallas kernels  28.6 us (12%)
  starting transfers between devices  15.1 us (7%)
  waiting for transfers between devices  4.3 us (2%)
  local copies, waits for them, and re-layouts  3.05 us (1%)
    all_to_all x13, blocking collectives, exchange(): return lax.all_to_all(blocks, axes, 0, 0)  180 us
    pallas_call x16, Pallas kernels, call(): pl.pallas_call(kernel, name=name, out_shape=outs[0] if single else outs,...  28.6 us
    all_to_all x1, starting transfers between devices, exchange(): return lax.all_to_all(blocks, axes, 0, 0)  15.1 us
  transfers between devices with their start and end apart: 1, of which 1 were waited for; matrix products, arithmetic and copies ran while one was open for 1% of the time, Pallas kernels for 5%

profile of v6, /device:TPU:2, one launch (start us, length us, event | category | flops | bytes accessed | tf_op | source)
XLA Modules:
  0.0 231.1 jit_solution(15255895282723345387)
XLA Ops:
  0.0 0.8 copy-done.1
  0.8 0.8 units.1
  1.6 15.1 %all-to-all-start = ((bf16[8,16,768]{2,1,0:T(8,128)(2,1)}), bf16[8,16,768]{2,1,0:T(8,128)(2,1)S(1)}, u32[]{:S(2)}, u32[]{:S(2)}) async-start(bf16[8,16,768]{2,1,0:T(8,128)(2,1)} %units.1), calls=%async_computation | async-start | bytes 393216 | tf_op jit(solution)/shard_map/all_to_all | solution.py:29
  16.7 0.9 reshape.9
  17.6 0.1 reshape.10.group_ref
  17.7 1.2 copy.8.ids_ref
  18.9 12.1 %prepare.1 = (bf16[2048,768]{1,0:T(8,128)(2,1)}, bf16[2048,1024]{1,0:T(8,128)(2,1)}) custom-call(bf16[2048,768]{1,0:T(8,128)(2,1)} %x_ref.1, s32[2048,16]{1,0:T(8,128)S(1)} %copy.8.ids_ref, s32[1,1024]{1,0:T(1,128)S(1)} %reshape.10.group_ref), custom_call_target="tpu_custom_call" | custom-call | flops 8589934592 | bytes 10620928 | tf_op jit(solution)/shard_map/prepare/pallas_call | solution.py:211
  31.0 4.3 %all-to-all-done.block_ref = bf16[8,16,768]{2,1,0:T(8,128)(2,1)S(1)} async-done(((bf16[8,16,768]{2,1,0:T(8,128)(2,1)}), bf16[8,16,768]{2,1,0:T(8,128)(2,1)S(1)}, u32[]{:S(2)}, u32[]{:S(2)}) %all-to-all-start) | async-done | bytes 196640 | tf_op jit(solution)/shard_map/all_to_all | solution.py:29
  35.3 0.1 copies.1
  35.5 20.8 %all_to_all.70 = bf16[8,8,16,768]{3,2,1,0:T(8,128)(2,1)S(1)} all-to-all(bf16[8,8,16,768]{3,2,1,0:T(8,128)(2,1)S(1)} %copies.1), channel_id=1, replica_groups=mesh['x'=4,'zh'=8,'zl'=2,'y'=4,'core'=2] {'x','zl'}, dimensions={0} | all-to-all | bytes 3145728 | tf_op jit(solution)/shard_map/all_to_all | solution.py:29
  56.2 5.0 %similarity.1 = (bf16[2048,1024]{1,0:T(8,128)(2,1)S(1)}, f32[8,16,128]{2,1,0:T(8,128)S(1)}) custom-call(bf16[2048,768]{1,0:T(8,128)(2,1)S(1)} %copy-done.4, bf16[1024,768]{1,0:T(8,128)(2,1)S(1)} %bitcast.8, bf16[2048,1024]{1,0:T(8,128)(2,1)S(1)} %copy-done), custom_call_target="tpu_custom_call" | custom-call | flops 3221225472 | bytes 13172736 | tf_op jit(solution)/shard_map/similarity/pallas_call | solution.py:211
  61.3 9.9 %all_to_all.71.parts_ref = f32[8,16,128]{2,1,0:T(8,128)S(1)} all-to-all(f32[8,16,128]{2,1,0:T(8,128)S(1)} %get-tuple-element.11), channel_id=1, replica_groups=mesh['x'=4,'zh'=8,'zl'=2,'y'=4,'core'=2] {'y','core'}, dimensions={0} | all-to-all | bytes 131072 | tf_op jit(solution)/shard_map/all_to_all | solution.py:29
  71.1 0.7 columns.3
  71.8 8.0 %all_to_all.72.parts_ref = f32[4,8,128]{2,1,0:T(8,128)S(1)} all-to-all(f32[4,8,128]{2,1,0:T(8,128)S(1)} %columns.3), channel_id=1, replica_groups=mesh['x'=4,'zh'=8,'zl'=2,'y'=4,'core'=2] {'x'}, dimensions={0} | all-to-all | bytes 32768 | tf_op jit(solution)/shard_map/all_to_all | solution.py:29
  79.9 24.0 %all_to_all.73.parts_ref = f32[16,8,128]{2,1,0:T(8,128)S(1)} all-to-all(f32[16,8,128]{2,1,0:T(8,128)S(1)} %across.3), channel_id=1, replica_groups=mesh['x'=4,'zh'=8,'zl'=2,'y'=4,'core'=2] {'zh','zl'}, dimensions={0} | all-to-all | bytes 131072 | tf_op jit(solution)/shard_map/all_to_all | solution.py:29
  103.9 1.2 rows.3
  105.1 8.0 %all_to_all.74.parts_ref = f32[8,16,128]{2,1,0:T(8,128)S(1)} all-to-all(f32[8,16,128]{2,1,0:T(8,128)S(1)} %rows.3), channel_id=1, replica_groups=mesh['x'=4,'zh'=8,'zl'=2,'y'=4,'core'=2] {'y','core'}, dimensions={0} | all-to-all | bytes 131072 | tf_op jit(solution)/shard_map/all_to_all | solution.py:29
  113.1 0.7 columns.4
  113.7 7.7 %all_to_all.75.parts_ref = f32[4,8,128]{2,1,0:T(8,128)S(1)} all-to-all(f32[4,8,128]{2,1,0:T(8,128)S(1)} %columns.4), channel_id=1, replica_groups=mesh['x'=4,'zh'=8,'zl'=2,'y'=4,'core'=2] {'x'}, dimensions={0} | all-to-all | bytes 32768 | tf_op jit(solution)/shard_map/all_to_all | solution.py:29
  121.5 15.5 %all_to_all.76.parts_ref = f32[16,8,128]{2,1,0:T(8,128)S(1)} all-to-all(f32[16,8,128]{2,1,0:T(8,128)S(1)} %across.4), channel_id=1, replica_groups=mesh['x'=4,'zh'=8,'zl'=2,'y'=4,'core'=2] {'zh','zl'}, dimensions={0} | all-to-all | bytes 131072 | tf_op jit(solution)/shard_map/all_to_all | solution.py:29
  137.0 1.2 rows.4
  138.2 8.0 %all_to_all.77.parts_ref = f32[8,16,128]{2,1,0:T(8,128)S(1)} all-to-all(f32[8,16,128]{2,1,0:T(8,128)S(1)} %rows.4), channel_id=1, replica_groups=mesh['x'=4,'zh'=8,'zl'=2,'y'=4,'core'=2] {'y','core'}, dimensions={0} | all-to-all | bytes 131072 | tf_op jit(solution)/shard_map/all_to_all | solution.py:29
  146.2 0.7 columns.5
  146.9 8.0 %all_to_all.78.parts_ref = f32[4,8,128]{2,1,0:T(8,128)S(1)} all-to-all(f32[4,8,128]{2,1,0:T(8,128)S(1)} %columns.5), channel_id=1, replica_groups=mesh['x'=4,'zh'=8,'zl'=2,'y'=4,'core'=2] {'x'}, dimensions={0} | all-to-all | bytes 32768 | tf_op jit(solution)/shard_map/all_to_all | solution.py:29
  154.9 15.5 %all_to_all.79.parts_ref = f32[16,8,128]{2,1,0:T(8,128)S(1)} all-to-all(f32[16,8,128]{2,1,0:T(8,128)S(1)} %across.5), channel_id=1, replica_groups=mesh['x'=4,'zh'=8,'zl'=2,'y'=4,'core'=2] {'zh','zl'}, dimensions={0} | all-to-all | bytes 131072 | tf_op jit(solution)/shard_map/all_to_all | solution.py:29
  170.4 1.2 rows.5
  171.6 8.0 %all_to_all.80.parts_ref = f32[8,16,128]{2,1,0:T(8,128)S(1)} all-to-all(f32[8,16,128]{2,1,0:T(8,128)S(1)} %rows.5), channel_id=1, replica_groups=mesh['x'=4,'zh'=8,'zl'=2,'y'=4,'core'=2] {'y','core'}, dimensions={0} | all-to-all | bytes 131072 | tf_op jit(solution)/shard_map/all_to_all | solution.py:29
  179.6 4.0 %numerator.1 = bf16[8,784,128]{2,1,0:T(8,128)(2,1)S(1)} custom-call(f32[8,16,128]{2,1,0:T(8,128)S(1)} %all_to_all.80.parts_ref, bf16[2048,1024]{1,0:T(8,128)(2,1)S(1)} %get-tuple-element.12.sim_ref, bf16[2048,768]{1,0:T(8,128)(2,1)S(1)} %copy-done.3), custom_call_target="tpu_custom_call" | custom-call | flops 3221225472 | bytes 9011200 | tf_op jit(solution)/shard_map/numerator/pallas_call | solution.py:211
  183.6 24.8 %all_to_all.81.parts_ref = bf16[8,784,128]{2,1,0:T(8,128)(2,1)S(1)} all-to-all(bf16[8,784,128]{2,1,0:T(8,128)(2,1)S(1)} %numerator.1), channel_id=1, replica_groups=mesh['x'=4,'zh'=8,'zl'=2,'y'=4,'core'=2] {'x','zl'}, dimensions={0} | all-to-all | bytes 3211264 | tf_op jit(solution)/shard_map/all_to_all | solution.py:29
  208.4 0.3 hand_on.1
  208.7 21.7 %all_to_all.82.parts_ref = bf16[8,112,128]{2,1,0:T(8,128)(2,1)S(1)} all-to-all(bf16[8,112,128]{2,1,0:T(8,128)(2,1)S(1)} %hand_on.1), channel_id=1, replica_groups=mesh['x'=4,'zh'=8,'zl'=2,'y'=4,'core'=2] {'zh'}, dimensions={0} | all-to-all | bytes 458752 | tf_op jit(solution)/shard_map/all_to_all | solution.py:29
  230.4 0.7 update.1
  (14 shorter events, 0.1 us)
Async XLA Ops:
  0.0 0.8 copy-start.1
  1.6 33.8 %all-to-all-start = ((bf16[8,16,768]{2,1,0:T(8,128)(2,1)}), bf16[8,16,768]{2,1,0:T(8,128)(2,1)S(1)}, u32[]{:S(2)}, u32[]{:S(2)}) async-start(bf16[8,16,768]{2,1,0:T(8,128)(2,1)} %units.1), calls=%async_computation | async-start | bytes 393216 | tf_op jit(solution)/shard_map/all_to_all | solution.py:29
  35.3 20.9 %copy-start = (bf16[2048,1024]{1,0:T(8,128)(2,1)S(1)}, bf16[2048,1024]{1,0:T(8,128)(2,1)}, u32[]{:S(2)}) copy-start(bf16[2048,1024]{1,0:T(8,128)(2,1)} %get-tuple-element.10.unused.match_ref) | copy-start | bytes 12582916
  35.3 20.9 %copy-start.4 = (bf16[2048,768]{1,0:T(8,128)(2,1)S(1)}, bf16[2048,768]{1,0:T(8,128)(2,1)}, u32[]{:S(2)}) copy-start(bf16[2048,768]{1,0:T(8,128)(2,1)} %get-tuple-element.9.unit_ref) | copy-start | bytes 9437188
  146.9 32.7 %copy-start.3 = (bf16[2048,768]{1,0:T(8,128)(2,1)S(1)}, bf16[2048,768]{1,0:T(8,128)(2,1)}, u32[]{:S(2)}) copy-start(bf16[2048,768]{1,0:T(8,128)(2,1)} %x_ref.1) | copy-start | bytes 9437188
  183.6 46.8 %copy-start.2 = (f32[16,768]{1,0:T(8,128)S(1)}, f32[16,768]{1,0:T(8,128)}, u32[]{:S(2)}) copy-start(f32[16,768]{1,0:T(8,128)} %cent_ref.3) | copy-start | bytes 147460

commit v7 on v5

--- a/solution.py
+++ b/solution.py
@@ -102,7 +102,7 @@
     out_ref[...] = jnp.broadcast_to(unit_rows(cent_ref[...]).astype(bf16)[None], out_ref.shape)
 
 
-def copies_kernel(block_ref, out_ref):
+def copies_kernel(block_ref, unused, out_ref):
     for i in range(out_ref.shape[0]):
         out_ref[i] = block_ref[...]
 
@@ -114,26 +114,30 @@
 def similarity_kernel(unit_hbm, cent_ref, match_hbm, sim_ref, total_ref, unit_ref, match_ref, sems):
     ones = jnp.ones((total_ref.shape[0], sim_ref.shape[1]), bf16)
     scale = math.log2(math.e) / entropic_smoothing
+    total_rows = unit_ref.shape[0]
+    starts = [0, TILE] + list(range(2 * TILE, total_rows, 2 * TILE))
+    spans = [pl.ds(i, j - i) for i, j in zip(starts, starts[1:] + [total_rows])]
 
     def into(b):
-        rows = pl.ds(b * TILE, TILE)
+        rows = spans[b]
         return (
             pltpu.make_async_copy(unit_hbm.at[rows], unit_ref.at[rows], sems.at[0, b]),
             pltpu.make_async_copy(match_hbm.at[rows], match_ref.at[rows], sems.at[1, b]),
         )
 
     def work(b):
-        rows = pl.ds(b * TILE, TILE)
-        dots = lax.dot_general(
-            unit_ref[rows, :], cent_ref[...], (((1,), (1,)), ((), ())), preferred_element_type=f32
-        )
-        sim = (jnp.exp2(dots * scale) * match_ref[rows, :].astype(f32)).astype(bf16)
-        sim_ref[rows, :] = sim
-        totals = lax.dot_general(ones, sim, (((1,), (1,)), ((), ())), preferred_element_type=f32)
-        for q in range(TILE // LANES):
-            total_ref[:, b * (TILE // LANES) + q, :] = totals[:, q * LANES : (q + 1) * LANES]
-
-    in_turn(unit_ref.shape[0] // TILE, into, work)
+        for first in range(starts[b], starts[b] + spans[b].size, TILE):
+            rows = pl.ds(first, TILE)
+            dots = lax.dot_general(
+                unit_ref[rows, :], cent_ref[...], (((1,), (1,)), ((), ())), preferred_element_type=f32
+            )
+            sim = (jnp.exp2(dots * scale) * match_ref[rows, :].astype(f32)).astype(bf16)
+            sim_ref[rows, :] = sim
+            totals = lax.dot_general(ones, sim, (((1,), (1,)), ((), ())), preferred_element_type=f32)
+            for q in range(TILE // LANES):
+                total_ref[:, first // LANES + q, :] = totals[:, q * LANES : (q + 1) * LANES]
+
+    in_turn(len(spans), into, work, ahead=3)
 
 
 def column_kernel(parts_ref, sim_ref, out_ref):
@@ -269,7 +273,15 @@
         unit_copies_kernel, "units", (centroids,), (array((far_size, local_count, width), bf16),), 4, 0
     )
     part = exchange(copies, far)
-    copies = call(copies_kernel, "copies", (part,), (array((near_size,) + part.shape, bf16),), 4, 0)
+    copies = call(
+        copies_kernel,
+        "copies",
+        (part, matched),
+        (array((near_size,) + part.shape, bf16),),
+        4,
+        0,
+        hbm_in=(1,),
+    )
     group_centroids = exchange(copies, near).reshape(columns, width)
 
     product = 2 * row_count * columns

time: 231 us -> 234 us (1.013)
  starting transfers between devices: 4.83 us -> 15.1 us
  blocking collectives: 188 us -> 180 us
    all_to_all x1, starting transfers between devices: 4.83 us -> 15.1 us  [exchange(): return lax.all_to_all(blocks, axes, 0, 0)]
    all_to_all x13, blocking collectives: 188 us -> 180 us  [exchange(): return lax.all_to_all(blocks, axes, 0, 0)]
  transfers between devices with their start and end apart: 1 -> 1, of which waited for: 1 -> 1; matrix products, arithmetic and copies ran while one was open for 0% -> 1% of each run, Pallas kernels for 5% -> 5%
where the time goes in v7:
time: 234 us; the launch traced here: 233 us
  blocking collectives  180 us (77%)
  Pallas kernels  31 us (13%)
  starting transfers between devices  15.1 us (6%)
  waiting for transfers between devices  4.3 us (2%)
  local copies, waits for them, and re-layouts  3.04 us (1%)
    all_to_all x13, blocking collectives, exchange(): return lax.all_to_all(blocks, axes, 0, 0)  180 us
    pallas_call x16, Pallas kernels, call(): pl.pallas_call(kernel, name=name, out_shape=outs[0] if single else outs,...  31 us
    all_to_all x1, starting transfers between devices, exchange(): return lax.all_to_all(blocks, axes, 0, 0)  15.1 us
  transfers between devices with their start and end apart: 1, of which 1 were waited for; matrix products, arithmetic and copies ran while one was open for 1% of the time, Pallas kernels for 5%

profile of v7, /device:TPU:2, one launch (start us, length us, event | category | flops | bytes accessed | tf_op | source)
XLA Modules:
  0.0 233.2 jit_solution(16036861779938636137)
XLA Ops:
  0.0 0.8 copy-done
  0.8 0.8 units.1
  1.6 15.1 %all-to-all-start = ((bf16[8,16,768]{2,1,0:T(8,128)(2,1)}), bf16[8,16,768]{2,1,0:T(8,128)(2,1)S(1)}, u32[]{:S(2)}, u32[]{:S(2)}) async-start(bf16[8,16,768]{2,1,0:T(8,128)(2,1)} %units.1), calls=%async_computation | async-start | bytes 393216 | tf_op jit(solution)/shard_map/all_to_all | solution.py:29
  16.7 0.9 reshape.9
  17.6 0.1 reshape.10.group_ref
  17.7 1.2 copy.8.ids_ref
  18.9 12.1 %prepare.1 = (bf16[2048,768]{1,0:T(8,128)(2,1)}, bf16[2048,1024]{1,0:T(8,128)(2,1)}) custom-call(bf16[2048,768]{1,0:T(8,128)(2,1)} %x_ref.1, s32[2048,16]{1,0:T(8,128)S(1)} %copy.8.ids_ref, s32[1,1024]{1,0:T(1,128)S(1)} %reshape.10.group_ref), custom_call_target="tpu_custom_call" | custom-call | flops 8589934592 | bytes 10620928 | tf_op jit(solution)/shard_map/prepare/pallas_call | solution.py:225
  31.0 4.3 %all-to-all-done.block_ref = bf16[8,16,768]{2,1,0:T(8,128)(2,1)S(1)} async-done(((bf16[8,16,768]{2,1,0:T(8,128)(2,1)}), bf16[8,16,768]{2,1,0:T(8,128)(2,1)S(1)}, u32[]{:S(2)}, u32[]{:S(2)}) %all-to-all-start) | async-done | bytes 196640 | tf_op jit(solution)/shard_map/all_to_all | solution.py:29
  35.3 0.1 copies.1
  35.4 20.5 %all_to_all.70 = bf16[8,8,16,768]{3,2,1,0:T(8,128)(2,1)S(1)} all-to-all(bf16[8,8,16,768]{3,2,1,0:T(8,128)(2,1)S(1)} %copies.1), channel_id=1, replica_groups=mesh['x'=4,'zh'=8,'zl'=2,'y'=4,'core'=2] {'x','zl'}, dimensions={0} | all-to-all | bytes 3145728 | tf_op jit(solution)/shard_map/all_to_all | solution.py:29
  55.9 7.4 %similarity.1 = (bf16[2048,1024]{1,0:T(8,128)(2,1)S(1)}, f32[8,16,128]{2,1,0:T(8,128)S(1)}) custom-call(bf16[2048,768]{1,0:T(8,128)(2,1)} %get-tuple-element.9.unit_hbm, bf16[1024,768]{1,0:T(8,128)(2,1)S(1)} %bitcast.8, bf16[2048,1024]{1,0:T(8,128)(2,1)} %get-tuple-element.10.unused.match_hbm), custom_call_target="tpu_custom_call" | custom-call | flops 3221225472 | bytes 13172736 | tf_op jit(solution)/shard_map/similarity/pallas_call | solution.py:225
  63.3 9.9 %all_to_all.71.parts_ref = f32[8,16,128]{2,1,0:T(8,128)S(1)} all-to-all(f32[8,16,128]{2,1,0:T(8,128)S(1)} %get-tuple-element.11), channel_id=1, replica_groups=mesh['x'=4,'zh'=8,'zl'=2,'y'=4,'core'=2] {'y','core'}, dimensions={0} | all-to-all | bytes 131072 | tf_op jit(solution)/shard_map/all_to_all | solution.py:29
  73.2 0.7 columns.3
  73.9 8.0 %all_to_all.72.parts_ref = f32[4,8,128]{2,1,0:T(8,128)S(1)} all-to-all(f32[4,8,128]{2,1,0:T(8,128)S(1)} %columns.3), channel_id=1, replica_groups=mesh['x'=4,'zh'=8,'zl'=2,'y'=4,'core'=2] {'x'}, dimensions={0} | all-to-all | bytes 32768 | tf_op jit(solution)/shard_map/all_to_all | solution.py:29
  81.9 24.0 %all_to_all.73.parts_ref = f32[16,8,128]{2,1,0:T(8,128)S(1)} all-to-all(f32[16,8,128]{2,1,0:T(8,128)S(1)} %across.3), channel_id=1, replica_groups=mesh['x'=4,'zh'=8,'zl'=2,'y'=4,'core'=2] {'zh','zl'}, dimensions={0} | all-to-all | bytes 131072 | tf_op jit(solution)/shard_map/all_to_all | solution.py:29
  105.9 1.2 rows.3
  107.1 8.0 %all_to_all.74.parts_ref = f32[8,16,128]{2,1,0:T(8,128)S(1)} all-to-all(f32[8,16,128]{2,1,0:T(8,128)S(1)} %rows.3), channel_id=1, replica_groups=mesh['x'=4,'zh'=8,'zl'=2,'y'=4,'core'=2] {'y','core'}, dimensions={0} | all-to-all | bytes 131072 | tf_op jit(solution)/shard_map/all_to_all | solution.py:29
  115.1 0.7 columns.4
  115.8 7.7 %all_to_all.75.parts_ref = f32[4,8,128]{2,1,0:T(8,128)S(1)} all-to-all(f32[4,8,128]{2,1,0:T(8,128)S(1)} %columns.4), channel_id=1, replica_groups=mesh['x'=4,'zh'=8,'zl'=2,'y'=4,'core'=2] {'x'}, dimensions={0} | all-to-all | bytes 32768 | tf_op jit(solution)/shard_map/all_to_all | solution.py:29
  123.5 15.5 %all_to_all.76.parts_ref = f32[16,8,128]{2,1,0:T(8,128)S(1)} all-to-all(f32[16,8,128]{2,1,0:T(8,128)S(1)} %across.4), channel_id=1, replica_groups=mesh['x'=4,'zh'=8,'zl'=2,'y'=4,'core'=2] {'zh','zl'}, dimensions={0} | all-to-all | bytes 131072 | tf_op jit(solution)/shard_map/all_to_all | solution.py:29
  139.1 1.2 rows.4
  140.3 8.0 %all_to_all.77.parts_ref = f32[8,16,128]{2,1,0:T(8,128)S(1)} all-to-all(f32[8,16,128]{2,1,0:T(8,128)S(1)} %rows.4), channel_id=1, replica_groups=mesh['x'=4,'zh'=8,'zl'=2,'y'=4,'core'=2] {'y','core'}, dimensions={0} | all-to-all | bytes 131072 | tf_op jit(solution)/shard_map/all_to_all | solution.py:29
  148.3 0.7 columns.5
  149.0 8.0 %all_to_all.78.parts_ref = f32[4,8,128]{2,1,0:T(8,128)S(1)} all-to-all(f32[4,8,128]{2,1,0:T(8,128)S(1)} %columns.5), channel_id=1, replica_groups=mesh['x'=4,'zh'=8,'zl'=2,'y'=4,'core'=2] {'x'}, dimensions={0} | all-to-all | bytes 32768 | tf_op jit(solution)/shard_map/all_to_all | solution.py:29
  156.9 15.5 %all_to_all.79.parts_ref = f32[16,8,128]{2,1,0:T(8,128)S(1)} all-to-all(f32[16,8,128]{2,1,0:T(8,128)S(1)} %across.5), channel_id=1, replica_groups=mesh['x'=4,'zh'=8,'zl'=2,'y'=4,'core'=2] {'zh','zl'}, dimensions={0} | all-to-all | bytes 131072 | tf_op jit(solution)/shard_map/all_to_all | solution.py:29
  172.5 1.2 rows.5
  173.7 8.0 %all_to_all.80.parts_ref = f32[8,16,128]{2,1,0:T(8,128)S(1)} all-to-all(f32[8,16,128]{2,1,0:T(8,128)S(1)} %rows.5), channel_id=1, replica_groups=mesh['x'=4,'zh'=8,'zl'=2,'y'=4,'core'=2] {'y','core'}, dimensions={0} | all-to-all | bytes 131072 | tf_op jit(solution)/shard_map/all_to_all | solution.py:29
  181.7 4.0 %numerator.1 = bf16[8,784,128]{2,1,0:T(8,128)(2,1)S(1)} custom-call(f32[8,16,128]{2,1,0:T(8,128)S(1)} %all_to_all.80.parts_ref, bf16[2048,1024]{1,0:T(8,128)(2,1)S(1)} %get-tuple-element.12.sim_ref, bf16[2048,768]{1,0:T(8,128)(2,1)S(1)} %copy-done.2), custom_call_target="tpu_custom_call" | custom-call | flops 3221225472 | bytes 9011200 | tf_op jit(solution)/shard_map/numerator/pallas_call | solution.py:225
  185.7 24.8 %all_to_all.81.parts_ref = bf16[8,784,128]{2,1,0:T(8,128)(2,1)S(1)} all-to-all(bf16[8,784,128]{2,1,0:T(8,128)(2,1)S(1)} %numerator.1), channel_id=1, replica_groups=mesh['x'=4,'zh'=8,'zl'=2,'y'=4,'core'=2] {'x','zl'}, dimensions={0} | all-to-all | bytes 3211264 | tf_op jit(solution)/shard_map/all_to_all | solution.py:29
  210.5 0.3 hand_on.1
  210.8 21.7 %all_to_all.82.parts_ref = bf16[8,112,128]{2,1,0:T(8,128)(2,1)S(1)} all-to-all(bf16[8,112,128]{2,1,0:T(8,128)(2,1)S(1)} %hand_on.1), channel_id=1, replica_groups=mesh['x'=4,'zh'=8,'zl'=2,'y'=4,'core'=2] {'zh'}, dimensions={0} | all-to-all | bytes 458752 | tf_op jit(solution)/shard_map/all_to_all | solution.py:29
  232.5 0.7 update.1
  (10 shorter events, 0.1 us)
Async XLA Ops:
  0.0 0.8 copy-start
  1.6 33.8 %all-to-all-start = ((bf16[8,16,768]{2,1,0:T(8,128)(2,1)}), bf16[8,16,768]{2,1,0:T(8,128)(2,1)S(1)}, u32[]{:S(2)}, u32[]{:S(2)}) async-start(bf16[8,16,768]{2,1,0:T(8,128)(2,1)} %units.1), calls=%async_computation | async-start | bytes 393216 | tf_op jit(solution)/shard_map/all_to_all | solution.py:29
  148.9 32.7 %copy-start.2 = (bf16[2048,768]{1,0:T(8,128)(2,1)S(1)}, bf16[2048,768]{1,0:T(8,128)(2,1)}, u32[]{:S(2)}) copy-start(bf16[2048,768]{1,0:T(8,128)(2,1)} %x_ref.1) | copy-start | bytes 9437188
  185.7 46.8 %copy-start.1 = (f32[16,768]{1,0:T(8,128)S(1)}, f32[16,768]{1,0:T(8,128)}, u32[]{:S(2)}) copy-start(f32[16,768]{1,0:T(8,128)} %cent_ref.3) | copy-start | bytes 147460

commit v8 on v7

--- a/solution.py
+++ b/solution.py
@@ -102,7 +102,7 @@
     out_ref[...] = jnp.broadcast_to(unit_rows(cent_ref[...]).astype(bf16)[None], out_ref.shape)
 
 
-def copies_kernel(block_ref, unused, out_ref):
+def copies_kernel(block_ref, out_ref):
     for i in range(out_ref.shape[0]):
         out_ref[i] = block_ref[...]
 
@@ -191,14 +191,14 @@
 
 def hand_on_kernel(count, parts_ref, out_ref):
     total = jnp.sum(parts_ref[...].astype(f32), axis=0)
-    chunk_rows = out_ref.shape[1] - 16
+    chunk_rows = out_ref.shape[1] - 8
     base = chunk_rows * out_ref.shape[0]
     for z in range(out_ref.shape[0]):
         out_ref[z, pl.ds(0, chunk_rows), :] = total[z * chunk_rows : (z + 1) * chunk_rows].astype(bf16)
         at = z * count % LANES
         row = total[base + z * count // LANES : base + z * count // LANES + 1]
         row = jnp.concatenate([row[:, at:], row[:, :at]], axis=1) if at else row
-        out_ref[z, pl.ds(chunk_rows, 16), :] = jnp.broadcast_to(row, (16, LANES)).astype(bf16)
+        out_ref[z, pl.ds(chunk_rows, 8), :] = jnp.broadcast_to(row, (8, LANES)).astype(bf16)
 
 
 def update_kernel(parts_ref, cent_ref, out_ref):
@@ -273,15 +273,7 @@
         unit_copies_kernel, "units", (centroids,), (array((far_size, local_count, width), bf16),), 4, 0
     )
     part = exchange(copies, far)
-    copies = call(
-        copies_kernel,
-        "copies",
-        (part, matched),
-        (array((near_size,) + part.shape, bf16),),
-        4,
-        0,
-        hbm_in=(1,),
-    )
+    copies = call(copies_kernel, "copies", (part,), (array((near_size,) + part.shape, bf16),), 4, 0)
     group_centroids = exchange(copies, near).reshape(columns, width)
 
     product = 2 * row_count * columns
@@ -329,7 +321,7 @@
         functools.partial(hand_on_kernel, local_count),
         "hand_on",
         (exchange(sums, near),),
-        (array((far_size, chunk_rows + 16, LANES), bf16),),
+        (array((far_size, chunk_rows + 8, LANES), bf16),),
         8,
         0,
     )

time: 234 us -> 230 us (0.983)
  starting transfers between devices: 15.1 us -> 4.83 us
  blocking collectives: 180 us -> 188 us
    all_to_all x1, starting transfers between devices: 15.1 us -> 4.83 us  [exchange(): return lax.all_to_all(blocks, axes, 0, 0)]
    all_to_all x13, blocking collectives: 180 us -> 188 us  [exchange(): return lax.all_to_all(blocks, axes, 0, 0)]
  transfers between devices with their start and end apart: 1 -> 1, of which waited for: 1 -> 1; matrix products, arithmetic and copies ran while one was open for 1% -> 0% of each run, Pallas kernels for 5% -> 5%
where the time goes in v8:
time: 230 us; the launch traced here: 229 us
  blocking collectives  188 us (82%)
  Pallas kernels  31.7 us (14%)
  starting transfers between devices  4.83 us (2%)
  waiting for transfers between devices  3.25 us (1%)
    all_to_all x13, blocking collectives, exchange(): return lax.all_to_all(blocks, axes, 0, 0)  188 us
    pallas_call x16, Pallas kernels, call(): pl.pallas_call(kernel, name=name, out_shape=outs[0] if single else outs,...  31.7 us
    all_to_all x1, starting transfers between devices, exchange(): return lax.all_to_all(blocks, axes, 0, 0)  4.83 us
  transfers between devices with their start and end apart: 1, of which 1 were waited for; matrix products, arithmetic and copies ran while one was open for 0% of the time, Pallas kernels for 5%

profile of v8, /device:TPU:2, one launch (start us, length us, event | category | flops | bytes accessed | tf_op | source)
XLA Modules:
  0.0 229.0 jit_solution(16670785700922231660)
XLA Ops:
  0.0 0.8 copy-done
  0.8 0.1 units.1
  0.9 33.6 %all_to_all.70.block_ref = bf16[8,16,768]{2,1,0:T(8,128)(2,1)S(1)} all-to-all(bf16[8,16,768]{2,1,0:T(8,128)(2,1)S(1)} %units.1), channel_id=1, replica_groups=mesh['x'=4,'zh'=8,'zl'=2,'y'=4,'core'=2] {'zh'}, dimensions={0} | all-to-all | bytes 393216 | tf_op jit(solution)/shard_map/all_to_all | solution.py:29
  34.5 1.3 copies.1
  35.8 4.8 %all-to-all-start.1 = ((bf16[8,8,16,768]{3,2,1,0:T(8,128)(2,1)}), bf16[8,8,16,768]{3,2,1,0:T(8,128)(2,1)S(1)}, u32[]{:S(2)}, u32[]{:S(2)}) async-start(bf16[8,8,16,768]{3,2,1,0:T(8,128)(2,1)} %copies.1), calls=%async_computation.1 | async-start | bytes 3145728 | tf_op jit(solution)/shard_map/all_to_all | solution.py:29
  40.6 0.1 reshape.9
  40.8 0.1 reshape.10.group_ref
  40.9 0.3 copy.8.ids_ref
  41.2 12.1 %prepare.1 = (bf16[2048,768]{1,0:T(8,128)(2,1)}, bf16[2048,1024]{1,0:T(8,128)(2,1)}) custom-call(bf16[2048,768]{1,0:T(8,128)(2,1)} %x_ref.1, s32[2048,16]{1,0:T(8,128)S(1)} %copy.8.ids_ref, s32[1,1024]{1,0:T(1,128)S(1)} %reshape.10.group_ref), custom_call_target="tpu_custom_call" | custom-call | flops 8589934592 | bytes 10620928 | tf_op jit(solution)/shard_map/prepare/pallas_call | solution.py:225
  53.3 3.3 %all-to-all-done.1 = bf16[8,8,16,768]{3,2,1,0:T(8,128)(2,1)S(1)} async-done(((bf16[8,8,16,768]{3,2,1,0:T(8,128)(2,1)}), bf16[8,8,16,768]{3,2,1,0:T(8,128)(2,1)S(1)}, u32[]{:S(2)}, u32[]{:S(2)}) %all-to-all-start.1) | async-done | bytes 1572896 | tf_op jit(solution)/shard_map/all_to_all | solution.py:29
  56.6 7.6 %similarity.1 = (bf16[2048,1024]{1,0:T(8,128)(2,1)S(1)}, f32[8,16,128]{2,1,0:T(8,128)S(1)}) custom-call(bf16[2048,768]{1,0:T(8,128)(2,1)} %get-tuple-element.9.unit_hbm, bf16[1024,768]{1,0:T(8,128)(2,1)S(1)} %bitcast.8, bf16[2048,1024]{1,0:T(8,128)(2,1)} %get-tuple-element.10.match_hbm), custom_call_target="tpu_custom_call" | custom-call | flops 3221225472 | bytes 13172736 | tf_op jit(solution)/shard_map/similarity/pallas_call | solution.py:225
  64.2 9.9 %all_to_all.71.parts_ref = f32[8,16,128]{2,1,0:T(8,128)S(1)} all-to-all(f32[8,16,128]{2,1,0:T(8,128)S(1)} %get-tuple-element.11), channel_id=1, replica_groups=mesh['x'=4,'zh'=8,'zl'=2,'y'=4,'core'=2] {'y','core'}, dimensions={0} | all-to-all | bytes 131072 | tf_op jit(solution)/shard_map/all_to_all | solution.py:29
  74.1 0.7 columns.3
  74.7 8.2 %all_to_all.72.parts_ref = f32[4,8,128]{2,1,0:T(8,128)S(1)} all-to-all(f32[4,8,128]{2,1,0:T(8,128)S(1)} %columns.3), channel_id=1, replica_groups=mesh['x'=4,'zh'=8,'zl'=2,'y'=4,'core'=2] {'x'}, dimensions={0} | all-to-all | bytes 32768 | tf_op jit(solution)/shard_map/all_to_all | solution.py:29
  82.9 19.7 %all_to_all.73.parts_ref = f32[16,8,128]{2,1,0:T(8,128)S(1)} all-to-all(f32[16,8,128]{2,1,0:T(8,128)S(1)} %across.3), channel_id=1, replica_groups=mesh['x'=4,'zh'=8,'zl'=2,'y'=4,'core'=2] {'zh','zl'}, dimensions={0} | all-to-all | bytes 131072 | tf_op jit(solution)/shard_map/all_to_all | solution.py:29
  102.6 1.2 rows.3
  103.8 8.0 %all_to_all.74.parts_ref = f32[8,16,128]{2,1,0:T(8,128)S(1)} all-to-all(f32[8,16,128]{2,1,0:T(8,128)S(1)} %rows.3), channel_id=1, replica_groups=mesh['x'=4,'zh'=8,'zl'=2,'y'=4,'core'=2] {'y','core'}, dimensions={0} | all-to-all | bytes 131072 | tf_op jit(solution)/shard_map/all_to_all | solution.py:29
  111.8 0.7 columns.4
  112.5 7.7 %all_to_all.75.parts_ref = f32[4,8,128]{2,1,0:T(8,128)S(1)} all-to-all(f32[4,8,128]{2,1,0:T(8,128)S(1)} %columns.4), channel_id=1, replica_groups=mesh['x'=4,'zh'=8,'zl'=2,'y'=4,'core'=2] {'x'}, dimensions={0} | all-to-all | bytes 32768 | tf_op jit(solution)/shard_map/all_to_all | solution.py:29
  120.2 15.5 %all_to_all.76.parts_ref = f32[16,8,128]{2,1,0:T(8,128)S(1)} all-to-all(f32[16,8,128]{2,1,0:T(8,128)S(1)} %across.4), channel_id=1, replica_groups=mesh['x'=4,'zh'=8,'zl'=2,'y'=4,'core'=2] {'zh','zl'}, dimensions={0} | all-to-all | bytes 131072 | tf_op jit(solution)/shard_map/all_to_all | solution.py:29
  135.7 1.2 rows.4
  136.9 8.0 %all_to_all.77.parts_ref = f32[8,16,128]{2,1,0:T(8,128)S(1)} all-to-all(f32[8,16,128]{2,1,0:T(8,128)S(1)} %rows.4), channel_id=1, replica_groups=mesh['x'=4,'zh'=8,'zl'=2,'y'=4,'core'=2] {'y','core'}, dimensions={0} | all-to-all | bytes 131072 | tf_op jit(solution)/shard_map/all_to_all | solution.py:29
  144.9 0.7 columns.5
  145.6 8.0 %all_to_all.78.parts_ref = f32[4,8,128]{2,1,0:T(8,128)S(1)} all-to-all(f32[4,8,128]{2,1,0:T(8,128)S(1)} %columns.5), channel_id=1, replica_groups=mesh['x'=4,'zh'=8,'zl'=2,'y'=4,'core'=2] {'x'}, dimensions={0} | all-to-all | bytes 32768 | tf_op jit(solution)/shard_map/all_to_all | solution.py:29
  153.6 15.5 %all_to_all.79.parts_ref = f32[16,8,128]{2,1,0:T(8,128)S(1)} all-to-all(f32[16,8,128]{2,1,0:T(8,128)S(1)} %across.5), channel_id=1, replica_groups=mesh['x'=4,'zh'=8,'zl'=2,'y'=4,'core'=2] {'zh','zl'}, dimensions={0} | all-to-all | bytes 131072 | tf_op jit(solution)/shard_map/all_to_all | solution.py:29
  169.1 1.2 rows.5
  170.3 8.0 %all_to_all.80.parts_ref = f32[8,16,128]{2,1,0:T(8,128)S(1)} all-to-all(f32[8,16,128]{2,1,0:T(8,128)S(1)} %rows.5), channel_id=1, replica_groups=mesh['x'=4,'zh'=8,'zl'=2,'y'=4,'core'=2] {'y','core'}, dimensions={0} | all-to-all | bytes 131072 | tf_op jit(solution)/shard_map/all_to_all | solution.py:29
  178.3 4.0 %numerator.1 = bf16[8,784,128]{2,1,0:T(8,128)(2,1)S(1)} custom-call(f32[8,16,128]{2,1,0:T(8,128)S(1)} %all_to_all.80.parts_ref, bf16[2048,1024]{1,0:T(8,128)(2,1)S(1)} %get-tuple-element.12.sim_ref, bf16[2048,768]{1,0:T(8,128)(2,1)S(1)} %copy-done.2), custom_call_target="tpu_custom_call" | custom-call | flops 3221225472 | bytes 9011200 | tf_op jit(solution)/shard_map/numerator/pallas_call | solution.py:225
  182.3 24.8 %all_to_all.81.parts_ref = bf16[8,784,128]{2,1,0:T(8,128)(2,1)S(1)} all-to-all(bf16[8,784,128]{2,1,0:T(8,128)(2,1)S(1)} %numerator.1), channel_id=1, replica_groups=mesh['x'=4,'zh'=8,'zl'=2,'y'=4,'core'=2] {'x','zl'}, dimensions={0} | all-to-all | bytes 3211264 | tf_op jit(solution)/shard_map/all_to_all | solution.py:29
  207.1 0.3 hand_on.1
  207.4 20.9 %all_to_all.82.parts_ref = bf16[8,104,128]{2,1,0:T(8,128)(2,1)S(1)} all-to-all(bf16[8,104,128]{2,1,0:T(8,128)(2,1)S(1)} %hand_on.1), channel_id=1, replica_groups=mesh['x'=4,'zh'=8,'zl'=2,'y'=4,'core'=2] {'zh'}, dimensions={0} | all-to-all | bytes 425984 | tf_op jit(solution)/shard_map/all_to_all | solution.py:29
  228.3 0.7 update.1
  (14 shorter events, 0.1 us)
Async XLA Ops:
  0.0 0.8 copy-start
  0.8 39.8 %copy-start.4 = (s32[8192]{0:T(1024)S(1)}, s32[8192]{0:T(1024)}, u32[]{:S(2)}) copy-start(s32[8192]{0:T(1024)} %param.7) | copy-start | bytes 98308
  0.8 40.1 %copy-start.3 = (s32[2048,16]{0,1:T(8,128)S(1)}, s32[2048,16]{0,1:T(8,128)}, u32[]{:S(2)}) copy-start(s32[2048,16]{0,1:T(8,128)} %param.5) | copy-start | bytes 393220
  35.8 20.8 %all-to-all-start.1 = ((bf16[8,8,16,768]{3,2,1,0:T(8,128)(2,1)}), bf16[8,8,16,768]{3,2,1,0:T(8,128)(2,1)S(1)}, u32[]{:S(2)}, u32[]{:S(2)}) async-start(bf16[8,8,16,768]{3,2,1,0:T(8,128)(2,1)} %copies.1), calls=%async_computation.1 | async-start | bytes 3145728 | tf_op jit(solution)/shard_map/all_to_all | solution.py:29
  145.6 32.7 %copy-start.2 = (bf16[2048,768]{1,0:T(8,128)(2,1)S(1)}, bf16[2048,768]{1,0:T(8,128)(2,1)}, u32[]{:S(2)}) copy-start(bf16[2048,768]{1,0:T(8,128)(2,1)} %x_ref.1) | copy-start | bytes 9437188
  182.3 46.0 %copy-start.1 = (f32[16,768]{1,0:T(8,128)S(1)}, f32[16,768]{1,0:T(8,128)}, u32[]{:S(2)}) copy-start(f32[16,768]{1,0:T(8,128)} %cent_ref.3) | copy-start | bytes 147460

commit v9 on v8

--- a/solution.py
+++ b/solution.py
@@ -102,9 +102,14 @@
     out_ref[...] = jnp.broadcast_to(unit_rows(cent_ref[...]).astype(bf16)[None], out_ref.shape)
 
 
-def copies_kernel(block_ref, out_ref):
-    for i in range(out_ref.shape[0]):
-        out_ref[i] = block_ref[...]
+def copies_kernel(block_ref, out_hbm, sems):
+    copies = [
+        pltpu.make_async_copy(block_ref, out_hbm.at[i], sems.at[i]) for i in range(out_hbm.shape[0])
+    ]
+    for copy in copies:
+        copy.start()
+    for copy in copies:
+        copy.wait()
 
 
 def sum_copies_kernel(parts_ref, out_ref):
@@ -115,7 +120,7 @@
     ones = jnp.ones((total_ref.shape[0], sim_ref.shape[1]), bf16)
     scale = math.log2(math.e) / entropic_smoothing
     total_rows = unit_ref.shape[0]
-    starts = [0, TILE] + list(range(2 * TILE, total_rows, 2 * TILE))
+    starts = [0, LANES, TILE] + list(range(2 * TILE, total_rows, 2 * TILE))
     spans = [pl.ds(i, j - i) for i, j in zip(starts, starts[1:] + [total_rows])]
 
     def into(b):
@@ -126,18 +131,19 @@
         )
 
     def work(b):
-        for first in range(starts[b], starts[b] + spans[b].size, TILE):
-            rows = pl.ds(first, TILE)
+        step = min(TILE, spans[b].size)
+        for first in range(starts[b], starts[b] + spans[b].size, step):
+            rows = pl.ds(first, step)
             dots = lax.dot_general(
                 unit_ref[rows, :], cent_ref[...], (((1,), (1,)), ((), ())), preferred_element_type=f32
             )
             sim = (jnp.exp2(dots * scale) * match_ref[rows, :].astype(f32)).astype(bf16)
             sim_ref[rows, :] = sim
             totals = lax.dot_general(ones, sim, (((1,), (1,)), ((), ())), preferred_element_type=f32)
-            for q in range(TILE // LANES):
+            for q in range(step // LANES):
                 total_ref[:, first // LANES + q, :] = totals[:, q * LANES : (q + 1) * LANES]
 
-    in_turn(len(spans), into, work, ahead=3)
+    in_turn(len(spans), into, work)
 
 
 def column_kernel(parts_ref, sim_ref, out_ref):
@@ -217,7 +223,7 @@
     out = hbm if hbm_out else vmem
     single = len(outs) == 1
     if hbm_out:
-        outs = [pltpu.HBM(o.shape, o.dtype) for o in outs]
+        outs = tuple(pltpu.HBM(o.shape, o.dtype) for o in outs)
     operands = [
         pltpu.with_memory_space_constraint(o, pltpu.HBM) if i in hbm_in else o
         for i, o in enumerate(operands)
@@ -273,7 +279,16 @@
         unit_copies_kernel, "units", (centroids,), (array((far_size, local_count, width), bf16),), 4, 0
     )
     part = exchange(copies, far)
-    copies = call(copies_kernel, "copies", (part,), (array((near_size,) + part.shape, bf16),), 4, 0)
+    copies = call(
+        copies_kernel,
+        "copies",
+        (part,),
+        (array((near_size,) + part.shape, bf16),),
+        4,
+        0,
+        scratch=[pltpu.SemaphoreType.DMA((near_size,))],
+        hbm_out=True,
+    )
     group_centroids = exchange(copies, near).reshape(columns, width)
 
     product = 2 * row_count * columns

time: 230 us -> 230 us (level)
  no operation moved by 1% of the time
where the time goes in v9:
time: 230 us
  blocking collectives  188 us (82%)
  Pallas kernels  32.4 us (14%)
  starting transfers between devices  4.84 us (2%)
  waiting for transfers between devices  3.23 us (1%)
    all_to_all x13, blocking collectives, exchange(): return lax.all_to_all(blocks, axes, 0, 0)  188 us
    pallas_call x16, Pallas kernels, call(): pl.pallas_call(kernel, name=name, out_shape=outs[0] if single else outs,...  32.4 us
    all_to_all x1, starting transfers between devices, exchange(): return lax.all_to_all(blocks, axes, 0, 0)  4.84 us
  transfers between devices with their start and end apart: 1, of which 1 were waited for; matrix products, arithmetic and copies ran while one was open for 0% of the time, Pallas kernels for 5%

profile of v9, /device:TPU:2, one launch (start us, length us, event | category | flops | bytes accessed | tf_op | source)
XLA Modules:
  0.0 229.7 jit_solution(18315798442286091847)
XLA Ops:
  0.0 0.8 copy-done
  0.8 0.1 units.1
  0.9 33.6 %all_to_all.70.block_ref = bf16[8,16,768]{2,1,0:T(8,128)(2,1)S(1)} all-to-all(bf16[8,16,768]{2,1,0:T(8,128)(2,1)S(1)} %units.1), channel_id=1, replica_groups=mesh['x'=4,'zh'=8,'zl'=2,'y'=4,'core'=2] {'zh'}, dimensions={0} | all-to-all | bytes 393216 | tf_op jit(solution)/shard_map/all_to_all | solution.py:29
  34.5 1.3 copies.1
  35.8 4.8 %all-to-all-start.1 = ((bf16[8,8,16,768]{3,2,1,0:T(8,128)(2,1)}), bf16[8,8,16,768]{3,2,1,0:T(8,128)(2,1)S(1)}, u32[]{:S(2)}, u32[]{:S(2)}) async-start(bf16[8,8,16,768]{3,2,1,0:T(8,128)(2,1)} %copies.1), calls=%async_computation.1 | async-start | bytes 3145728 | tf_op jit(solution)/shard_map/all_to_all | solution.py:29
  40.6 0.1 reshape.9
  40.8 0.1 reshape.10.group_ref
  40.9 0.3 copy.8.ids_ref
  41.2 12.1 %prepare.1 = (bf16[2048,768]{1,0:T(8,128)(2,1)}, bf16[2048,1024]{1,0:T(8,128)(2,1)}) custom-call(bf16[2048,768]{1,0:T(8,128)(2,1)} %x_ref.1, s32[2048,16]{1,0:T(8,128)S(1)} %copy.8.ids_ref, s32[1,1024]{1,0:T(1,128)S(1)} %reshape.10.group_ref), custom_call_target="tpu_custom_call" | custom-call | flops 8589934592 | bytes 10620928 | tf_op jit(solution)/shard_map/prepare/pallas_call | solution.py:231
  53.4 3.2 %all-to-all-done.1 = bf16[8,8,16,768]{3,2,1,0:T(8,128)(2,1)S(1)} async-done(((bf16[8,8,16,768]{3,2,1,0:T(8,128)(2,1)}), bf16[8,8,16,768]{3,2,1,0:T(8,128)(2,1)S(1)}, u32[]{:S(2)}, u32[]{:S(2)}) %all-to-all-start.1) | async-done | bytes 1572896 | tf_op jit(solution)/shard_map/all_to_all | solution.py:29
  56.6 8.3 %similarity.1 = (bf16[2048,1024]{1,0:T(8,128)(2,1)S(1)}, f32[8,16,128]{2,1,0:T(8,128)S(1)}) custom-call(bf16[2048,768]{1,0:T(8,128)(2,1)} %get-tuple-element.9.unit_hbm, bf16[1024,768]{1,0:T(8,128)(2,1)S(1)} %bitcast.8, bf16[2048,1024]{1,0:T(8,128)(2,1)} %get-tuple-element.10.match_hbm), custom_call_target="tpu_custom_call" | custom-call | flops 3221225472 | bytes 13172736 | tf_op jit(solution)/shard_map/similarity/pallas_call | solution.py:231
  64.9 9.9 %all_to_all.71.parts_ref = f32[8,16,128]{2,1,0:T(8,128)S(1)} all-to-all(f32[8,16,128]{2,1,0:T(8,128)S(1)} %get-tuple-element.11), channel_id=1, replica_groups=mesh['x'=4,'zh'=8,'zl'=2,'y'=4,'core'=2] {'y','core'}, dimensions={0} | all-to-all | bytes 131072 | tf_op jit(solution)/shard_map/all_to_all | solution.py:29
  74.8 0.7 columns.3
  75.4 8.2 %all_to_all.72.parts_ref = f32[4,8,128]{2,1,0:T(8,128)S(1)} all-to-all(f32[4,8,128]{2,1,0:T(8,128)S(1)} %columns.3), channel_id=1, replica_groups=mesh['x'=4,'zh'=8,'zl'=2,'y'=4,'core'=2] {'x'}, dimensions={0} | all-to-all | bytes 32768 | tf_op jit(solution)/shard_map/all_to_all | solution.py:29
  83.6 19.7 %all_to_all.73.parts_ref = f32[16,8,128]{2,1,0:T(8,128)S(1)} all-to-all(f32[16,8,128]{2,1,0:T(8,128)S(1)} %across.3), channel_id=1, replica_groups=mesh['x'=4,'zh'=8,'zl'=2,'y'=4,'core'=2] {'zh','zl'}, dimensions={0} | all-to-all | bytes 131072 | tf_op jit(solution)/shard_map/all_to_all | solution.py:29
  103.3 1.2 rows.3
  104.5 8.0 %all_to_all.74.parts_ref = f32[8,16,128]{2,1,0:T(8,128)S(1)} all-to-all(f32[8,16,128]{2,1,0:T(8,128)S(1)} %rows.3), channel_id=1, replica_groups=mesh['x'=4,'zh'=8,'zl'=2,'y'=4,'core'=2] {'y','core'}, dimensions={0} | all-to-all | bytes 131072 | tf_op jit(solution)/shard_map/all_to_all | solution.py:29
  112.5 0.7 columns.4
  113.2 7.7 %all_to_all.75.parts_ref = f32[4,8,128]{2,1,0:T(8,128)S(1)} all-to-all(f32[4,8,128]{2,1,0:T(8,128)S(1)} %columns.4), channel_id=1, replica_groups=mesh['x'=4,'zh'=8,'zl'=2,'y'=4,'core'=2] {'x'}, dimensions={0} | all-to-all | bytes 32768 | tf_op jit(solution)/shard_map/all_to_all | solution.py:29
  120.9 15.5 %all_to_all.76.parts_ref = f32[16,8,128]{2,1,0:T(8,128)S(1)} all-to-all(f32[16,8,128]{2,1,0:T(8,128)S(1)} %across.4), channel_id=1, replica_groups=mesh['x'=4,'zh'=8,'zl'=2,'y'=4,'core'=2] {'zh','zl'}, dimensions={0} | all-to-all | bytes 131072 | tf_op jit(solution)/shard_map/all_to_all | solution.py:29
  136.4 1.2 rows.4
  137.6 8.0 %all_to_all.77.parts_ref = f32[8,16,128]{2,1,0:T(8,128)S(1)} all-to-all(f32[8,16,128]{2,1,0:T(8,128)S(1)} %rows.4), channel_id=1, replica_groups=mesh['x'=4,'zh'=8,'zl'=2,'y'=4,'core'=2] {'y','core'}, dimensions={0} | all-to-all | bytes 131072 | tf_op jit(solution)/shard_map/all_to_all | solution.py:29
  145.6 0.7 columns.5
  146.3 8.0 %all_to_all.78.parts_ref = f32[4,8,128]{2,1,0:T(8,128)S(1)} all-to-all(f32[4,8,128]{2,1,0:T(8,128)S(1)} %columns.5), channel_id=1, replica_groups=mesh['x'=4,'zh'=8,'zl'=2,'y'=4,'core'=2] {'x'}, dimensions={0} | all-to-all | bytes 32768 | tf_op jit(solution)/shard_map/all_to_all | solution.py:29
  154.3 15.5 %all_to_all.79.parts_ref = f32[16,8,128]{2,1,0:T(8,128)S(1)} all-to-all(f32[16,8,128]{2,1,0:T(8,128)S(1)} %across.5), channel_id=1, replica_groups=mesh['x'=4,'zh'=8,'zl'=2,'y'=4,'core'=2] {'zh','zl'}, dimensions={0} | all-to-all | bytes 131072 | tf_op jit(solution)/shard_map/all_to_all | solution.py:29
  169.8 1.2 rows.5
  171.0 8.0 %all_to_all.80.parts_ref = f32[8,16,128]{2,1,0:T(8,128)S(1)} all-to-all(f32[8,16,128]{2,1,0:T(8,128)S(1)} %rows.5), channel_id=1, replica_groups=mesh['x'=4,'zh'=8,'zl'=2,'y'=4,'core'=2] {'y','core'}, dimensions={0} | all-to-all | bytes 131072 | tf_op jit(solution)/shard_map/all_to_all | solution.py:29
  179.0 4.0 %numerator.1 = bf16[8,784,128]{2,1,0:T(8,128)(2,1)S(1)} custom-call(f32[8,16,128]{2,1,0:T(8,128)S(1)} %all_to_all.80.parts_ref, bf16[2048,1024]{1,0:T(8,128)(2,1)S(1)} %get-tuple-element.12.sim_ref, bf16[2048,768]{1,0:T(8,128)(2,1)S(1)} %copy-done.2), custom_call_target="tpu_custom_call" | custom-call | flops 3221225472 | bytes 9011200 | tf_op jit(solution)/shard_map/numerator/pallas_call | solution.py:231
  183.0 24.8 %all_to_all.81.parts_ref = bf16[8,784,128]{2,1,0:T(8,128)(2,1)S(1)} all-to-all(bf16[8,784,128]{2,1,0:T(8,128)(2,1)S(1)} %numerator.1), channel_id=1, replica_groups=mesh['x'=4,'zh'=8,'zl'=2,'y'=4,'core'=2] {'x','zl'}, dimensions={0} | all-to-all | bytes 3211264 | tf_op jit(solution)/shard_map/all_to_all | solution.py:29
  207.8 0.3 hand_on.1
  208.1 20.9 %all_to_all.82.parts_ref = bf16[8,104,128]{2,1,0:T(8,128)(2,1)S(1)} all-to-all(bf16[8,104,128]{2,1,0:T(8,128)(2,1)S(1)} %hand_on.1), channel_id=1, replica_groups=mesh['x'=4,'zh'=8,'zl'=2,'y'=4,'core'=2] {'zh'}, dimensions={0} | all-to-all | bytes 425984 | tf_op jit(solution)/shard_map/all_to_all | solution.py:29
  229.0 0.7 update.1
  (14 shorter events, 0.1 us)
Async XLA Ops:
  0.0 0.8 copy-start
  0.8 39.8 %copy-start.4 = (s32[8192]{0:T(1024)S(1)}, s32[8192]{0:T(1024)}, u32[]{:S(2)}) copy-start(s32[8192]{0:T(1024)} %param.7) | copy-start | bytes 98308
  0.8 40.1 %copy-start.3 = (s32[2048,16]{0,1:T(8,128)S(1)}, s32[2048,16]{0,1:T(8,128)}, u32[]{:S(2)}) copy-start(s32[2048,16]{0,1:T(8,128)} %param.5) | copy-start | bytes 393220
  35.8 20.8 %all-to-all-start.1 = ((bf16[8,8,16,768]{3,2,1,0:T(8,128)(2,1)}), bf16[8,8,16,768]{3,2,1,0:T(8,128)(2,1)S(1)}, u32[]{:S(2)}, u32[]{:S(2)}) async-start(bf16[8,8,16,768]{3,2,1,0:T(8,128)(2,1)} %copies.1), calls=%async_computation.1 | async-start | bytes 3145728 | tf_op jit(solution)/shard_map/all_to_all | solution.py:29
  146.3 32.7 %copy-start.2 = (bf16[2048,768]{1,0:T(8,128)(2,1)S(1)}, bf16[2048,768]{1,0:T(8,128)(2,1)}, u32[]{:S(2)}) copy-start(bf16[2048,768]{1,0:T(8,128)(2,1)} %x_ref.1) | copy-start | bytes 9437188
  183.0 46.0 %copy-start.1 = (f32[16,768]{1,0:T(8,128)S(1)}, f32[16,768]{1,0:T(8,128)}, u32[]{:S(2)}) copy-start(f32[16,768]{1,0:T(8,128)} %cent_ref.3) | copy-start | bytes 147460

commit v10 on v8

--- a/solution.py
+++ b/solution.py
@@ -115,7 +115,7 @@
     ones = jnp.ones((total_ref.shape[0], sim_ref.shape[1]), bf16)
     scale = math.log2(math.e) / entropic_smoothing
     total_rows = unit_ref.shape[0]
-    starts = [0, TILE] + list(range(2 * TILE, total_rows, 2 * TILE))
+    starts = [0, total_rows // 4]
     spans = [pl.ds(i, j - i) for i, j in zip(starts, starts[1:] + [total_rows])]
 
     def into(b):
@@ -137,7 +137,7 @@
             for q in range(TILE // LANES):
                 total_ref[:, first // LANES + q, :] = totals[:, q * LANES : (q + 1) * LANES]
 
-    in_turn(len(spans), into, work, ahead=3)
+    in_turn(len(spans), into, work)
 
 
 def column_kernel(parts_ref, sim_ref, out_ref):

time: 230 us -> 230 us (level)
  no operation moved by 1% of the time
where the time goes in v10:
time: 230 us; the launch traced here: 229 us
  blocking collectives  188 us (82%)
  Pallas kernels  31.5 us (14%)
  starting transfers between devices  4.83 us (2%)
  waiting for transfers between devices  3.25 us (1%)
    all_to_all x13, blocking collectives, exchange(): return lax.all_to_all(blocks, axes, 0, 0)  188 us
    pallas_call x16, Pallas kernels, call(): pl.pallas_call(kernel, name=name, out_shape=outs[0] if single else outs,...  31.5 us
    all_to_all x1, starting transfers between devices, exchange(): return lax.all_to_all(blocks, axes, 0, 0)  4.83 us
  transfers between devices with their start and end apart: 1, of which 1 were waited for; matrix products, arithmetic and copies ran while one was open for 0% of the time, Pallas kernels for 5%

profile of v10, /device:TPU:2, one launch (start us, length us, event | category | flops | bytes accessed | tf_op | source)
XLA Modules:
  0.0 228.8 jit_solution(2038985037414199833)
XLA Ops:
  0.0 0.8 copy-done
  0.8 0.1 units.1
  0.9 33.6 %all_to_all.70.block_ref = bf16[8,16,768]{2,1,0:T(8,128)(2,1)S(1)} all-to-all(bf16[8,16,768]{2,1,0:T(8,128)(2,1)S(1)} %units.1), channel_id=1, replica_groups=mesh['x'=4,'zh'=8,'zl'=2,'y'=4,'core'=2] {'zh'}, dimensions={0} | all-to-all | bytes 393216 | tf_op jit(solution)/shard_map/all_to_all | solution.py:29
  34.5 1.3 copies.1
  35.8 4.8 %all-to-all-start.1 = ((bf16[8,8,16,768]{3,2,1,0:T(8,128)(2,1)}), bf16[8,8,16,768]{3,2,1,0:T(8,128)(2,1)S(1)}, u32[]{:S(2)}, u32[]{:S(2)}) async-start(bf16[8,8,16,768]{3,2,1,0:T(8,128)(2,1)} %copies.1), calls=%async_computation.1 | async-start | bytes 3145728 | tf_op jit(solution)/shard_map/all_to_all | solution.py:29
  40.6 0.1 reshape.9
  40.8 0.1 reshape.10.group_ref
  40.9 0.3 copy.8.ids_ref
  41.2 12.1 %prepare.1 = (bf16[2048,768]{1,0:T(8,128)(2,1)}, bf16[2048,1024]{1,0:T(8,128)(2,1)}) custom-call(bf16[2048,768]{1,0:T(8,128)(2,1)} %x_ref.1, s32[2048,16]{1,0:T(8,128)S(1)} %copy.8.ids_ref, s32[1,1024]{1,0:T(1,128)S(1)} %reshape.10.group_ref), custom_call_target="tpu_custom_call" | custom-call | flops 8589934592 | bytes 10620928 | tf_op jit(solution)/shard_map/prepare/pallas_call | solution.py:225
  53.3 3.3 %all-to-all-done.1 = bf16[8,8,16,768]{3,2,1,0:T(8,128)(2,1)S(1)} async-done(((bf16[8,8,16,768]{3,2,1,0:T(8,128)(2,1)}), bf16[8,8,16,768]{3,2,1,0:T(8,128)(2,1)S(1)}, u32[]{:S(2)}, u32[]{:S(2)}) %all-to-all-start.1) | async-done | bytes 1572896 | tf_op jit(solution)/shard_map/all_to_all | solution.py:29
  56.6 7.4 %similarity.1 = (bf16[2048,1024]{1,0:T(8,128)(2,1)S(1)}, f32[8,16,128]{2,1,0:T(8,128)S(1)}) custom-call(bf16[2048,768]{1,0:T(8,128)(2,1)} %get-tuple-element.9.unit_hbm, bf16[1024,768]{1,0:T(8,128)(2,1)S(1)} %bitcast.8, bf16[2048,1024]{1,0:T(8,128)(2,1)} %get-tuple-element.10.match_hbm), custom_call_target="tpu_custom_call" | custom-call | flops 3221225472 | bytes 13172736 | tf_op jit(solution)/shard_map/similarity/pallas_call | solution.py:225
  64.0 9.9 %all_to_all.71.parts_ref = f32[8,16,128]{2,1,0:T(8,128)S(1)} all-to-all(f32[8,16,128]{2,1,0:T(8,128)S(1)} %get-tuple-element.11), channel_id=1, replica_groups=mesh['x'=4,'zh'=8,'zl'=2,'y'=4,'core'=2] {'y','core'}, dimensions={0} | all-to-all | bytes 131072 | tf_op jit(solution)/shard_map/all_to_all | solution.py:29
  73.9 0.7 columns.3
  74.5 8.2 %all_to_all.72.parts_ref = f32[4,8,128]{2,1,0:T(8,128)S(1)} all-to-all(f32[4,8,128]{2,1,0:T(8,128)S(1)} %columns.3), channel_id=1, replica_groups=mesh['x'=4,'zh'=8,'zl'=2,'y'=4,'core'=2] {'x'}, dimensions={0} | all-to-all | bytes 32768 | tf_op jit(solution)/shard_map/all_to_all | solution.py:29
  82.7 19.7 %all_to_all.73.parts_ref = f32[16,8,128]{2,1,0:T(8,128)S(1)} all-to-all(f32[16,8,128]{2,1,0:T(8,128)S(1)} %across.3), channel_id=1, replica_groups=mesh['x'=4,'zh'=8,'zl'=2,'y'=4,'core'=2] {'zh','zl'}, dimensions={0} | all-to-all | bytes 131072 | tf_op jit(solution)/shard_map/all_to_all | solution.py:29
  102.4 1.2 rows.3
  103.6 8.0 %all_to_all.74.parts_ref = f32[8,16,128]{2,1,0:T(8,128)S(1)} all-to-all(f32[8,16,128]{2,1,0:T(8,128)S(1)} %rows.3), channel_id=1, replica_groups=mesh['x'=4,'zh'=8,'zl'=2,'y'=4,'core'=2] {'y','core'}, dimensions={0} | all-to-all | bytes 131072 | tf_op jit(solution)/shard_map/all_to_all | solution.py:29
  111.6 0.7 columns.4
  112.3 7.7 %all_to_all.75.parts_ref = f32[4,8,128]{2,1,0:T(8,128)S(1)} all-to-all(f32[4,8,128]{2,1,0:T(8,128)S(1)} %columns.4), channel_id=1, replica_groups=mesh['x'=4,'zh'=8,'zl'=2,'y'=4,'core'=2] {'x'}, dimensions={0} | all-to-all | bytes 32768 | tf_op jit(solution)/shard_map/all_to_all | solution.py:29
  120.0 15.5 %all_to_all.76.parts_ref = f32[16,8,128]{2,1,0:T(8,128)S(1)} all-to-all(f32[16,8,128]{2,1,0:T(8,128)S(1)} %across.4), channel_id=1, replica_groups=mesh['x'=4,'zh'=8,'zl'=2,'y'=4,'core'=2] {'zh','zl'}, dimensions={0} | all-to-all | bytes 131072 | tf_op jit(solution)/shard_map/all_to_all | solution.py:29
  135.5 1.2 rows.4
  136.7 8.0 %all_to_all.77.parts_ref = f32[8,16,128]{2,1,0:T(8,128)S(1)} all-to-all(f32[8,16,128]{2,1,0:T(8,128)S(1)} %rows.4), channel_id=1, replica_groups=mesh['x'=4,'zh'=8,'zl'=2,'y'=4,'core'=2] {'y','core'}, dimensions={0} | all-to-all | bytes 131072 | tf_op jit(solution)/shard_map/all_to_all | solution.py:29
  144.7 0.7 columns.5
  145.4 8.0 %all_to_all.78.parts_ref = f32[4,8,128]{2,1,0:T(8,128)S(1)} all-to-all(f32[4,8,128]{2,1,0:T(8,128)S(1)} %columns.5), channel_id=1, replica_groups=mesh['x'=4,'zh'=8,'zl'=2,'y'=4,'core'=2] {'x'}, dimensions={0} | all-to-all | bytes 32768 | tf_op jit(solution)/shard_map/all_to_all | solution.py:29
  153.4 15.5 %all_to_all.79.parts_ref = f32[16,8,128]{2,1,0:T(8,128)S(1)} all-to-all(f32[16,8,128]{2,1,0:T(8,128)S(1)} %across.5), channel_id=1, replica_groups=mesh['x'=4,'zh'=8,'zl'=2,'y'=4,'core'=2] {'zh','zl'}, dimensions={0} | all-to-all | bytes 131072 | tf_op jit(solution)/shard_map/all_to_all | solution.py:29
  168.9 1.2 rows.5
  170.1 8.0 %all_to_all.80.parts_ref = f32[8,16,128]{2,1,0:T(8,128)S(1)} all-to-all(f32[8,16,128]{2,1,0:T(8,128)S(1)} %rows.5), channel_id=1, replica_groups=mesh['x'=4,'zh'=8,'zl'=2,'y'=4,'core'=2] {'y','core'}, dimensions={0} | all-to-all | bytes 131072 | tf_op jit(solution)/shard_map/all_to_all | solution.py:29
  178.1 4.0 %numerator.1 = bf16[8,784,128]{2,1,0:T(8,128)(2,1)S(1)} custom-call(f32[8,16,128]{2,1,0:T(8,128)S(1)} %all_to_all.80.parts_ref, bf16[2048,1024]{1,0:T(8,128)(2,1)S(1)} %get-tuple-element.12.sim_ref, bf16[2048,768]{1,0:T(8,128)(2,1)S(1)} %copy-done.2), custom_call_target="tpu_custom_call" | custom-call | flops 3221225472 | bytes 9011200 | tf_op jit(solution)/shard_map/numerator/pallas_call | solution.py:225
  182.1 24.8 %all_to_all.81.parts_ref = bf16[8,784,128]{2,1,0:T(8,128)(2,1)S(1)} all-to-all(bf16[8,784,128]{2,1,0:T(8,128)(2,1)S(1)} %numerator.1), channel_id=1, replica_groups=mesh['x'=4,'zh'=8,'zl'=2,'y'=4,'core'=2] {'x','zl'}, dimensions={0} | all-to-all | bytes 3211264 | tf_op jit(solution)/shard_map/all_to_all | solution.py:29
  206.9 0.3 hand_on.1
  207.2 20.9 %all_to_all.82.parts_ref = bf16[8,104,128]{2,1,0:T(8,128)(2,1)S(1)} all-to-all(bf16[8,104,128]{2,1,0:T(8,128)(2,1)S(1)} %hand_on.1), channel_id=1, replica_groups=mesh['x'=4,'zh'=8,'zl'=2,'y'=4,'core'=2] {'zh'}, dimensions={0} | all-to-all | bytes 425984 | tf_op jit(solution)/shard_map/all_to_all | solution.py:29
  228.1 0.7 update.1
  (14 shorter events, 0.1 us)
Async XLA Ops:
  0.0 0.8 copy-start
  0.8 39.8 %copy-start.4 = (s32[8192]{0:T(1024)S(1)}, s32[8192]{0:T(1024)}, u32[]{:S(2)}) copy-start(s32[8192]{0:T(1024)} %param.7) | copy-start | bytes 98308
  0.8 40.1 %copy-start.3 = (s32[2048,16]{0,1:T(8,128)S(1)}, s32[2048,16]{0,1:T(8,128)}, u32[]{:S(2)}) copy-start(s32[2048,16]{0,1:T(8,128)} %param.5) | copy-start | bytes 393220
  35.8 20.8 %all-to-all-start.1 = ((bf16[8,8,16,768]{3,2,1,0:T(8,128)(2,1)}), bf16[8,8,16,768]{3,2,1,0:T(8,128)(2,1)S(1)}, u32[]{:S(2)}, u32[]{:S(2)}) async-start(bf16[8,8,16,768]{3,2,1,0:T(8,128)(2,1)} %copies.1), calls=%async_computation.1 | async-start | bytes 3145728 | tf_op jit(solution)/shard_map/all_to_all | solution.py:29
  145.4 32.7 %copy-start.2 = (bf16[2048,768]{1,0:T(8,128)(2,1)S(1)}, bf16[2048,768]{1,0:T(8,128)(2,1)}, u32[]{:S(2)}) copy-start(bf16[2048,768]{1,0:T(8,128)(2,1)} %x_ref.1) | copy-start | bytes 9437188
  182.1 46.0 %copy-start.1 = (f32[16,768]{1,0:T(8,128)S(1)}, f32[16,768]{1,0:T(8,128)}, u32[]{:S(2)}) copy-start(f32[16,768]{1,0:T(8,128)} %cent_ref.3) | copy-start | bytes 147460

commit v11 on v6

--- a/solution.py
+++ b/solution.py
@@ -64,7 +64,8 @@
     half = CLUSTERS // 2
     cluster = lax.broadcasted_iota(jnp.int32, hot_ref.shape, 0)
     hot_ref[...] = jnp.where(cluster == group_ref[...], 1.0, 0.0).astype(bf16)
-    lane = lax.broadcasted_iota(jnp.int32, (TILE, half), 1).astype(f32).astype(bf16)
+    which = lax.broadcasted_iota(jnp.int32, (half, TILE), 0).astype(f32).astype(bf16)
+    which = which.reshape(half // 16, 16, TILE)
 
     def into(b):
         rows = pl.ds(b * TILE, TILE)
@@ -80,14 +81,20 @@
     def work(b):
         rows = pl.ds(b * TILE, TILE)
         unit_ref[rows, :] = unit_rows(x_ref[rows, :]).astype(bf16)
-        ids = ids_ref[rows, :]
+        ids = ids_ref[:, rows]
         matched = jnp.zeros((TILE, match_ref.shape[1]), f32)
         for first in (0, half):
-            near = (ids - first).astype(f32).astype(bf16)
-            picked = jnp.zeros(lane.shape, bf16)
-            for p in range(ids.shape[1]):
-                picked = jnp.where(near[:, p : p + 1] == lane, jnp.ones_like(picked), picked)
-            matched += jnp.dot(picked, hot_ref[first : first + half, :], preferred_element_type=f32)
+            near = (ids - first).astype(f32)
+            picked = jnp.zeros(which.shape, bf16)
+            for p in range(ids.shape[0]):
+                pick = jnp.broadcast_to(near[p : p + 1], (16, TILE)).astype(bf16)[None]
+                picked = jnp.where(pick == which, jnp.ones_like(picked), picked)
+            matched += lax.dot_general(
+                picked.reshape(half, TILE),
+                hot_ref[first : first + half, :],
+                (((0,), (0,)), ((), ())),
+                preferred_element_type=f32,
+            )
         match_ref[rows, :] = matched.astype(bf16)
         for copy in out_of(b):
             copy.start()
@@ -177,14 +184,14 @@
 
 def hand_on_kernel(count, parts_ref, out_ref):
     total = jnp.sum(parts_ref[...].astype(f32), axis=0)
-    chunk_rows = out_ref.shape[1] - 16
+    chunk_rows = out_ref.shape[1] - 8
     base = chunk_rows * out_ref.shape[0]
     for z in range(out_ref.shape[0]):
         out_ref[z, pl.ds(0, chunk_rows), :] = total[z * chunk_rows : (z + 1) * chunk_rows].astype(bf16)
         at = z * count % LANES
         row = total[base + z * count // LANES : base + z * count // LANES + 1]
         row = jnp.concatenate([row[:, at:], row[:, :at]], axis=1) if at else row
-        out_ref[z, pl.ds(chunk_rows, 16), :] = jnp.broadcast_to(row, (16, LANES)).astype(bf16)
+        out_ref[z, pl.ds(chunk_rows, 8), :] = jnp.broadcast_to(row, (8, LANES)).astype(bf16)
 
 
 def update_kernel(parts_ref, cent_ref, out_ref):
@@ -241,7 +248,7 @@
     unit_x, matched = call(
         prepare_kernel,
         "prepare",
-        (embeddings, coarse_ids, group_ids),
+        (embeddings, coarse_ids.T, group_ids),
         (unit_like, match_like),
         24,
         8 * row_count * CLUSTERS * columns,
@@ -309,7 +316,7 @@
         functools.partial(hand_on_kernel, local_count),
         "hand_on",
         (exchange(sums, near),),
-        (array((far_size, chunk_rows + 16, LANES), bf16),),
+        (array((far_size, chunk_rows + 8, LANES), bf16),),
         8,
         0,
     )

time: 232 us -> 227 us (0.978)
  blocking collectives: 180 us -> 175 us
  waiting for transfers between devices: 4.3 us -> 9.23 us
  Pallas kernels: 28.6 us -> 24 us
    all_to_all x1, waiting for transfers between devices: 4.3 us -> 9.23 us  [exchange(): return lax.all_to_all(blocks, axes, 0, 0)]
    all_to_all x13, blocking collectives: 180 us -> 175 us  [exchange(): return lax.all_to_all(blocks, axes, 0, 0)]
    pallas_call x16, Pallas kernels: 28.6 us -> 24 us  [call(): pl.pallas_call(kernel, name=name, out_shape=outs[0] if single else outs,...]
  transfers between devices with their start and end apart: 1 -> 1, of which waited for: 1 -> 1; matrix products, arithmetic and copies ran while one was open for 1% -> 0% of each run, Pallas kernels for 5% -> 3%
where the time goes in v11:
time: 227 us; the launch traced here: 226 us
  blocking collectives  175 us (77%)
  Pallas kernels  24 us (11%)
  starting transfers between devices  15.1 us (7%)
  waiting for transfers between devices  9.23 us (4%)
  local copies, waits for them, and re-layouts  2.72 us (1%)
    all_to_all x13, blocking collectives, exchange(): return lax.all_to_all(blocks, axes, 0, 0)  175 us
    pallas_call x16, Pallas kernels, call(): pl.pallas_call(kernel, name=name, out_shape=outs[0] if single else outs,...  24 us
    all_to_all x1, starting transfers between devices, exchange(): return lax.all_to_all(blocks, axes, 0, 0)  15.1 us
    all_to_all x1, waiting for transfers between devices, exchange(): return lax.all_to_all(blocks, axes, 0, 0)  9.23 us
  transfers between devices with their start and end apart: 1, of which 1 were waited for; matrix products, arithmetic and copies ran while one was open for 0% of the time, Pallas kernels for 3%

profile of v11, /device:TPU:2, one launch (start us, length us, event | category | flops | bytes accessed | tf_op | source)
XLA Modules:
  0.0 226.3 jit_solution(861908149882046719)
XLA Ops:
  0.0 0.8 copy-done.1
  0.8 0.8 units.1
  1.6 15.1 %all-to-all-start = ((bf16[8,16,768]{2,1,0:T(8,128)(2,1)}), bf16[8,16,768]{2,1,0:T(8,128)(2,1)S(1)}, u32[]{:S(2)}, u32[]{:S(2)}) async-start(bf16[8,16,768]{2,1,0:T(8,128)(2,1)} %units.1), calls=%async_computation | async-start | bytes 393216 | tf_op jit(solution)/shard_map/all_to_all | solution.py:29
  16.7 0.9 reshape.9
  17.6 0.1 reshape.10.group_ref
  17.7 0.9 copy-done.4
  18.6 7.5 %prepare.1 = (bf16[2048,768]{1,0:T(8,128)(2,1)}, bf16[2048,1024]{1,0:T(8,128)(2,1)}) custom-call(bf16[2048,768]{1,0:T(8,128)(2,1)} %x_ref.1, s32[16,2048]{1,0:T(8,128)S(1)} %bitcast.10, s32[1,1024]{1,0:T(1,128)S(1)} %reshape.10.group_ref), custom_call_target="tpu_custom_call" | custom-call | flops 8589934592 | bytes 10620928 | tf_op jit(solution)/shard_map/prepare/pallas_call | solution.py:218
  26.1 9.2 %all-to-all-done.block_ref = bf16[8,16,768]{2,1,0:T(8,128)(2,1)S(1)} async-done(((bf16[8,16,768]{2,1,0:T(8,128)(2,1)}), bf16[8,16,768]{2,1,0:T(8,128)(2,1)S(1)}, u32[]{:S(2)}, u32[]{:S(2)}) %all-to-all-start) | async-done | bytes 196640 | tf_op jit(solution)/shard_map/all_to_all | solution.py:29
  35.3 0.1 copies.1
  35.4 20.8 %all_to_all.70 = bf16[8,8,16,768]{3,2,1,0:T(8,128)(2,1)S(1)} all-to-all(bf16[8,8,16,768]{3,2,1,0:T(8,128)(2,1)S(1)} %copies.1), channel_id=1, replica_groups=mesh['x'=4,'zh'=8,'zl'=2,'y'=4,'core'=2] {'x','zl'}, dimensions={0} | all-to-all | bytes 3145728 | tf_op jit(solution)/shard_map/all_to_all | solution.py:29
  56.2 5.0 %similarity.1 = (bf16[2048,1024]{1,0:T(8,128)(2,1)S(1)}, f32[8,16,128]{2,1,0:T(8,128)S(1)}) custom-call(bf16[2048,768]{1,0:T(8,128)(2,1)S(1)} %copy-done.5, bf16[1024,768]{1,0:T(8,128)(2,1)S(1)} %bitcast.9, bf16[2048,1024]{1,0:T(8,128)(2,1)S(1)} %copy-done), custom_call_target="tpu_custom_call" | custom-call | flops 3221225472 | bytes 13172736 | tf_op jit(solution)/shard_map/similarity/pallas_call | solution.py:218
  61.2 9.9 %all_to_all.71.parts_ref = f32[8,16,128]{2,1,0:T(8,128)S(1)} all-to-all(f32[8,16,128]{2,1,0:T(8,128)S(1)} %get-tuple-element.11), channel_id=1, replica_groups=mesh['x'=4,'zh'=8,'zl'=2,'y'=4,'core'=2] {'y','core'}, dimensions={0} | all-to-all | bytes 131072 | tf_op jit(solution)/shard_map/all_to_all | solution.py:29
  71.1 0.7 columns.3
  71.8 8.0 %all_to_all.72.parts_ref = f32[4,8,128]{2,1,0:T(8,128)S(1)} all-to-all(f32[4,8,128]{2,1,0:T(8,128)S(1)} %columns.3), channel_id=1, replica_groups=mesh['x'=4,'zh'=8,'zl'=2,'y'=4,'core'=2] {'x'}, dimensions={0} | all-to-all | bytes 32768 | tf_op jit(solution)/shard_map/all_to_all | solution.py:29
  79.8 19.9 %all_to_all.73.parts_ref = f32[16,8,128]{2,1,0:T(8,128)S(1)} all-to-all(f32[16,8,128]{2,1,0:T(8,128)S(1)} %across.3), channel_id=1, replica_groups=mesh['x'=4,'zh'=8,'zl'=2,'y'=4,'core'=2] {'zh','zl'}, dimensions={0} | all-to-all | bytes 131072 | tf_op jit(solution)/shard_map/all_to_all | solution.py:29
  99.7 1.2 rows.3
  100.9 8.0 %all_to_all.74.parts_ref = f32[8,16,128]{2,1,0:T(8,128)S(1)} all-to-all(f32[8,16,128]{2,1,0:T(8,128)S(1)} %rows.3), channel_id=1, replica_groups=mesh['x'=4,'zh'=8,'zl'=2,'y'=4,'core'=2] {'y','core'}, dimensions={0} | all-to-all | bytes 131072 | tf_op jit(solution)/shard_map/all_to_all | solution.py:29
  108.9 0.7 columns.4
  109.6 7.9 %all_to_all.75.parts_ref = f32[4,8,128]{2,1,0:T(8,128)S(1)} all-to-all(f32[4,8,128]{2,1,0:T(8,128)S(1)} %columns.4), channel_id=1, replica_groups=mesh['x'=4,'zh'=8,'zl'=2,'y'=4,'core'=2] {'x'}, dimensions={0} | all-to-all | bytes 32768 | tf_op jit(solution)/shard_map/all_to_all | solution.py:29
  117.5 15.5 %all_to_all.76.parts_ref = f32[16,8,128]{2,1,0:T(8,128)S(1)} all-to-all(f32[16,8,128]{2,1,0:T(8,128)S(1)} %across.4), channel_id=1, replica_groups=mesh['x'=4,'zh'=8,'zl'=2,'y'=4,'core'=2] {'zh','zl'}, dimensions={0} | all-to-all | bytes 131072 | tf_op jit(solution)/shard_map/all_to_all | solution.py:29
  133.0 1.2 rows.4
  134.3 8.0 %all_to_all.77.parts_ref = f32[8,16,128]{2,1,0:T(8,128)S(1)} all-to-all(f32[8,16,128]{2,1,0:T(8,128)S(1)} %rows.4), channel_id=1, replica_groups=mesh['x'=4,'zh'=8,'zl'=2,'y'=4,'core'=2] {'y','core'}, dimensions={0} | all-to-all | bytes 131072 | tf_op jit(solution)/shard_map/all_to_all | solution.py:29
  142.2 0.7 columns.5
  142.9 8.0 %all_to_all.78.parts_ref = f32[4,8,128]{2,1,0:T(8,128)S(1)} all-to-all(f32[4,8,128]{2,1,0:T(8,128)S(1)} %columns.5), channel_id=1, replica_groups=mesh['x'=4,'zh'=8,'zl'=2,'y'=4,'core'=2] {'x'}, dimensions={0} | all-to-all | bytes 32768 | tf_op jit(solution)/shard_map/all_to_all | solution.py:29
  150.9 15.5 %all_to_all.79.parts_ref = f32[16,8,128]{2,1,0:T(8,128)S(1)} all-to-all(f32[16,8,128]{2,1,0:T(8,128)S(1)} %across.5), channel_id=1, replica_groups=mesh['x'=4,'zh'=8,'zl'=2,'y'=4,'core'=2] {'zh','zl'}, dimensions={0} | all-to-all | bytes 131072 | tf_op jit(solution)/shard_map/all_to_all | solution.py:29
  166.4 1.2 rows.5
  167.7 8.0 %all_to_all.80.parts_ref = f32[8,16,128]{2,1,0:T(8,128)S(1)} all-to-all(f32[8,16,128]{2,1,0:T(8,128)S(1)} %rows.5), channel_id=1, replica_groups=mesh['x'=4,'zh'=8,'zl'=2,'y'=4,'core'=2] {'y','core'}, dimensions={0} | all-to-all | bytes 131072 | tf_op jit(solution)/shard_map/all_to_all | solution.py:29
  175.7 4.0 %numerator.1 = bf16[8,784,128]{2,1,0:T(8,128)(2,1)S(1)} custom-call(f32[8,16,128]{2,1,0:T(8,128)S(1)} %all_to_all.80.parts_ref, bf16[2048,1024]{1,0:T(8,128)(2,1)S(1)} %get-tuple-element.12.sim_ref, bf16[2048,768]{1,0:T(8,128)(2,1)S(1)} %copy-done.3), custom_call_target="tpu_custom_call" | custom-call | flops 3221225472 | bytes 9011200 | tf_op jit(solution)/shard_map/numerator/pallas_call | solution.py:218
  179.7 24.8 %all_to_all.81.parts_ref = bf16[8,784,128]{2,1,0:T(8,128)(2,1)S(1)} all-to-all(bf16[8,784,128]{2,1,0:T(8,128)(2,1)S(1)} %numerator.1), channel_id=1, replica_groups=mesh['x'=4,'zh'=8,'zl'=2,'y'=4,'core'=2] {'x','zl'}, dimensions={0} | all-to-all | bytes 3211264 | tf_op jit(solution)/shard_map/all_to_all | solution.py:29
  204.5 0.3 hand_on.1
  204.8 20.9 %all_to_all.82.parts_ref = bf16[8,104,128]{2,1,0:T(8,128)(2,1)S(1)} all-to-all(bf16[8,104,128]{2,1,0:T(8,128)(2,1)S(1)} %hand_on.1), channel_id=1, replica_groups=mesh['x'=4,'zh'=8,'zl'=2,'y'=4,'core'=2] {'zh'}, dimensions={0} | all-to-all | bytes 425984 | tf_op jit(solution)/shard_map/all_to_all | solution.py:29
  225.6 0.7 update.1
  (15 shorter events, 0.1 us)
Async XLA Ops:
  0.0 0.8 copy-start.1
  1.6 33.8 %all-to-all-start = ((bf16[8,16,768]{2,1,0:T(8,128)(2,1)}), bf16[8,16,768]{2,1,0:T(8,128)(2,1)S(1)}, u32[]{:S(2)}, u32[]{:S(2)}) async-start(bf16[8,16,768]{2,1,0:T(8,128)(2,1)} %units.1), calls=%async_computation | async-start | bytes 393216 | tf_op jit(solution)/shard_map/all_to_all | solution.py:29
  17.7 0.9 copy-start.4
  35.3 20.9 %copy-start = (bf16[2048,1024]{1,0:T(8,128)(2,1)S(1)}, bf16[2048,1024]{1,0:T(8,128)(2,1)}, u32[]{:S(2)}) copy-start(bf16[2048,1024]{1,0:T(8,128)(2,1)} %get-tuple-element.10.unused.match_ref) | copy-start | bytes 12582916
  35.3 20.9 %copy-start.5 = (bf16[2048,768]{1,0:T(8,128)(2,1)S(1)}, bf16[2048,768]{1,0:T(8,128)(2,1)}, u32[]{:S(2)}) copy-start(bf16[2048,768]{1,0:T(8,128)(2,1)} %get-tuple-element.9.unit_ref) | copy-start | bytes 9437188
  142.9 32.7 %copy-start.3 = (bf16[2048,768]{1,0:T(8,128)(2,1)S(1)}, bf16[2048,768]{1,0:T(8,128)(2,1)}, u32[]{:S(2)}) copy-start(bf16[2048,768]{1,0:T(8,128)(2,1)} %x_ref.1) | copy-start | bytes 9437188
  179.6 46.0 %copy-start.2 = (f32[16,768]{1,0:T(8,128)S(1)}, f32[16,768]{1,0:T(8,128)}, u32[]{:S(2)}) copy-start(f32[16,768]{1,0:T(8,128)} %cent_ref.3) | copy-start | bytes 147460

commit v12 on v11

--- a/solution.py
+++ b/solution.py
@@ -105,8 +105,17 @@
             copy.wait()
 
 
-def unit_copies_kernel(cent_ref, out_ref):
-    out_ref[...] = jnp.broadcast_to(unit_rows(cent_ref[...]).astype(bf16)[None], out_ref.shape)
+def unit_copies_kernel(cent_hbm, out_hbm, cent_ref, unit_ref, sems):
+    count = out_hbm.shape[0]
+    fetch = pltpu.make_async_copy(cent_hbm, cent_ref, sems.at[count])
+    fetch.start()
+    fetch.wait()
+    unit_ref[...] = unit_rows(cent_ref[...]).astype(bf16)
+    copies = [pltpu.make_async_copy(unit_ref, out_hbm.at[i], sems.at[i]) for i in range(count)]
+    for copy in copies:
+        copy.start()
+    for copy in copies:
+        copy.wait()
 
 
 def copies_kernel(block_ref, unused, out_ref):
@@ -153,13 +162,15 @@
 
 def numerator_kernel(count, parts_ref, sim_ref, x_ref, out_ref, weight_ref):
     factor = 1.0 / jnp.sum(parts_ref[...], axis=0)
-    lhs = two_terms(as_row(factor))
-    mass = jnp.sum(jnp.dot(lhs, sim_ref[...], preferred_element_type=f32), axis=0, keepdims=True)
     columns = sim_ref.shape[1]
+    mass = jnp.zeros((8, columns), f32)
     for q in range(sim_ref.shape[0] // LANES):
         rows = pl.ds(q * LANES, LANES)
         scale = jnp.concatenate([down(factor[q : q + 1])] * (columns // LANES), axis=1)
-        weight_ref[rows, :] = (sim_ref[rows, :].astype(f32) * scale).astype(bf16)
+        weight = sim_ref[rows, :].astype(f32) * scale
+        weight_ref[rows, :] = weight.astype(bf16)
+        mass += jnp.sum(weight.reshape(LANES // 8, 8, columns), axis=0)
+    mass = jnp.sum(mass, axis=0, keepdims=True)
     chunks = x_ref.shape[1] // LANES
     held = columns // out_ref.shape[0]
     base = held * chunks
@@ -210,7 +221,7 @@
     out = hbm if hbm_out else vmem
     single = len(outs) == 1
     if hbm_out:
-        outs = [pltpu.HBM(o.shape, o.dtype) for o in outs]
+        outs = tuple(pltpu.HBM(o.shape, o.dtype) for o in outs)
     operands = [
         pltpu.with_memory_space_constraint(o, pltpu.HBM) if i in hbm_in else o
         for i, o in enumerate(operands)
@@ -263,7 +274,19 @@
         hbm_out=True,
     )
     copies = call(
-        unit_copies_kernel, "units", (centroids,), (array((far_size, local_count, width), bf16),), 4, 0
+        unit_copies_kernel,
+        "units",
+        (centroids,),
+        (array((far_size, local_count, width), bf16),),
+        4,
+        0,
+        scratch=[
+            pltpu.VMEM(centroids.shape, f32),
+            pltpu.VMEM(centroids.shape, bf16),
+            pltpu.SemaphoreType.DMA((far_size + 1,)),
+        ],
+        hbm_in=(0,),
+        hbm_out=True,
     )
     part = exchange(copies, far)
     copies = call(

time: 227 us -> 228 us (level)
  no operation moved by 1% of the time
where the time goes in v12:
time: 228 us; the launch traced here: 227 us
  blocking collectives  175 us (77%)
  Pallas kernels  25.1 us (11%)
  starting transfers between devices  15.1 us (7%)
  waiting for transfers between devices  9.23 us (4%)
    all_to_all x13, blocking collectives, exchange(): return lax.all_to_all(blocks, axes, 0, 0)  175 us
    pallas_call x16, Pallas kernels, call(): pl.pallas_call(kernel, name=name, out_shape=outs[0] if single else outs,...  25.1 us
    all_to_all x1, starting transfers between devices, exchange(): return lax.all_to_all(blocks, axes, 0, 0)  15.1 us
    all_to_all x1, waiting for transfers between devices, exchange(): return lax.all_to_all(blocks, axes, 0, 0)  9.23 us
  transfers between devices with their start and end apart: 1, of which 1 were waited for; matrix products, arithmetic and copies ran while one was open for 0% of the time, Pallas kernels for 3%

profile of v12, /device:TPU:2, one launch (start us, length us, event | category | flops | bytes accessed | tf_op | source)
XLA Modules:
  0.0 226.6 jit_solution(16821476248742270413)
XLA Ops:
  0.0 1.7 units.1
  1.7 15.1 %all-to-all-start = ((bf16[8,16,768]{2,1,0:T(8,128)(2,1)}), bf16[8,16,768]{2,1,0:T(8,128)(2,1)S(1)}, u32[]{:S(2)}, u32[]{:S(2)}) async-start(bf16[8,16,768]{2,1,0:T(8,128)(2,1)} %units.1), calls=%async_computation | async-start | bytes 393216 | tf_op jit(solution)/shard_map/all_to_all | solution.py:29
  16.8 0.9 reshape.9
  17.7 0.1 reshape.10.group_ref
  17.8 0.9 copy-done.3
  18.7 7.5 %prepare.1 = (bf16[2048,768]{1,0:T(8,128)(2,1)}, bf16[2048,1024]{1,0:T(8,128)(2,1)}) custom-call(bf16[2048,768]{1,0:T(8,128)(2,1)} %x_ref.1, s32[16,2048]{1,0:T(8,128)S(1)} %bitcast.10, s32[1,1024]{1,0:T(1,128)S(1)} %reshape.10.group_ref), custom_call_target="tpu_custom_call" | custom-call | flops 8589934592 | bytes 10620928 | tf_op jit(solution)/shard_map/prepare/pallas_call | solution.py:229
  26.2 9.2 %all-to-all-done.block_ref = bf16[8,16,768]{2,1,0:T(8,128)(2,1)S(1)} async-done(((bf16[8,16,768]{2,1,0:T(8,128)(2,1)}), bf16[8,16,768]{2,1,0:T(8,128)(2,1)S(1)}, u32[]{:S(2)}, u32[]{:S(2)}) %all-to-all-start) | async-done | bytes 196640 | tf_op jit(solution)/shard_map/all_to_all | solution.py:29
  35.4 0.1 copies.1
  35.5 20.8 %all_to_all.70 = bf16[8,8,16,768]{3,2,1,0:T(8,128)(2,1)S(1)} all-to-all(bf16[8,8,16,768]{3,2,1,0:T(8,128)(2,1)S(1)} %copies.1), channel_id=1, replica_groups=mesh['x'=4,'zh'=8,'zl'=2,'y'=4,'core'=2] {'x','zl'}, dimensions={0} | all-to-all | bytes 3145728 | tf_op jit(solution)/shard_map/all_to_all | solution.py:29
  56.3 5.0 %similarity.1 = (bf16[2048,1024]{1,0:T(8,128)(2,1)S(1)}, f32[8,16,128]{2,1,0:T(8,128)S(1)}) custom-call(bf16[2048,768]{1,0:T(8,128)(2,1)S(1)} %copy-done.4, bf16[1024,768]{1,0:T(8,128)(2,1)S(1)} %bitcast.9, bf16[2048,1024]{1,0:T(8,128)(2,1)S(1)} %copy-done), custom_call_target="tpu_custom_call" | custom-call | flops 3221225472 | bytes 13172736 | tf_op jit(solution)/shard_map/similarity/pallas_call | solution.py:229
  61.3 9.9 %all_to_all.71.parts_ref = f32[8,16,128]{2,1,0:T(8,128)S(1)} all-to-all(f32[8,16,128]{2,1,0:T(8,128)S(1)} %get-tuple-element.11), channel_id=1, replica_groups=mesh['x'=4,'zh'=8,'zl'=2,'y'=4,'core'=2] {'y','core'}, dimensions={0} | all-to-all | bytes 131072 | tf_op jit(solution)/shard_map/all_to_all | solution.py:29
  71.2 0.7 columns.3
  71.9 8.0 %all_to_all.72.parts_ref = f32[4,8,128]{2,1,0:T(8,128)S(1)} all-to-all(f32[4,8,128]{2,1,0:T(8,128)S(1)} %columns.3), channel_id=1, replica_groups=mesh['x'=4,'zh'=8,'zl'=2,'y'=4,'core'=2] {'x'}, dimensions={0} | all-to-all | bytes 32768 | tf_op jit(solution)/shard_map/all_to_all | solution.py:29
  79.9 19.9 %all_to_all.73.parts_ref = f32[16,8,128]{2,1,0:T(8,128)S(1)} all-to-all(f32[16,8,128]{2,1,0:T(8,128)S(1)} %across.3), channel_id=1, replica_groups=mesh['x'=4,'zh'=8,'zl'=2,'y'=4,'core'=2] {'zh','zl'}, dimensions={0} | all-to-all | bytes 131072 | tf_op jit(solution)/shard_map/all_to_all | solution.py:29
  99.8 1.2 rows.3
  101.0 8.0 %all_to_all.74.parts_ref = f32[8,16,128]{2,1,0:T(8,128)S(1)} all-to-all(f32[8,16,128]{2,1,0:T(8,128)S(1)} %rows.3), channel_id=1, replica_groups=mesh['x'=4,'zh'=8,'zl'=2,'y'=4,'core'=2] {'y','core'}, dimensions={0} | all-to-all | bytes 131072 | tf_op jit(solution)/shard_map/all_to_all | solution.py:29
  109.0 0.7 columns.4
  109.7 7.9 %all_to_all.75.parts_ref = f32[4,8,128]{2,1,0:T(8,128)S(1)} all-to-all(f32[4,8,128]{2,1,0:T(8,128)S(1)} %columns.4), channel_id=1, replica_groups=mesh['x'=4,'zh'=8,'zl'=2,'y'=4,'core'=2] {'x'}, dimensions={0} | all-to-all | bytes 32768 | tf_op jit(solution)/shard_map/all_to_all | solution.py:29
  117.6 15.5 %all_to_all.76.parts_ref = f32[16,8,128]{2,1,0:T(8,128)S(1)} all-to-all(f32[16,8,128]{2,1,0:T(8,128)S(1)} %across.4), channel_id=1, replica_groups=mesh['x'=4,'zh'=8,'zl'=2,'y'=4,'core'=2] {'zh','zl'}, dimensions={0} | all-to-all | bytes 131072 | tf_op jit(solution)/shard_map/all_to_all | solution.py:29
  133.1 1.2 rows.4
  134.4 8.0 %all_to_all.77.parts_ref = f32[8,16,128]{2,1,0:T(8,128)S(1)} all-to-all(f32[8,16,128]{2,1,0:T(8,128)S(1)} %rows.4), channel_id=1, replica_groups=mesh['x'=4,'zh'=8,'zl'=2,'y'=4,'core'=2] {'y','core'}, dimensions={0} | all-to-all | bytes 131072 | tf_op jit(solution)/shard_map/all_to_all | solution.py:29
  142.4 0.7 columns.5
  143.0 0.0 copy-start.2
  143.0 8.0 %all_to_all.78.parts_ref = f32[4,8,128]{2,1,0:T(8,128)S(1)} all-to-all(f32[4,8,128]{2,1,0:T(8,128)S(1)} %columns.5), channel_id=1, replica_groups=mesh['x'=4,'zh'=8,'zl'=2,'y'=4,'core'=2] {'x'}, dimensions={0} | all-to-all | bytes 32768 | tf_op jit(solution)/shard_map/all_to_all | solution.py:29
  151.0 15.5 %all_to_all.79.parts_ref = f32[16,8,128]{2,1,0:T(8,128)S(1)} all-to-all(f32[16,8,128]{2,1,0:T(8,128)S(1)} %across.5), channel_id=1, replica_groups=mesh['x'=4,'zh'=8,'zl'=2,'y'=4,'core'=2] {'zh','zl'}, dimensions={0} | all-to-all | bytes 131072 | tf_op jit(solution)/shard_map/all_to_all | solution.py:29
  166.5 1.2 rows.5
  167.8 8.0 %all_to_all.80.parts_ref = f32[8,16,128]{2,1,0:T(8,128)S(1)} all-to-all(f32[8,16,128]{2,1,0:T(8,128)S(1)} %rows.5), channel_id=1, replica_groups=mesh['x'=4,'zh'=8,'zl'=2,'y'=4,'core'=2] {'y','core'}, dimensions={0} | all-to-all | bytes 131072 | tf_op jit(solution)/shard_map/all_to_all | solution.py:29
  175.8 4.2 %numerator.1 = bf16[8,784,128]{2,1,0:T(8,128)(2,1)S(1)} custom-call(f32[8,16,128]{2,1,0:T(8,128)S(1)} %all_to_all.80.parts_ref, bf16[2048,1024]{1,0:T(8,128)(2,1)S(1)} %get-tuple-element.12.sim_ref, bf16[2048,768]{1,0:T(8,128)(2,1)S(1)} %copy-done.2), custom_call_target="tpu_custom_call" | custom-call | flops 3221225472 | bytes 9011200 | tf_op jit(solution)/shard_map/numerator/pallas_call | solution.py:229
  179.9 24.8 %all_to_all.81.parts_ref = bf16[8,784,128]{2,1,0:T(8,128)(2,1)S(1)} all-to-all(bf16[8,784,128]{2,1,0:T(8,128)(2,1)S(1)} %numerator.1), channel_id=1, replica_groups=mesh['x'=4,'zh'=8,'zl'=2,'y'=4,'core'=2] {'x','zl'}, dimensions={0} | all-to-all | bytes 3211264 | tf_op jit(solution)/shard_map/all_to_all | solution.py:29
  204.7 0.3 hand_on.1
  205.0 20.9 %all_to_all.82.parts_ref = bf16[8,104,128]{2,1,0:T(8,128)(2,1)S(1)} all-to-all(bf16[8,104,128]{2,1,0:T(8,128)(2,1)S(1)} %hand_on.1), channel_id=1, replica_groups=mesh['x'=4,'zh'=8,'zl'=2,'y'=4,'core'=2] {'zh'}, dimensions={0} | all-to-all | bytes 425984 | tf_op jit(solution)/shard_map/all_to_all | solution.py:29
  225.9 0.7 update.1
  (13 shorter events, 0.1 us)
Async XLA Ops:
  1.7 33.8 %all-to-all-start = ((bf16[8,16,768]{2,1,0:T(8,128)(2,1)}), bf16[8,16,768]{2,1,0:T(8,128)(2,1)S(1)}, u32[]{:S(2)}, u32[]{:S(2)}) async-start(bf16[8,16,768]{2,1,0:T(8,128)(2,1)} %units.1), calls=%async_computation | async-start | bytes 393216 | tf_op jit(solution)/shard_map/all_to_all | solution.py:29
  17.8 0.9 copy-start.3
  35.4 20.9 %copy-start = (bf16[2048,1024]{1,0:T(8,128)(2,1)S(1)}, bf16[2048,1024]{1,0:T(8,128)(2,1)}, u32[]{:S(2)}) copy-start(bf16[2048,1024]{1,0:T(8,128)(2,1)} %get-tuple-element.10.unused.match_ref) | copy-start | bytes 12582916
  35.4 20.9 %copy-start.4 = (bf16[2048,768]{1,0:T(8,128)(2,1)S(1)}, bf16[2048,768]{1,0:T(8,128)(2,1)}, u32[]{:S(2)}) copy-start(bf16[2048,768]{1,0:T(8,128)(2,1)} %get-tuple-element.9.unit_ref) | copy-start | bytes 9437188
  143.0 32.7 %copy-start.2 = (bf16[2048,768]{1,0:T(8,128)(2,1)S(1)}, bf16[2048,768]{1,0:T(8,128)(2,1)}, u32[]{:S(2)}) copy-start(bf16[2048,768]{1,0:T(8,128)(2,1)} %x_ref.1) | copy-start | bytes 9437188
  179.9 46.0 %copy-start.1 = (f32[16,768]{1,0:T(8,128)S(1)}, f32[16,768]{1,0:T(8,128)}, u32[]{:S(2)}) copy-start(f32[16,768]{1,0:T(8,128)} %cent_ref.1) | copy-start | bytes 147460

commit v13 on v11

--- a/solution.py
+++ b/solution.py
@@ -279,8 +279,8 @@
 
     product = 2 * row_count * columns
     row_parts = array((cent_size, row_count // LANES, LANES), f32)
-    column_parts = array((x_size, columns // LANES, LANES), f32)
-    column_sums = array((z_size, columns // LANES, LANES), f32)
+    column_parts = array((near_size, columns // LANES, LANES), f32)
+    column_sums = array((far_size, columns // LANES, LANES), f32)
     similarity, parts = call(
         similarity_kernel,
         "similarity",
@@ -292,11 +292,11 @@
     parts = exchange(parts, ("y", "core"))
     for sweep in range(SWEEPS):
         parts = call(column_kernel, "columns", (parts, similarity), (column_parts,), 8, product * 16)
-        parts = call(sum_copies_kernel, "across", (exchange(parts, "x"),), (column_sums,), 2, 0)
+        parts = call(sum_copies_kernel, "across", (exchange(parts, near),), (column_sums,), 2, 0)
         parts = call(
             functools.partial(row_kernel, desired_load),
             "rows",
-            (exchange(parts, along_z), similarity),
+            (exchange(parts, far), similarity),
             (row_parts,),
             8,
             product * 16,

time: 227 us -> 229 us (level)
  no operation moved by 1% of the time
where the time goes in v13:
time: 229 us
  blocking collectives  177 us (77%)
  Pallas kernels  24 us (10%)
  starting transfers between devices  15.1 us (7%)
  waiting for transfers between devices  9.23 us (4%)
  local copies, waits for them, and re-layouts  2.72 us (1%)
    all_to_all x13, blocking collectives, exchange(): return lax.all_to_all(blocks, axes, 0, 0)  177 us
    pallas_call x16, Pallas kernels, call(): pl.pallas_call(kernel, name=name, out_shape=outs[0] if single else outs,...  24 us
    all_to_all x1, starting transfers between devices, exchange(): return lax.all_to_all(blocks, axes, 0, 0)  15.1 us
    all_to_all x1, waiting for transfers between devices, exchange(): return lax.all_to_all(blocks, axes, 0, 0)  9.23 us
  transfers between devices with their start and end apart: 1, of which 1 were waited for; matrix products, arithmetic and copies ran while one was open for 0% of the time, Pallas kernels for 3%

profile of v13, /device:TPU:2, one launch (start us, length us, event | category | flops | bytes accessed | tf_op | source)
XLA Modules:
  0.0 228.6 jit_solution(16553171269449613494)
XLA Ops:
  0.0 0.8 copy-done.1
  0.8 0.8 units.1
  1.6 15.1 %all-to-all-start = ((bf16[8,16,768]{2,1,0:T(8,128)(2,1)}), bf16[8,16,768]{2,1,0:T(8,128)(2,1)S(1)}, u32[]{:S(2)}, u32[]{:S(2)}) async-start(bf16[8,16,768]{2,1,0:T(8,128)(2,1)} %units.1), calls=%async_computation | async-start | bytes 393216 | tf_op jit(solution)/shard_map/all_to_all | solution.py:29
  16.7 0.9 reshape.9
  17.6 0.1 reshape.10.group_ref
  17.7 0.9 copy-done.4
  18.6 7.5 %prepare.1 = (bf16[2048,768]{1,0:T(8,128)(2,1)}, bf16[2048,1024]{1,0:T(8,128)(2,1)}) custom-call(bf16[2048,768]{1,0:T(8,128)(2,1)} %x_ref.1, s32[16,2048]{1,0:T(8,128)S(1)} %bitcast.10, s32[1,1024]{1,0:T(1,128)S(1)} %reshape.10.group_ref), custom_call_target="tpu_custom_call" | custom-call | flops 8589934592 | bytes 10620928 | tf_op jit(solution)/shard_map/prepare/pallas_call | solution.py:218
  26.1 9.2 %all-to-all-done.block_ref = bf16[8,16,768]{2,1,0:T(8,128)(2,1)S(1)} async-done(((bf16[8,16,768]{2,1,0:T(8,128)(2,1)}), bf16[8,16,768]{2,1,0:T(8,128)(2,1)S(1)}, u32[]{:S(2)}, u32[]{:S(2)}) %all-to-all-start) | async-done | bytes 196640 | tf_op jit(solution)/shard_map/all_to_all | solution.py:29
  35.3 0.1 copies.1
  35.4 20.8 %all_to_all.70 = bf16[8,8,16,768]{3,2,1,0:T(8,128)(2,1)S(1)} all-to-all(bf16[8,8,16,768]{3,2,1,0:T(8,128)(2,1)S(1)} %copies.1), channel_id=1, replica_groups=mesh['x'=4,'zh'=8,'zl'=2,'y'=4,'core'=2] {'x','zl'}, dimensions={0} | all-to-all | bytes 3145728 | tf_op jit(solution)/shard_map/all_to_all | solution.py:29
  56.2 5.0 %similarity.1 = (bf16[2048,1024]{1,0:T(8,128)(2,1)S(1)}, f32[8,16,128]{2,1,0:T(8,128)S(1)}) custom-call(bf16[2048,768]{1,0:T(8,128)(2,1)S(1)} %copy-done.5, bf16[1024,768]{1,0:T(8,128)(2,1)S(1)} %bitcast.9, bf16[2048,1024]{1,0:T(8,128)(2,1)S(1)} %copy-done), custom_call_target="tpu_custom_call" | custom-call | flops 3221225472 | bytes 13172736 | tf_op jit(solution)/shard_map/similarity/pallas_call | solution.py:218
  61.2 9.9 %all_to_all.71.parts_ref = f32[8,16,128]{2,1,0:T(8,128)S(1)} all-to-all(f32[8,16,128]{2,1,0:T(8,128)S(1)} %get-tuple-element.11), channel_id=1, replica_groups=mesh['x'=4,'zh'=8,'zl'=2,'y'=4,'core'=2] {'y','core'}, dimensions={0} | all-to-all | bytes 131072 | tf_op jit(solution)/shard_map/all_to_all | solution.py:29
  71.1 0.7 columns.3
  71.8 9.1 %all_to_all.72.parts_ref = f32[8,8,128]{2,1,0:T(8,128)S(1)} all-to-all(f32[8,8,128]{2,1,0:T(8,128)S(1)} %columns.3), channel_id=1, replica_groups=mesh['x'=4,'zh'=8,'zl'=2,'y'=4,'core'=2] {'x','zl'}, dimensions={0} | all-to-all | bytes 65536 | tf_op jit(solution)/shard_map/all_to_all | solution.py:29
  80.9 19.8 %all_to_all.73.parts_ref = f32[8,8,128]{2,1,0:T(8,128)S(1)} all-to-all(f32[8,8,128]{2,1,0:T(8,128)S(1)} %across.3), channel_id=1, replica_groups=mesh['x'=4,'zh'=8,'zl'=2,'y'=4,'core'=2] {'zh'}, dimensions={0} | all-to-all | bytes 65536 | tf_op jit(solution)/shard_map/all_to_all | solution.py:29
  100.7 1.2 rows.3
  101.9 8.0 %all_to_all.74.parts_ref = f32[8,16,128]{2,1,0:T(8,128)S(1)} all-to-all(f32[8,16,128]{2,1,0:T(8,128)S(1)} %rows.3), channel_id=1, replica_groups=mesh['x'=4,'zh'=8,'zl'=2,'y'=4,'core'=2] {'y','core'}, dimensions={0} | all-to-all | bytes 131072 | tf_op jit(solution)/shard_map/all_to_all | solution.py:29
  109.9 0.7 columns.4
  110.6 8.8 %all_to_all.75.parts_ref = f32[8,8,128]{2,1,0:T(8,128)S(1)} all-to-all(f32[8,8,128]{2,1,0:T(8,128)S(1)} %columns.4), channel_id=1, replica_groups=mesh['x'=4,'zh'=8,'zl'=2,'y'=4,'core'=2] {'x','zl'}, dimensions={0} | all-to-all | bytes 65536 | tf_op jit(solution)/shard_map/all_to_all | solution.py:29
  119.4 15.3 %all_to_all.76.parts_ref = f32[8,8,128]{2,1,0:T(8,128)S(1)} all-to-all(f32[8,8,128]{2,1,0:T(8,128)S(1)} %across.4), channel_id=1, replica_groups=mesh['x'=4,'zh'=8,'zl'=2,'y'=4,'core'=2] {'zh'}, dimensions={0} | all-to-all | bytes 65536 | tf_op jit(solution)/shard_map/all_to_all | solution.py:29
  134.7 1.2 rows.4
  135.9 8.0 %all_to_all.77.parts_ref = f32[8,16,128]{2,1,0:T(8,128)S(1)} all-to-all(f32[8,16,128]{2,1,0:T(8,128)S(1)} %rows.4), channel_id=1, replica_groups=mesh['x'=4,'zh'=8,'zl'=2,'y'=4,'core'=2] {'y','core'}, dimensions={0} | all-to-all | bytes 131072 | tf_op jit(solution)/shard_map/all_to_all | solution.py:29
  143.9 0.7 columns.5
  144.6 9.0 %all_to_all.78.parts_ref = f32[8,8,128]{2,1,0:T(8,128)S(1)} all-to-all(f32[8,8,128]{2,1,0:T(8,128)S(1)} %columns.5), channel_id=1, replica_groups=mesh['x'=4,'zh'=8,'zl'=2,'y'=4,'core'=2] {'x','zl'}, dimensions={0} | all-to-all | bytes 65536 | tf_op jit(solution)/shard_map/all_to_all | solution.py:29
  153.6 15.3 %all_to_all.79.parts_ref = f32[8,8,128]{2,1,0:T(8,128)S(1)} all-to-all(f32[8,8,128]{2,1,0:T(8,128)S(1)} %across.5), channel_id=1, replica_groups=mesh['x'=4,'zh'=8,'zl'=2,'y'=4,'core'=2] {'zh'}, dimensions={0} | all-to-all | bytes 65536 | tf_op jit(solution)/shard_map/all_to_all | solution.py:29
  168.9 1.2 rows.5
  170.1 8.0 %all_to_all.80.parts_ref = f32[8,16,128]{2,1,0:T(8,128)S(1)} all-to-all(f32[8,16,128]{2,1,0:T(8,128)S(1)} %rows.5), channel_id=1, replica_groups=mesh['x'=4,'zh'=8,'zl'=2,'y'=4,'core'=2] {'y','core'}, dimensions={0} | all-to-all | bytes 131072 | tf_op jit(solution)/shard_map/all_to_all | solution.py:29
  178.1 4.0 %numerator.1 = bf16[8,784,128]{2,1,0:T(8,128)(2,1)S(1)} custom-call(f32[8,16,128]{2,1,0:T(8,128)S(1)} %all_to_all.80.parts_ref, bf16[2048,1024]{1,0:T(8,128)(2,1)S(1)} %get-tuple-element.12.sim_ref, bf16[2048,768]{1,0:T(8,128)(2,1)S(1)} %copy-done.3), custom_call_target="tpu_custom_call" | custom-call | flops 3221225472 | bytes 9011200 | tf_op jit(solution)/shard_map/numerator/pallas_call | solution.py:218
  182.1 24.8 %all_to_all.81.parts_ref = bf16[8,784,128]{2,1,0:T(8,128)(2,1)S(1)} all-to-all(bf16[8,784,128]{2,1,0:T(8,128)(2,1)S(1)} %numerator.1), channel_id=1, replica_groups=mesh['x'=4,'zh'=8,'zl'=2,'y'=4,'core'=2] {'x','zl'}, dimensions={0} | all-to-all | bytes 3211264 | tf_op jit(solution)/shard_map/all_to_all | solution.py:29
  206.9 0.3 hand_on.1
  207.2 20.6 %all_to_all.82.parts_ref = bf16[8,104,128]{2,1,0:T(8,128)(2,1)S(1)} all-to-all(bf16[8,104,128]{2,1,0:T(8,128)(2,1)S(1)} %hand_on.1), channel_id=1, replica_groups=mesh['x'=4,'zh'=8,'zl'=2,'y'=4,'core'=2] {'zh'}, dimensions={0} | all-to-all | bytes 425984 | tf_op jit(solution)/shard_map/all_to_all | solution.py:29
  227.9 0.7 update.1
  (15 shorter events, 0.1 us)
Async XLA Ops:
  0.0 0.8 copy-start.1
  1.6 33.8 %all-to-all-start = ((bf16[8,16,768]{2,1,0:T(8,128)(2,1)}), bf16[8,16,768]{2,1,0:T(8,128)(2,1)S(1)}, u32[]{:S(2)}, u32[]{:S(2)}) async-start(bf16[8,16,768]{2,1,0:T(8,128)(2,1)} %units.1), calls=%async_computation | async-start | bytes 393216 | tf_op jit(solution)/shard_map/all_to_all | solution.py:29
  17.7 0.9 copy-start.4
  35.3 20.9 %copy-start = (bf16[2048,1024]{1,0:T(8,128)(2,1)S(1)}, bf16[2048,1024]{1,0:T(8,128)(2,1)}, u32[]{:S(2)}) copy-start(bf16[2048,1024]{1,0:T(8,128)(2,1)} %get-tuple-element.10.unused.match_ref) | copy-start | bytes 12582916
  35.3 20.9 %copy-start.5 = (bf16[2048,768]{1,0:T(8,128)(2,1)S(1)}, bf16[2048,768]{1,0:T(8,128)(2,1)}, u32[]{:S(2)}) copy-start(bf16[2048,768]{1,0:T(8,128)(2,1)} %get-tuple-element.9.unit_ref) | copy-start | bytes 9437188
  144.6 33.6 %copy-start.3 = (bf16[2048,768]{1,0:T(8,128)(2,1)S(1)}, bf16[2048,768]{1,0:T(8,128)(2,1)}, u32[]{:S(2)}) copy-start(bf16[2048,768]{1,0:T(8,128)(2,1)} %x_ref.1) | copy-start | bytes 9437188
  182.1 45.8 %copy-start.2 = (f32[16,768]{1,0:T(8,128)S(1)}, f32[16,768]{1,0:T(8,128)}, u32[]{:S(2)}) copy-start(f32[16,768]{1,0:T(8,128)} %cent_ref.3) | copy-start | bytes 147460

commit v14 on v11

--- a/solution.py
+++ b/solution.py
@@ -121,16 +121,17 @@
 def similarity_kernel(unit_ref, cent_ref, match_ref, sim_ref, total_ref):
     ones = jnp.ones((total_ref.shape[0], sim_ref.shape[1]), bf16)
     scale = math.log2(math.e) / entropic_smoothing
-    for b in range(unit_ref.shape[0] // TILE):
-        rows = pl.ds(b * TILE, TILE)
+    step = 2 * TILE
+    for b in range(unit_ref.shape[0] // step):
+        rows = pl.ds(b * step, step)
         dots = lax.dot_general(
             unit_ref[rows, :], cent_ref[...], (((1,), (1,)), ((), ())), preferred_element_type=f32
         )
         sim = (jnp.exp2(dots * scale) * match_ref[rows, :].astype(f32)).astype(bf16)
         sim_ref[rows, :] = sim
         totals = lax.dot_general(ones, sim, (((1,), (1,)), ((), ())), preferred_element_type=f32)
-        for q in range(TILE // LANES):
-            total_ref[:, b * (TILE // LANES) + q, :] = totals[:, q * LANES : (q + 1) * LANES]
+        for q in range(step // LANES):
+            total_ref[:, b * (step // LANES) + q, :] = totals[:, q * LANES : (q + 1) * LANES]
 
 
 def column_kernel(parts_ref, sim_ref, out_ref):

time: 227 us -> 227 us (level)
  no operation moved by 1% of the time
where the time goes in v14:
time: 227 us; the launch traced here: 226 us
  blocking collectives  175 us (77%)
  Pallas kernels  23.7 us (10%)
  starting transfers between devices  15.1 us (7%)
  waiting for transfers between devices  9.23 us (4%)
  local copies, waits for them, and re-layouts  2.72 us (1%)
    all_to_all x13, blocking collectives, exchange(): return lax.all_to_all(blocks, axes, 0, 0)  175 us
    pallas_call x16, Pallas kernels, call(): pl.pallas_call(kernel, name=name, out_shape=outs[0] if single else outs,...  23.7 us
    all_to_all x1, starting transfers between devices, exchange(): return lax.all_to_all(blocks, axes, 0, 0)  15.1 us
    all_to_all x1, waiting for transfers between devices, exchange(): return lax.all_to_all(blocks, axes, 0, 0)  9.23 us
  transfers between devices with their start and end apart: 1, of which 1 were waited for; matrix products, arithmetic and copies ran while one was open for 0% of the time, Pallas kernels for 3%

profile of v14, /device:TPU:2, one launch (start us, length us, event | category | flops | bytes accessed | tf_op | source)
XLA Modules:
  0.0 225.8 jit_solution(9690852110885318595)
XLA Ops:
  0.0 0.8 copy-done.1
  0.8 0.8 units.1
  1.6 15.1 %all-to-all-start = ((bf16[8,16,768]{2,1,0:T(8,128)(2,1)}), bf16[8,16,768]{2,1,0:T(8,128)(2,1)S(1)}, u32[]{:S(2)}, u32[]{:S(2)}) async-start(bf16[8,16,768]{2,1,0:T(8,128)(2,1)} %units.1), calls=%async_computation | async-start | bytes 393216 | tf_op jit(solution)/shard_map/all_to_all | solution.py:29
  16.7 0.9 reshape.9
  17.6 0.1 reshape.10.group_ref
  17.7 0.9 copy-done.4
  18.6 7.5 %prepare.1 = (bf16[2048,768]{1,0:T(8,128)(2,1)}, bf16[2048,1024]{1,0:T(8,128)(2,1)}) custom-call(bf16[2048,768]{1,0:T(8,128)(2,1)} %x_ref.1, s32[16,2048]{1,0:T(8,128)S(1)} %bitcast.10, s32[1,1024]{1,0:T(1,128)S(1)} %reshape.10.group_ref), custom_call_target="tpu_custom_call" | custom-call | flops 8589934592 | bytes 10620928 | tf_op jit(solution)/shard_map/prepare/pallas_call | solution.py:219
  26.1 9.2 %all-to-all-done.block_ref = bf16[8,16,768]{2,1,0:T(8,128)(2,1)S(1)} async-done(((bf16[8,16,768]{2,1,0:T(8,128)(2,1)}), bf16[8,16,768]{2,1,0:T(8,128)(2,1)S(1)}, u32[]{:S(2)}, u32[]{:S(2)}) %all-to-all-start) | async-done | bytes 196640 | tf_op jit(solution)/shard_map/all_to_all | solution.py:29
  35.3 0.1 copies.1
  35.4 20.8 %all_to_all.70 = bf16[8,8,16,768]{3,2,1,0:T(8,128)(2,1)S(1)} all-to-all(bf16[8,8,16,768]{3,2,1,0:T(8,128)(2,1)S(1)} %copies.1), channel_id=1, replica_groups=mesh['x'=4,'zh'=8,'zl'=2,'y'=4,'core'=2] {'x','zl'}, dimensions={0} | all-to-all | bytes 3145728 | tf_op jit(solution)/shard_map/all_to_all | solution.py:29
  56.2 4.7 %similarity.1 = (bf16[2048,1024]{1,0:T(8,128)(2,1)S(1)}, f32[8,16,128]{2,1,0:T(8,128)S(1)}) custom-call(bf16[2048,768]{1,0:T(8,128)(2,1)S(1)} %copy-done.5, bf16[1024,768]{1,0:T(8,128)(2,1)S(1)} %bitcast.9, bf16[2048,1024]{1,0:T(8,128)(2,1)S(1)} %copy-done), custom_call_target="tpu_custom_call" | custom-call | flops 3221225472 | bytes 13172736 | tf_op jit(solution)/shard_map/similarity/pallas_call | solution.py:219
  60.9 9.9 %all_to_all.71.parts_ref = f32[8,16,128]{2,1,0:T(8,128)S(1)} all-to-all(f32[8,16,128]{2,1,0:T(8,128)S(1)} %get-tuple-element.11), channel_id=1, replica_groups=mesh['x'=4,'zh'=8,'zl'=2,'y'=4,'core'=2] {'y','core'}, dimensions={0} | all-to-all | bytes 131072 | tf_op jit(solution)/shard_map/all_to_all | solution.py:29
  70.8 0.7 columns.3
  71.5 8.0 %all_to_all.72.parts_ref = f32[4,8,128]{2,1,0:T(8,128)S(1)} all-to-all(f32[4,8,128]{2,1,0:T(8,128)S(1)} %columns.3), channel_id=1, replica_groups=mesh['x'=4,'zh'=8,'zl'=2,'y'=4,'core'=2] {'x'}, dimensions={0} | all-to-all | bytes 32768 | tf_op jit(solution)/shard_map/all_to_all | solution.py:29
  79.5 19.9 %all_to_all.73.parts_ref = f32[16,8,128]{2,1,0:T(8,128)S(1)} all-to-all(f32[16,8,128]{2,1,0:T(8,128)S(1)} %across.3), channel_id=1, replica_groups=mesh['x'=4,'zh'=8,'zl'=2,'y'=4,'core'=2] {'zh','zl'}, dimensions={0} | all-to-all | bytes 131072 | tf_op jit(solution)/shard_map/all_to_all | solution.py:29
  99.4 1.2 rows.3
  100.6 8.0 %all_to_all.74.parts_ref = f32[8,16,128]{2,1,0:T(8,128)S(1)} all-to-all(f32[8,16,128]{2,1,0:T(8,128)S(1)} %rows.3), channel_id=1, replica_groups=mesh['x'=4,'zh'=8,'zl'=2,'y'=4,'core'=2] {'y','core'}, dimensions={0} | all-to-all | bytes 131072 | tf_op jit(solution)/shard_map/all_to_all | solution.py:29
  108.6 0.7 columns.4
  109.3 7.7 %all_to_all.75.parts_ref = f32[4,8,128]{2,1,0:T(8,128)S(1)} all-to-all(f32[4,8,128]{2,1,0:T(8,128)S(1)} %columns.4), channel_id=1, replica_groups=mesh['x'=4,'zh'=8,'zl'=2,'y'=4,'core'=2] {'x'}, dimensions={0} | all-to-all | bytes 32768 | tf_op jit(solution)/shard_map/all_to_all | solution.py:29
  117.0 15.6 %all_to_all.76.parts_ref = f32[16,8,128]{2,1,0:T(8,128)S(1)} all-to-all(f32[16,8,128]{2,1,0:T(8,128)S(1)} %across.4), channel_id=1, replica_groups=mesh['x'=4,'zh'=8,'zl'=2,'y'=4,'core'=2] {'zh','zl'}, dimensions={0} | all-to-all | bytes 131072 | tf_op jit(solution)/shard_map/all_to_all | solution.py:29
  132.6 1.2 rows.4
  133.8 8.0 %all_to_all.77.parts_ref = f32[8,16,128]{2,1,0:T(8,128)S(1)} all-to-all(f32[8,16,128]{2,1,0:T(8,128)S(1)} %rows.4), channel_id=1, replica_groups=mesh['x'=4,'zh'=8,'zl'=2,'y'=4,'core'=2] {'y','core'}, dimensions={0} | all-to-all | bytes 131072 | tf_op jit(solution)/shard_map/all_to_all | solution.py:29
  141.8 0.7 columns.5
  142.5 8.0 %all_to_all.78.parts_ref = f32[4,8,128]{2,1,0:T(8,128)S(1)} all-to-all(f32[4,8,128]{2,1,0:T(8,128)S(1)} %columns.5), channel_id=1, replica_groups=mesh['x'=4,'zh'=8,'zl'=2,'y'=4,'core'=2] {'x'}, dimensions={0} | all-to-all | bytes 32768 | tf_op jit(solution)/shard_map/all_to_all | solution.py:29
  150.4 15.5 %all_to_all.79.parts_ref = f32[16,8,128]{2,1,0:T(8,128)S(1)} all-to-all(f32[16,8,128]{2,1,0:T(8,128)S(1)} %across.5), channel_id=1, replica_groups=mesh['x'=4,'zh'=8,'zl'=2,'y'=4,'core'=2] {'zh','zl'}, dimensions={0} | all-to-all | bytes 131072 | tf_op jit(solution)/shard_map/all_to_all | solution.py:29
  165.9 1.2 rows.5
  167.2 8.0 %all_to_all.80.parts_ref = f32[8,16,128]{2,1,0:T(8,128)S(1)} all-to-all(f32[8,16,128]{2,1,0:T(8,128)S(1)} %rows.5), channel_id=1, replica_groups=mesh['x'=4,'zh'=8,'zl'=2,'y'=4,'core'=2] {'y','core'}, dimensions={0} | all-to-all | bytes 131072 | tf_op jit(solution)/shard_map/all_to_all | solution.py:29
  175.2 4.0 %numerator.1 = bf16[8,784,128]{2,1,0:T(8,128)(2,1)S(1)} custom-call(f32[8,16,128]{2,1,0:T(8,128)S(1)} %all_to_all.80.parts_ref, bf16[2048,1024]{1,0:T(8,128)(2,1)S(1)} %get-tuple-element.12.sim_ref, bf16[2048,768]{1,0:T(8,128)(2,1)S(1)} %copy-done.3), custom_call_target="tpu_custom_call" | custom-call | flops 3221225472 | bytes 9011200 | tf_op jit(solution)/shard_map/numerator/pallas_call | solution.py:219
  179.1 24.8 %all_to_all.81.parts_ref = bf16[8,784,128]{2,1,0:T(8,128)(2,1)S(1)} all-to-all(bf16[8,784,128]{2,1,0:T(8,128)(2,1)S(1)} %numerator.1), channel_id=1, replica_groups=mesh['x'=4,'zh'=8,'zl'=2,'y'=4,'core'=2] {'x','zl'}, dimensions={0} | all-to-all | bytes 3211264 | tf_op jit(solution)/shard_map/all_to_all | solution.py:29
  203.9 0.3 hand_on.1
  204.3 20.9 %all_to_all.82.parts_ref = bf16[8,104,128]{2,1,0:T(8,128)(2,1)S(1)} all-to-all(bf16[8,104,128]{2,1,0:T(8,128)(2,1)S(1)} %hand_on.1), channel_id=1, replica_groups=mesh['x'=4,'zh'=8,'zl'=2,'y'=4,'core'=2] {'zh'}, dimensions={0} | all-to-all | bytes 425984 | tf_op jit(solution)/shard_map/all_to_all | solution.py:29
  225.1 0.7 update.1
  (15 shorter events, 0.1 us)
Async XLA Ops:
  0.0 0.8 copy-start.1
  1.6 33.8 %all-to-all-start = ((bf16[8,16,768]{2,1,0:T(8,128)(2,1)}), bf16[8,16,768]{2,1,0:T(8,128)(2,1)S(1)}, u32[]{:S(2)}, u32[]{:S(2)}) async-start(bf16[8,16,768]{2,1,0:T(8,128)(2,1)} %units.1), calls=%async_computation | async-start | bytes 393216 | tf_op jit(solution)/shard_map/all_to_all | solution.py:29
  17.7 0.9 copy-start.4
  35.3 20.9 %copy-start = (bf16[2048,1024]{1,0:T(8,128)(2,1)S(1)}, bf16[2048,1024]{1,0:T(8,128)(2,1)}, u32[]{:S(2)}) copy-start(bf16[2048,1024]{1,0:T(8,128)(2,1)} %get-tuple-element.10.unused.match_ref) | copy-start | bytes 12582916
  35.3 20.9 %copy-start.5 = (bf16[2048,768]{1,0:T(8,128)(2,1)S(1)}, bf16[2048,768]{1,0:T(8,128)(2,1)}, u32[]{:S(2)}) copy-start(bf16[2048,768]{1,0:T(8,128)(2,1)} %get-tuple-element.9.unit_ref) | copy-start | bytes 9437188
  142.5 32.7 %copy-start.3 = (bf16[2048,768]{1,0:T(8,128)(2,1)S(1)}, bf16[2048,768]{1,0:T(8,128)(2,1)}, u32[]{:S(2)}) copy-start(bf16[2048,768]{1,0:T(8,128)(2,1)} %x_ref.1) | copy-start | bytes 9437188
  179.1 46.0 %copy-start.2 = (f32[16,768]{1,0:T(8,128)S(1)}, f32[16,768]{1,0:T(8,128)}, u32[]{:S(2)}) copy-start(f32[16,768]{1,0:T(8,128)} %cent_ref.3) | copy-start | bytes 147460
